TPU v7x, 32 devices: a whole 2x2x4 slice. The times are simulated.
32 devices in a mesh: groups: 2 (over x), row: 8 (over z, y), col: 2 (over core).
Axes of the slice: x: 2, y: 2, z: 4, core: 2. Of those that a mesh axis runs over, the one named last changes fastest.
Arguments:
- a_values: bfloat16 [64, 8, 2, 128, 128], P(('groups', 'col'), 'row'), parts along dimension 0, may hold values from -6 to 6
- a_index: int32 [64, 8, 2], P(('groups', 'col'), 'row'), parts along dimension 0, may hold values from -1 to 3
- b_values: bfloat16 [64, 8, 4, 128, 128], P(('groups', 'col'), 'row'), parts along dimension 0, may hold values from -0.125 to 0.125
- b_index: int32 [64, 8, 4], P(('groups', 'col'), 'row'), parts along dimension 0, may hold values from -1 to 7
Outputs:
- product: bfloat16 [64, 8, 8, 128, 128], P(('groups', 'col'), 'row'), parts along dimension 0
There are 2 independent parts, one for each index of `groups`. A program takes and returns all parts, laid end to end along the dimension named above; each array names one. Nothing has to cross between parts.
Inputs may be any that keep to these rules, and one draw needn't show every extreme that they name: `a_index`: a value of -1 marks an empty slot. `b_index`: a value of -1 marks an empty slot.
All inputs are finite; a program needn't handle non-finite values.
Results may differ from a plain program's by a relative error of at most 0.0034.
Values may be sent and summed in bfloat16 or wider, within the bound.
No kernel may reach another device: no remote copies, remote signals or barrier semaphores. Data moves between devices by JAX's collectives and lax.ppermute only.
A program may use at most 320 MiB of HBM per device.

v0:
```python
import jax
import jax.numpy as jnp
from jax import lax
from jax.sharding import PartitionSpec as P

BK = 4
BJ = 8


def densify(index, values, count):
    columns = jnp.arange(count, dtype=jnp.int32)
    onehot = (index[:, :, None] == columns).astype(jnp.bfloat16)
    return jnp.einsum("ksw,ksxy->kwxy", onehot, values, preferred_element_type=jnp.float32).astype(
        jnp.bfloat16
    )


def body(a_values, a_index, b_values, b_index):
    count = BJ
    inner_width = BK
    half_dense = densify(b_index[:, 0], b_values[:, 0], count)
    right_dense = lax.all_gather(half_dense, "col", axis=0, tiled=True)
    whole_values, whole_index = (
        lax.all_gather(a_values, "row", axis=1, tiled=True),
        lax.all_gather(a_index, "row", axis=1, tiled=True),
    )
    number = whole_index.shape[1]
    positions = jnp.arange(number, dtype=jnp.int32)
    valid = whole_index >= 0
    inner = jnp.where(valid, positions[None, :, None] * inner_width + whole_index, 0).astype(
        jnp.int32
    )
    chosen = right_dense[inner]
    masked = whole_values * valid[:, :, :, None, None].astype(jnp.bfloat16)
    total = jnp.einsum("insxy,insjyz->ijxz", masked, chosen, preferred_element_type=jnp.float32)
    return total.astype(jnp.bfloat16)[:, None]


def solution(mesh):
    placed = (
        P(("groups", "col"), "row", None, None, None),
        P(("groups", "col"), "row", None),
        P(("groups", "col"), "row", None, None, None),
        P(("groups", "col"), "row", None),
    )
    return jax.shard_map(
        body,
        mesh=mesh,
        in_specs=placed,
        out_specs=P(("groups", "col"), "row", None, None, None),
        check_vma=False,
    )
```

profile of v0, /device:TPU:0, one launch (start us, length us, event | category | flops | bytes accessed | tf_op | source)
XLA Modules:
  0.0 215.2 jit_solution(10733847004252724083)
XLA Ops:
  6.5 0.0 copy-start
  6.5 0.0 all-gather.3.cloned.1.call-start
  6.5 0.9 copy.16
  7.4 0.7 copy-done
  8.1 2.1 convolution_convert_fusion
  10.2 0.0 copy-start.1
  10.2 3.3 %copy.18 = bf16[16,8,128,128]{3,2,1,0:T(8,128)(2,1)} copy(bf16[16,8,128,128]{3,1,2,0:T(8,128)(2,1)S(1)} %convolution_convert_fusion) | data formatting | bytes 8388608 | tf_op jit(solution)/shard_map/convert_element_type | solution.py:13
  13.5 0.0 all-gather.3.cloned.1.call-update
  13.5 0.0 all-gather.5.cloned.1.call-start
  13.5 0.7 all-gather.5.cloned.1.call-update
  14.2 0.0 copy-done.1
  14.3 22.3 %all_gather.10 = s32[16,8,2]{0,2,1:T(2,128)S(1)} all-gather(s32[16,1,2]{0,2,1:T(2,128)S(1)} %copy-done.1), channel_id=1, replica_groups=mesh['groups'=2,'row'=8,'col'=2] {'row'}, dimensions={1}, use_global_device_ids=true | all-gather | bytes 1152 | tf_op jit(solution)/shard_map/all_gather | solution.py:25
  36.5 0.1 compare_select_fusion
  36.6 0.1 copy.19
  36.7 0.1 reshape.10
  36.9 0.1 copy.20
  37.1 0.0 all-gather.3.cloned.1.call-done
  37.1 27.0 %gather_fusion = bf16[256,8,128,128]{3,2,1,0:T(8,128)(2,1)} fusion(bf16[32,8,128,128]{3,2,1,0:T(8,128)(2,1)} %all-gather.3.cloned.1.call-done, s32[1024]{0:T(1024)S(1)} %pad_clamp_fusion), kind=kCustom, calls=%fused_computation | custom fusion | bytes 134218752 | tf_op jit(solution)/shard_map/gather | solution.py:33
  64.1 100.4 %all-gather.5.cloned.1.call-done = bf16[16,8,2,128,128]{4,3,2,1,0:T(8,128)(2,1)} async-done(((bf16[16,1,2,128,128]{4,3,2,1,0:T(8,128)(2,1)}), bf16[16,8,2,128,128]{4,3,2,1,0:T(8,128)(2,1)}) %all-gather.5.cloned.1.call-update) | async-done | bytes 8388624 | tf_op jit(solution)/shard_map/all_gather | solution.py:24
  164.5 32.7 %fusion = bf16[16,8,128,128,1,1]{3,2,5,0,1,4:T(8,128)(2,1)} fusion(bf16[16,8,2,8,128,128]{5,4,3,2,1,0:T(8,128)(2,1)} %bitcast.4, bf16[16,8,2,128,128]{4,3,2,1,0:T(8,128)(2,1)} %all-gather.5.cloned.1.call-done, bf16[16,8,2]{2,1,0:T(8,128)(2,1)S(1)} %copy.20), kind=kOutput, calls=%fused_computation.1 | convolution fusion | flops 8594128896 | bytes 79692288 | tf_op jit(solution)/shard_map/insxy,insjyz->ijxz/dot_general | solution.py:35
  197.2 4.7 %copy.37 = bf16[16,8,128,128,1,1]{3,2,1,0,4,5:T(8,128)(2,1)} copy(bf16[16,8,128,128,1,1]{3,2,5,0,1,4:T(8,128)(2,1)} %fusion) | data formatting | bytes 8388608 | tf_op jit(solution)/shard_map/insxy,insjyz->ijxz/dot_general | solution.py:35
  201.9 6.4 %copy.22 = bf16[16,1,8,128,128]{4,3,2,1,0:T(8,128)(2,1)} copy(bf16[16,1,8,128,128]{3,4,2,0,1:T(8,128)(2,1)} %bitcast.23) | data formatting | bytes 8388608 | tf_op jit(solution)/shard_map/broadcast_in_dim | solution.py:36
  (3 shorter events, 0.0 us)
Async XLA Ops:
  6.5 1.6 copy-start
  6.5 30.5 %all-gather.3.cloned.1.call-start = ((), (), s32[]{:S(2)}) async-start(), calls=%async_computation | async-start | bytes 12582912 | tf_op jit(solution)/shard_map/all_gather | solution.py:22
  10.2 4.0 %copy-start.1 = (s32[16,1,2]{0,2,1:T(2,128)S(1)}, s32[16,1,2]{0,2,1:T(2,128)}, u32[]{:S(2)}) copy-start(s32[16,1,2]{0,2,1:T(2,128)} %param.5) | copy-start | bytes 388
  13.5 151.0 %all-gather.5.cloned.1.call-start = ((), (), s32[]{:S(2)}) async-start(), calls=%async_computation.1 | async-start | bytes 9437184 | tf_op jit(solution)/shard_map/all_gather | solution.py:24
Sparse Core Ops, SparseCore 0:
  13.6 22.5 all-gather.2
  38.4 126.0 all-gather.4
where the time goes:
time: 216 us; the launch traced here: 215 us
  waiting for transfers between devices  101 us (47%)
  local copies, waits for them, and re-layouts  43.4 us (20%)
  matrix products  34.7 us (16%)
  blocking collectives  22.3 us (10%)
  between operations  13.5 us (6%)
    all_gather x1, waiting for transfers between devices, body(): lax.all_gather(a_values, 'row', axis=1, tiled=True)  100 us
    dot_general x1, matrix products, body(): jnp.einsum('insxy,insjyz->ijxz', masked, chosen, preferred_element_type=j...  32.7 us
    gather x1, local copies, waits for them, and re-layouts, body(): chosen = right_dense[inner]  27 us
    all_gather x1, blocking collectives, body(): lax.all_gather(a_index, 'row', axis=1, tiled=True)  22.3 us
    broadcast_in_dim x1, local copies, waits for them, and re-layouts, body(): return total.astype(jnp.bfloat16)[:, None]  6.39 us
    dot_general x1, local copies, waits for them, and re-layouts, body(): jnp.einsum('insxy,insjyz->ijxz', masked, chosen, preferred_element_type=j...  4.71 us
  transfers between devices with their start and end apart: 2, of which 1 were waited for; matrix products, arithmetic and copies ran while one was open for 13% of the time, Pallas kernels for 0%

commit v1 on v0

v1 whole, which is shorter than its diff:
```python
import functools

import jax
import jax.numpy as jnp
import numpy as np
from jax import lax
from jax.experimental import pallas as pl
from jax.experimental.pallas import tpu as pltpu
from jax.sharding import PartitionSpec as P

BJ = 8
VMEM_LIMIT = 20 * 1024 * 1024


def ring_order(n):
    if n == 8:
        return (0, 2, 4, 6, 7, 5, 3, 1)
    return tuple(range(n))


def densify_kernel(col_ref, own_index, other_index, own_ref, other_ref, dense_ref):
    source = pl.program_id(0)
    first = pl.program_id(1) * own_ref.shape[0]
    blk = own_ref.shape[-1]
    slots = own_ref.shape[1]
    for k in range(own_ref.shape[0]):
        stored = [
            jnp.where(source == 0, own_ref[k, t], other_ref[k, t]).astype(jnp.float32)
            for t in range(slots)
        ]
        at = [(first + k) * slots + t for t in range(slots)]
        columns = [jnp.where(source == 0, own_index[i], other_index[i]) for i in at]
        for j in range(BJ):
            total = jnp.zeros((blk, blk), jnp.float32)
            for t in range(slots):
                total = total + jnp.where(columns[t] == j, stored[t], 0.0)
            dense_ref[0, k, :, j * blk : (j + 1) * blk] = total.astype(jnp.bfloat16)


def densify(col, own_index, other_index, own, other, pieces, inner_width):
    slots, blk = own.shape[1], own.shape[-1]
    stored = (inner_width, slots, blk, blk)
    return pl.pallas_call(
        densify_kernel,
        out_shape=jax.ShapeDtypeStruct((2 * pieces, inner_width, blk, BJ * blk), jnp.bfloat16),
        grid_spec=pltpu.PrefetchScalarGridSpec(
            num_scalar_prefetch=3,
            grid=(2, pieces),
            in_specs=[
                pl.BlockSpec(stored, lambda s, g, c, *i: (jnp.where(s == 0, g, pieces - 1), 0, 0, 0)),
                pl.BlockSpec(stored, lambda s, g, c, *i: (jnp.where(s == 0, 0, g), 0, 0, 0)),
            ],
            out_specs=pl.BlockSpec(
                (1, inner_width, blk, BJ * blk),
                lambda s, g, c, *i: (jnp.where(s == 0, c[0], 1 - c[0]) * pieces + g, 0, 0, 0),
            ),
        ),
        compiler_params=pltpu.CompilerParams(vmem_limit_bytes=VMEM_LIMIT),
        cost_estimate=pl.CostEstimate(
            flops=2 * pieces * inner_width * slots * BJ * blk * blk * 2,
            bytes_accessed=2 * own.size * 2 + 2 * pieces * inner_width * BJ * blk * blk * 2,
            transcendentals=0,
        ),
    )(col, own_index, other_index, own, other)


def product_kernel(offsets, sides, starts, has_total, last, step, *refs):
    count = len(offsets)
    index = refs[1 : 1 + count]
    refs = refs[1 + count :]
    left = refs[: count * sides]
    right = refs[count * sides : count * (sides + 1)]
    rest = refs[count * (sides + 1) :]
    out_ref = rest[-1]
    total_ref = rest[0] if has_total else None
    slots, blk = left[0].shape[1], left[0].shape[-1]
    wide = 2 * blk
    g = pl.program_id(0)
    if sides == 2:
        each = pl.num_programs(0) // 2
        second = g >= each
        row0 = jnp.where(second, starts[1] + (g - each) * step, starts[0] + g * step)
    else:
        row0 = starts[0] + g * step
    for i in range(step):
        factors = []
        for m in range(count):
            inner = [index[m][(row0 + i) * slots + s] for s in range(slots)]
            parts = []
            for s in range(slots):
                part = left[m * sides][i, s]
                if sides == 2:
                    part = jnp.where(second, left[m * sides + 1][i, s], part)
                parts.append(jnp.where(inner[s] >= 0, part, jnp.zeros((), jnp.bfloat16)))
            factors.append((jnp.concatenate(parts, axis=1), [jnp.maximum(k, 0) for k in inner]))
        for c in range(BJ // 2):
            columns = slice(c * wide, (c + 1) * wide)
            total = total_ref[i, :, columns] if has_total else None
            for m in range(count):
                row, inner = factors[m]
                rows_of = jnp.concatenate([right[m][0, k, :, columns] for k in inner], axis=0)
                term = jnp.dot(row, rows_of, preferred_element_type=jnp.float32)
                total = term if total is None else total + term
            if last:
                for j in range(2):
                    out_ref[i, 0, c * 2 + j] = total[:, j * blk : (j + 1) * blk].astype(jnp.bfloat16)
            else:
                out_ref[i, :, columns] = total


def product(cycle, offsets, index, left, right, total, starts, rows, target=None, last=False, step=2):
    count, sides = len(offsets), len(starts)
    size, slots, blk, _ = left[0][0].shape
    step = min(step, size)
    each = size // step
    inner_width = right.shape[1]

    def of_side(s):
        if s == 0:
            return lambda g, *p: (jnp.minimum(g, each - 1), 0, 0, 0)
        return lambda g, *p: (jnp.maximum(g - each, 0), 0, 0, 0)

    def place(g):
        if sides == 1:
            return starts[0] // step + g
        return jnp.where(g < each, starts[0] // step + g, starts[1] // step + g - each)

    in_specs = [
        pl.BlockSpec((step, slots, blk, blk), of_side(s)) for _ in range(count) for s in range(sides)
    ]
    in_specs += [
        pl.BlockSpec(
            (1, inner_width, blk, BJ * blk), functools.partial(lambda o, g, c, *p: (c[o], 0, 0, 0), o)
        )
        for o in offsets
    ]
    operands = [cycle, *index, *(array for piece in left for array in piece), *([right] * count)]
    aliases = {}
    if total is not None:
        in_specs.append(pl.BlockSpec((step, blk, BJ * blk), lambda g, *p: (place(g), 0, 0)))
        operands.append(total)
        if not last:
            aliases = {len(operands) - 1: 0}
    if target is not None:
        in_specs.append(pl.BlockSpec(memory_space=pl.ANY))
        operands.append(target)
        aliases = {len(operands) - 1: 0}
    if last:
        out_shape = jax.ShapeDtypeStruct((rows, 1, BJ, blk, blk), jnp.bfloat16)
        out_spec = pl.BlockSpec((step, 1, BJ, blk, blk), lambda g, *p: (place(g), 0, 0, 0, 0))
    else:
        out_shape = jax.ShapeDtypeStruct((rows, blk, BJ * blk), jnp.float32)
        out_spec = pl.BlockSpec((step, blk, BJ * blk), lambda g, *p: (place(g), 0, 0))
    wide = BJ * blk * blk * size * sides
    return pl.pallas_call(
        functools.partial(
            product_kernel, offsets, sides, starts, total is not None, last, step
        ),
        out_shape=out_shape,
        grid_spec=pltpu.PrefetchScalarGridSpec(
            num_scalar_prefetch=1 + count,
            grid=(each * sides,),
            in_specs=in_specs,
            out_specs=out_spec,
        ),
        input_output_aliases=aliases,
        compiler_params=pltpu.CompilerParams(vmem_limit_bytes=VMEM_LIMIT),
        cost_estimate=pl.CostEstimate(
            flops=2 * wide * blk * slots * count,
            bytes_accessed=wide * (2 if last else 4)
            + (wide * 4 if total is not None else 0)
            + count * (size * sides * slots + inner_width * BJ) * blk * blk * 2,
            transcendentals=0,
        ),
    )(*operands)


def body(a_values, a_index, b_values, b_index):
    n = lax.axis_size("row")
    order = ring_order(n)
    ahead = [(order[q], order[(q + 1) % n]) for q in range(n)]
    back = [(dst, src) for src, dst in ahead]
    whole_steps = n // 2 - 1
    rows, _, slots, blk, _ = a_values.shape
    half = rows // 2

    swap = [(0, 1), (1, 0)]
    own = (a_values[:, 0], a_index.reshape(-1))
    from_behind, from_ahead = [own], [own]

    def advance():
        behind, ahead_of = from_behind[-1], from_ahead[-1]
        from_behind.append(tuple(lax.ppermute(x, "row", ahead) for x in behind[::-1])[::-1])
        from_ahead.append(tuple(lax.ppermute(x, "row", back) for x in ahead_of[::-1])[::-1])

    advance()
    col = lax.axis_index("col")
    stored, stored_index = b_values[:, 0], b_index.reshape(-1)
    other = lax.ppermute(stored, "col", swap)
    other_index = lax.ppermute(stored_index, "col", swap)
    inner_width = 2 * stored.shape[0] // n
    right = densify(col[None], stored_index, other_index, stored, other, n // 2, inner_width)

    around = np.array([[order[(order.index(r) + o) % n] for o in range(n)] for r in range(n)])
    cycle = lax.dynamic_index_in_dim(
        jnp.asarray(around, jnp.int32), lax.axis_index("row"), 0, keepdims=False
    )

    from_behind[1], from_ahead[1], right = lax.optimization_barrier(
        (from_behind[1], from_ahead[1], right)
    )
    total = None
    for k in range(1, whole_steps + 1):
        if k < whole_steps:
            advance()
        offsets, items = (n - k, k), [from_behind[k], from_ahead[k]]
        if k == 1:
            offsets, items = (0, *offsets), [own, *items]
        if k == whole_steps:
            cuts = [0, half - half // 4, half]
            low = [
                lax.ppermute(from_behind[-1][0][s:e], "row", ahead) for s, e in zip(cuts, cuts[1:])
            ]
            high = [
                lax.ppermute(from_ahead[-1][0][half + s : half + e], "row", back)
                for s, e in zip(cuts, cuts[1:])
            ]
            far_index = lax.ppermute(from_behind[-1][1], "row", ahead)
        index, left = [i for _, i in items], [[v] for v, _ in items]
        total = product(cycle, offsets, index, left, right, total, (0,), rows)
        if k < whole_steps:
            from_behind[-1], from_ahead[-1], total = lax.optimization_barrier(
                (from_behind[-1], from_ahead[-1], total)
            )
    out = None
    for c in range(2):
        starts = (cuts[c], half + cuts[c])
        left = [[low[c], high[c]]]
        out = product(cycle, (n // 2,), [far_index], left, right, total, starts, rows, out, True)
    return out


def solution(mesh):
    placed = (
        P(("groups", "col"), "row", None, None, None),
        P(("groups", "col"), "row", None),
        P(("groups", "col"), "row", None, None, None),
        P(("groups", "col"), "row", None),
    )
    return jax.shard_map(
        body,
        mesh=mesh,
        in_specs=placed,
        out_specs=P(("groups", "col"), "row", None, None, None),
        check_vma=False,
    )
```

time: 216 us -> 95.9 us (0.44)
  waiting for transfers between devices: 101 us -> 36.4 us
  matrix products: 34.7 us -> 0 us
  local copies, waits for them, and re-layouts: 43.4 us -> 10.7 us
  Pallas kernels: 0 us -> 29 us
  blocking collectives: 22.3 us -> 0 us
  starting transfers between devices: 0.04 us -> 19.3 us
  between operations: 13.5 us -> 0.12 us
    all_gather x2 -> x0, waiting for transfers between devices: 100 us -> none  [the longest x1 100 us: body(): lax.all_gather(a_values, 'row', axis=1, tiled=True)]
    ppermute x0 -> x19, waiting for transfers between devices: none -> 36.4 us  [the longest x6 25.4 us: advance(): lax.ppermute(x, 'row', ahead)]
    dot_general x2 -> x0, matrix products: 34.7 us -> none  [the longest x1 32.7 us: body(): jnp.einsum('insxy,insjyz->ijxz', masked, chosen, preferred_element_type=j...]
    pallas_call x0 -> x6, Pallas kernels: none -> 29 us  [the longest x5 23.1 us: product(): pl.pallas_call(functools.partial(product_kernel, offsets, sides, starts,...]
    gather x1 -> x0, local copies, waits for them, and re-layouts: 27 us -> none  [body(): chosen = right_dense[inner]]
    all_gather x1 -> x0, blocking collectives: 22.3 us -> none  [body(): lax.all_gather(a_index, 'row', axis=1, tiled=True)]
    ppermute x0 -> x19, starting transfers between devices: none -> 19.3 us  [the longest x6 8.49 us: advance(): lax.ppermute(x, 'row', back)]
    unnamed x4 -> x10, local copies, waits for them, and re-layouts: 0.7 us -> 9.74 us
  transfers between devices with their start and end apart: 2 -> 19, of which waited for: 1 -> 6; matrix products, arithmetic and copies ran while one was open for 13% -> 3% of each run, Pallas kernels for 0% -> 28%
where the time goes in v1:
time: 95.9 us; the launch traced here: 95.5 us
  waiting for transfers between devices  36.4 us (38%)
  Pallas kernels  29 us (30%)
  starting transfers between devices  19.3 us (20%)
  local copies, waits for them, and re-layouts  10.7 us (11%)
    ppermute x6, waiting for transfers between devices, advance(): lax.ppermute(x, 'row', ahead)  25.4 us
    pallas_call x5, Pallas kernels, product(): pl.pallas_call(functools.partial(product_kernel, offsets, sides, starts,...  23.1 us
    ppermute x6, waiting for transfers between devices, advance(): lax.ppermute(x, 'row', back)  11 us
    unnamed x10, local copies, waits for them, and re-layouts  9.74 us
    ppermute x6, starting transfers between devices, advance(): lax.ppermute(x, 'row', back)  8.49 us
    pallas_call x1, Pallas kernels, densify(): pl.pallas_call(densify_kernel, out_shape=jax.ShapeDtypeStruct((2 * pieces...  5.9 us
    ppermute x6, starting transfers between devices, advance(): lax.ppermute(x, 'row', ahead)  4.38 us
    ppermute x2, starting transfers between devices, body(): lax.ppermute(from_behind[-1][0][s:e], 'row', ahead)  3.13 us
  transfers between devices with their start and end apart: 19, of which 6 were waited for; matrix products, arithmetic and copies ran while one was open for 3% of the time, Pallas kernels for 28%

profile of v1, /device:TPU:0, one launch (start us, length us, event | category | flops | bytes accessed | tf_op | source)
XLA Modules:
  0.0 95.5 jit_solution(5063827942475726699)
XLA Ops:
  0.5 2.5 %collective-permute-start.2 = (bf16[16,2,128,128]{3,2,1,0:T(8,128)(2,1)}, bf16[16,2,128,128]{3,2,1,0:T(8,128)(2,1)}, u32[]{:S(2)}, u32[]{:S(2)}) collective-permute-start(bf16[16,2,128,128]{3,2,1,0:T(8,128)(2,1)} %bitcast.11), channel_id=1, source_target_pairs={{4,0},{8,4},{12,8},{14,12},{10,14},{6,10},{2,6},{0,2},{5,1},{9,5},... | collective-permute-start | bytes 3145736 | tf_op jit(solution)/shard_map/ppermute | solution.py:194
  3.1 0.8 copy.12
  5.0 1.8 %collective-permute-start.3 = (s32[32]{0:T(128)S(1)}, s32[32]{0:T(128)S(1)}, u32[]{:S(2)}, u32[]{:S(2)}) collective-permute-start(s32[32]{0:T(128)S(1)} %reshape.6.refs_1_), channel_id=1, source_target_pairs={{4,0},{8,4},{12,8},{14,12},{10,14},{6,10},{2,6},{0,2},{5,1},{9,5},... | collective-permute-start | bytes 392 | tf_op jit(solution)/shard_map/ppermute | solution.py:194
  7.2 1.6 %copy-done.2 = bf16[16,1,4,128,128]{4,3,2,1,0:T(8,128)(2,1)S(1)} copy-done((bf16[16,1,4,128,128]{4,3,2,1,0:T(8,128)(2,1)S(1)}, bf16[16,1,4,128,128]{4,3,2,1,0:T(8,128)(2,1)}, u32[]{:S(2)}) %copy-start.2) | copy-done | bytes 2097176
  8.7 5.9 %shard_map.55.refs_7_.refs_8_.refs_9_.refs_5_.refs_6_.refs_4_ = bf16[8,4,128,1024]{3,2,1,0:T(8,128)(2,1)S(1)} custom-call(s32[1]{0:T(128)} %bitcast.2.col_ref, s32[64]{0:T(128)S(1)} %reshape.7.own_index, s32[64]{0:T(128)S(1)} %collective-permute-done.4.other_index, bf16[16,4,128,128]{3,2,1,0:T(8,128)(2,1)S(1)} %bitcast.10, ...), custom_call_target="tpu_custom_call" | custom-call | flops 33554432 | bytes 12582912 | tf_op jit(solution)/shard_map/pallas_call | solution.py:43
  14.7 3.2 %copy-done = bf16[8,4,128,1024]{3,2,1,0:T(8,128)(2,1)} copy-done((bf16[8,4,128,1024]{3,2,1,0:T(8,128)(2,1)}, bf16[8,4,128,1024]{3,2,1,0:T(8,128)(2,1)S(1)}, u32[]{:S(2)}) %copy-start) | copy-done | bytes 8388632
  17.9 9.3 %collective-permute-done.3.refs_3_ = s32[32]{0:T(128)S(1)} collective-permute-done((s32[32]{0:T(128)S(1)}, s32[32]{0:T(128)S(1)}, u32[]{:S(2)}, u32[]{:S(2)}) %collective-permute-start.3) | collective-permute-done | bytes 160 | tf_op jit(solution)/shard_map/ppermute | solution.py:194
  27.2 1.4 %collective-permute-done.1.refs_2_ = s32[32]{0:T(128)S(1)} collective-permute-done((s32[32]{0:T(128)S(1)}, s32[32]{0:T(128)S(1)}, u32[]{:S(2)}, u32[]{:S(2)}) %collective-permute-start.1) | collective-permute-done | bytes 160 | tf_op jit(solution)/shard_map/ppermute | solution.py:193
  29.0 1.6 %collective-permute-start.8 = (bf16[16,2,128,128]{3,2,1,0:T(8,128)(2,1)}, bf16[16,2,128,128]{3,2,1,0:T(8,128)(2,1)S(1)}, u32[]{:S(2)}, u32[]{:S(2)}) collective-permute-start(bf16[16,2,128,128]{3,2,1,0:T(8,128)(2,1)} %collective-permute-done.2.refs_6_), channel_id=1, source_target_pairs={{4,0},{8,4},{12,8},{14,12},{10,14},{6,10},{2,6},{0,2},{5,1},{9,5},... | collective-permute-start | bytes 3145736 | tf_op jit(solution)/shard_map/ppermute | solution.py:194
  31.7 1.6 %collective-permute-start.9 = (s32[32]{0:T(128)S(1)}, s32[32]{0:T(128)S(1)}, u32[]{:S(2)}, u32[]{:S(2)}) collective-permute-start(s32[32]{0:T(128)S(1)} %collective-permute-done.3.refs_3_), channel_id=1, source_target_pairs={{4,0},{8,4},{12,8},{14,12},{10,14},{6,10},{2,6},{0,2},{5,1},{9,5},... | collective-permute-start | bytes 392 | tf_op jit(solution)/shard_map/ppermute | solution.py:194
  33.3 3.4 %copy-done.1 = bf16[8,4,128,1024]{3,2,1,0:T(8,128)(2,1)S(1)} copy-done((bf16[8,4,128,1024]{3,2,1,0:T(8,128)(2,1)S(1)}, bf16[8,4,128,1024]{3,2,1,0:T(8,128)(2,1)}, u32[]{:S(2)}) %copy-start.1) | copy-done | bytes 8388632
  36.7 7.5 %shard_map.56.refs_7_ = f32[16,128,1024]{2,1,0:T(8,128)S(1)} custom-call(s32[8]{0:T(128)S(1)} %dynamic-slice_bitcast_fusion.refs_0_, s32[32]{0:T(128)S(1)} %reshape.6.refs_1_, s32[32]{0:T(128)S(1)} %collective-permute-done.1.refs_2_, s32[32]{0:T(128)S(1)} %collective-permute-done.3.refs_3_, bf16[16,2,128,128]{3,2,1,0:T(8,128)(2,1)S(1)} %bitcast.13, ...), custom_call_target="tpu_custom_call" | custom-call | flops 3221225472 | bytes 14680064 | tf_op jit(solution)/shard_map/pallas_call | solution.py:155
  44.3 9.1 %collective-permute-done.7.refs_1_ = s32[32]{0:T(128)S(1)} collective-permute-done((s32[32]{0:T(128)S(1)}, s32[32]{0:T(128)S(1)}, u32[]{:S(2)}, u32[]{:S(2)}) %collective-permute-start.7) | collective-permute-done | bytes 160 | tf_op jit(solution)/shard_map/ppermute | solution.py:193
  53.8 1.6 %collective-permute-start.10 = (bf16[16,2,128,128]{3,2,1,0:T(8,128)(2,1)S(1)}, bf16[16,2,128,128]{3,2,1,0:T(8,128)(2,1)S(1)}, u32[]{:S(2)}, u32[]{:S(2)}) collective-permute-start(bf16[16,2,128,128]{3,2,1,0:T(8,128)(2,1)S(1)} %collective-permute-done.6.refs_3_), channel_id=1, source_target_pairs={{0,4},{4,8},{8,12},{12,14},{14,10},{10,6},{6,2},{2,0},{1,5},{5,9},... | collective-permute-start | bytes 3145736 | tf_op jit(solution)/shard_map/ppermute | solution.py:193
  55.8 1.6 %collective-permute-start.11 = (s32[32]{0:T(128)S(1)}, s32[32]{0:T(128)S(1)}, u32[]{:S(2)}, u32[]{:S(2)}) collective-permute-start(s32[32]{0:T(128)S(1)} %collective-permute-done.7.refs_1_), channel_id=1, source_target_pairs={{0,4},{4,8},{8,12},{12,14},{14,10},{10,6},{6,2},{2,0},{1,5},{5,9},... | collective-permute-start | bytes 392 | tf_op jit(solution)/shard_map/ppermute | solution.py:193
  57.8 4.6 %shard_map.57.refs_7_ = f32[16,128,1024]{2,1,0:T(8,128)S(1)} custom-call(s32[8]{0:T(128)S(1)} %dynamic-slice_bitcast_fusion.refs_0_, s32[32]{0:T(128)S(1)} %collective-permute-done.7.refs_1_, s32[32]{0:T(128)S(1)} %collective-permute-done.9.refs_2_, bf16[16,2,128,128]{3,2,1,0:T(8,128)(2,1)S(1)} %collective-permute-done.6.refs_3_, ...), custom_call_target="tpu_custom_call", output_to_operand_aliasing={{}: (7, {})} | custom-call | flops 2147483648 | bytes 20971520 | tf_op jit(solution)/shard_map/pallas_call | solution.py:155
  62.4 14.9 %collective-permute-done.11.refs_1_ = s32[32]{0:T(128)S(1)} collective-permute-done((s32[32]{0:T(128)S(1)}, s32[32]{0:T(128)S(1)}, u32[]{:S(2)}, u32[]{:S(2)}) %collective-permute-start.11) | collective-permute-done | bytes 160 | tf_op jit(solution)/shard_map/ppermute | solution.py:193
  77.4 1.3 %collective-permute-done.13.refs_2_ = s32[32]{0:T(128)S(1)} collective-permute-done((s32[32]{0:T(128)S(1)}, s32[32]{0:T(128)S(1)}, u32[]{:S(2)}, u32[]{:S(2)}) %collective-permute-start.13) | collective-permute-done | bytes 160 | tf_op jit(solution)/shard_map/ppermute | solution.py:194
  79.2 1.6 %collective-permute-start.17 = (bf16[6,2,128,128]{3,2,1,0:T(8,128)(2,1)S(1)}, bf16[6,2,128,128]{3,2,1,0:T(8,128)(2,1)S(1)}, u32[]{:S(2)}, u32[]{:S(2)}) collective-permute-start(bf16[6,2,128,128]{3,2,1,0:T(8,128)(2,1)S(1)} %slice.14), channel_id=1, source_target_pairs={{0,4},{4,8},{8,12},{12,14},{14,10},{10,6},{6,2},{2,0},{1,5},{5,9},... | collective-permute-start | bytes 1179656 | tf_op jit(solution)/shard_map/ppermute | solution.py:222
  80.8 1.6 %collective-permute-start.14 = (s32[32]{0:T(128)S(1)}, s32[32]{0:T(128)S(1)}, u32[]{:S(2)}, u32[]{:S(2)}) collective-permute-start(s32[32]{0:T(128)S(1)} %collective-permute-done.11.refs_1_), channel_id=1, source_target_pairs={{0,4},{4,8},{8,12},{12,14},{14,10},{10,6},{6,2},{2,0},{1,5},{5,9},... | collective-permute-start | bytes 392 | tf_op jit(solution)/shard_map/ppermute | solution.py:228
  82.9 1.6 %collective-permute-start.15 = (bf16[2,2,128,128]{3,2,1,0:T(8,128)(2,1)S(1)}, bf16[2,2,128,128]{3,2,1,0:T(8,128)(2,1)S(1)}, u32[]{:S(2)}, u32[]{:S(2)}) collective-permute-start(bf16[2,2,128,128]{3,2,1,0:T(8,128)(2,1)S(1)} %slice.12), channel_id=1, source_target_pairs={{0,4},{4,8},{8,12},{12,14},{14,10},{10,6},{6,2},{2,0},{1,5},{5,9},... | collective-permute-start | bytes 393224 | tf_op jit(solution)/shard_map/ppermute | solution.py:222
  84.5 4.7 %shard_map.58.refs_5_ = f32[16,128,1024]{2,1,0:T(8,128)S(1)} custom-call(s32[8]{0:T(128)S(1)} %dynamic-slice_bitcast_fusion.refs_0_, s32[32]{0:T(128)S(1)} %collective-permute-done.11.refs_1_, s32[32]{0:T(128)S(1)} %collective-permute-done.13.refs_2_, bf16[16,2,128,128]{3,2,1,0:T(8,128)(2,1)S(1)} %collective-permute-done.10.refs_3_, ...), custom_call_target="tpu_custom_call", output_to_operand_aliasing={{}: (7, {})} | custom-call | flops 2147483648 | bytes 20971520 | tf_op jit(solution)/shard_map/pallas_call | solution.py:155
  89.2 4.3 %shard_map.59.refs_6_ = bf16[16,1,8,128,128]{4,3,2,1,0:T(8,128)(2,1)} custom-call(s32[8]{0:T(128)S(1)} %dynamic-slice_bitcast_fusion.refs_0_, s32[32]{0:T(128)S(1)} %collective-permute-done.14.refs_1_, bf16[6,2,128,128]{3,2,1,0:T(8,128)(2,1)S(1)} %collective-permute-done.17.refs_2_, bf16[6,2,128,128]{3,2,1,0:T(8,128)(2,1)S(1)} %collective-permute-done.18.refs_3_, ...), custom_call_target="tpu_custom_call" | custom-call | flops 805306368 | bytes 11272192 | tf_op jit(solution)/shard_map/pallas_call | solution.py:155
  93.5 2.0 %shard_map.60 = bf16[16,1,8,128,128]{4,3,2,1,0:T(8,128)(2,1)} custom-call(s32[8]{0:T(128)S(1)} %dynamic-slice_bitcast_fusion.refs_0_, s32[32]{0:T(128)S(1)} %collective-permute-done.14.refs_1_, bf16[2,2,128,128]{3,2,1,0:T(8,128)(2,1)S(1)} %collective-permute-done.15.refs_2_, ...), custom_call_target="tpu_custom_call", output_to_operand_aliasing={{}: (6, {})} | custom-call | flops 268435456 | bytes 4456448 | tf_op jit(solution)/shard_map/pallas_call | solution.py:155
  (37 shorter events, 6.0 us)
Async XLA Ops:
  0.0 7.1 %collective-permute-start.5 = (bf16[16,4,128,128]{3,2,1,0:T(8,128)(2,1)}, bf16[16,4,128,128]{3,2,1,0:T(8,128)(2,1)S(1)}, u32[]{:S(2)}, u32[]{:S(2)}) collective-permute-start(bf16[16,4,128,128]{3,2,1,0:T(8,128)(2,1)} %bitcast.9), channel_id=1, source_target_pairs={{0,1},{1,0},{2,3},{3,2},{4,5},{5,4},{6,7},{7,6},{8,9},{9,8},{10,11... | collective-permute-start | bytes 6291464 | tf_op jit(solution)/shard_map/ppermute | solution.py:199
  0.5 28.1 %collective-permute-start.2 = (bf16[16,2,128,128]{3,2,1,0:T(8,128)(2,1)}, bf16[16,2,128,128]{3,2,1,0:T(8,128)(2,1)}, u32[]{:S(2)}, u32[]{:S(2)}) collective-permute-start(bf16[16,2,128,128]{3,2,1,0:T(8,128)(2,1)} %bitcast.11), channel_id=1, source_target_pairs={{4,0},{8,4},{12,8},{14,12},{10,14},{6,10},{2,6},{0,2},{5,1},{9,5},... | collective-permute-start | bytes 3145736 | tf_op jit(solution)/shard_map/ppermute | solution.py:194
  3.0 25.6 %collective-permute-start = (bf16[16,2,128,128]{3,2,1,0:T(8,128)(2,1)}, bf16[16,2,128,128]{3,2,1,0:T(8,128)(2,1)}, u32[]{:S(2)}, u32[]{:S(2)}) collective-permute-start(bf16[16,2,128,128]{3,2,1,0:T(8,128)(2,1)} %bitcast.12), channel_id=1, source_target_pairs={{0,4},{4,8},{8,12},{12,14},{14,10},{10,6},{6,2},{2,0},{1,5},{5,9},... | collective-permute-start | bytes 3145736 | tf_op jit(solution)/shard_map/ppermute | solution.py:193
  3.9 2.9 %collective-permute-start.4 = (s32[64]{0:T(128)S(1)}, s32[64]{0:T(128)S(1)}, u32[]{:S(2)}, u32[]{:S(2)}) collective-permute-start(s32[64]{0:T(128)S(1)} %reshape.7.own_index), channel_id=1, source_target_pairs={{0,1},{1,0},{2,3},{3,2},{4,5},{5,4},{6,7},{7,6},{8,9},{9,8},{10,11... | collective-permute-start | bytes 776 | tf_op jit(solution)/shard_map/ppermute | solution.py:200
  5.0 22.2 %collective-permute-start.3 = (s32[32]{0:T(128)S(1)}, s32[32]{0:T(128)S(1)}, u32[]{:S(2)}, u32[]{:S(2)}) collective-permute-start(s32[32]{0:T(128)S(1)} %reshape.6.refs_1_), channel_id=1, source_target_pairs={{4,0},{8,4},{12,8},{14,12},{10,14},{6,10},{2,6},{0,2},{5,1},{9,5},... | collective-permute-start | bytes 392 | tf_op jit(solution)/shard_map/ppermute | solution.py:194
  6.8 21.8 %collective-permute-start.1 = (s32[32]{0:T(128)S(1)}, s32[32]{0:T(128)S(1)}, u32[]{:S(2)}, u32[]{:S(2)}) collective-permute-start(s32[32]{0:T(128)S(1)} %reshape.6.refs_1_), channel_id=1, source_target_pairs={{0,4},{4,8},{8,12},{12,14},{14,10},{10,6},{6,2},{2,0},{1,5},{5,9},... | collective-permute-start | bytes 392 | tf_op jit(solution)/shard_map/ppermute | solution.py:193
  7.1 1.6 %copy-start.2 = (bf16[16,1,4,128,128]{4,3,2,1,0:T(8,128)(2,1)S(1)}, bf16[16,1,4,128,128]{4,3,2,1,0:T(8,128)(2,1)}, u32[]{:S(2)}) copy-start(bf16[16,1,4,128,128]{4,3,2,1,0:T(8,128)(2,1)} %param.7) | copy-start | bytes 6291460
  8.7 24.6 %copy-start.3 = (bf16[16,1,2,128,128]{4,3,2,1,0:T(8,128)(2,1)S(1)}, bf16[16,1,2,128,128]{4,3,2,1,0:T(8,128)(2,1)}, u32[]{:S(2)}) copy-start(bf16[16,1,2,128,128]{4,3,2,1,0:T(8,128)(2,1)} %param.5) | copy-start | bytes 3145732
  14.7 3.3 %copy-start = (bf16[8,4,128,1024]{3,2,1,0:T(8,128)(2,1)}, bf16[8,4,128,1024]{3,2,1,0:T(8,128)(2,1)S(1)}, u32[]{:S(2)}) copy-start(bf16[8,4,128,1024]{3,2,1,0:T(8,128)(2,1)S(1)} %shard_map.55.refs_7_.refs_8_.refs_9_.refs_5_.refs_6_.refs_4_) | copy-start | bytes 25165828
  28.6 25.2 %collective-permute-start.6 = (bf16[16,2,128,128]{3,2,1,0:T(8,128)(2,1)}, bf16[16,2,128,128]{3,2,1,0:T(8,128)(2,1)S(1)}, u32[]{:S(2)}, u32[]{:S(2)}) collective-permute-start(bf16[16,2,128,128]{3,2,1,0:T(8,128)(2,1)} %collective-permute-done.refs_5_), channel_id=1, source_target_pairs={{0,4},{4,8},{8,12},{12,14},{14,10},{10,6},{6,2},{2,0},{1,5},{5,9},... | collective-permute-start | bytes 3145736 | tf_op jit(solution)/shard_map/ppermute | solution.py:193
  29.0 24.8 %collective-permute-start.8 = (bf16[16,2,128,128]{3,2,1,0:T(8,128)(2,1)}, bf16[16,2,128,128]{3,2,1,0:T(8,128)(2,1)S(1)}, u32[]{:S(2)}, u32[]{:S(2)}) collective-permute-start(bf16[16,2,128,128]{3,2,1,0:T(8,128)(2,1)} %collective-permute-done.2.refs_6_), channel_id=1, source_target_pairs={{4,0},{8,4},{12,8},{14,12},{10,14},{6,10},{2,6},{0,2},{5,1},{9,5},... | collective-permute-start | bytes 3145736 | tf_op jit(solution)/shard_map/ppermute | solution.py:194
  31.3 22.0 %collective-permute-start.7 = (s32[32]{0:T(128)S(1)}, s32[32]{0:T(128)S(1)}, u32[]{:S(2)}, u32[]{:S(2)}) collective-permute-start(s32[32]{0:T(128)S(1)} %collective-permute-done.1.refs_2_), channel_id=1, source_target_pairs={{0,4},{4,8},{8,12},{12,14},{14,10},{10,6},{6,2},{2,0},{1,5},{5,9},... | collective-permute-start | bytes 392 | tf_op jit(solution)/shard_map/ppermute | solution.py:193
  31.7 22.1 %collective-permute-start.9 = (s32[32]{0:T(128)S(1)}, s32[32]{0:T(128)S(1)}, u32[]{:S(2)}, u32[]{:S(2)}) collective-permute-start(s32[32]{0:T(128)S(1)} %collective-permute-done.3.refs_3_), channel_id=1, source_target_pairs={{4,0},{8,4},{12,8},{14,12},{10,14},{6,10},{2,6},{0,2},{5,1},{9,5},... | collective-permute-start | bytes 392 | tf_op jit(solution)/shard_map/ppermute | solution.py:194
  33.3 3.4 %copy-start.1 = (bf16[8,4,128,1024]{3,2,1,0:T(8,128)(2,1)S(1)}, bf16[8,4,128,1024]{3,2,1,0:T(8,128)(2,1)}, u32[]{:S(2)}) copy-start(bf16[8,4,128,1024]{3,2,1,0:T(8,128)(2,1)} %copy-done) | copy-start | bytes 25165828
  53.8 24.9 %collective-permute-start.10 = (bf16[16,2,128,128]{3,2,1,0:T(8,128)(2,1)S(1)}, bf16[16,2,128,128]{3,2,1,0:T(8,128)(2,1)S(1)}, u32[]{:S(2)}, u32[]{:S(2)}) collective-permute-start(bf16[16,2,128,128]{3,2,1,0:T(8,128)(2,1)S(1)} %collective-permute-done.6.refs_3_), channel_id=1, source_target_pairs={{0,4},{4,8},{8,12},{12,14},{14,10},{10,6},{6,2},{2,0},{1,5},{5,9},... | collective-permute-start | bytes 3145736 | tf_op jit(solution)/shard_map/ppermute | solution.py:193
  55.4 23.3 %collective-permute-start.12 = (bf16[16,2,128,128]{3,2,1,0:T(8,128)(2,1)S(1)}, bf16[16,2,128,128]{3,2,1,0:T(8,128)(2,1)S(1)}, u32[]{:S(2)}, u32[]{:S(2)}) collective-permute-start(bf16[16,2,128,128]{3,2,1,0:T(8,128)(2,1)S(1)} %collective-permute-done.8.refs_4_), channel_id=1, source_target_pairs={{4,0},{8,4},{12,8},{14,12},{10,14},{6,10},{2,6},{0,2},{5,1},{9,5},... | collective-permute-start | bytes 3145736 | tf_op jit(solution)/shard_map/ppermute | solution.py:194
  55.8 21.6 %collective-permute-start.11 = (s32[32]{0:T(128)S(1)}, s32[32]{0:T(128)S(1)}, u32[]{:S(2)}, u32[]{:S(2)}) collective-permute-start(s32[32]{0:T(128)S(1)} %collective-permute-done.7.refs_1_), channel_id=1, source_target_pairs={{0,4},{4,8},{8,12},{12,14},{14,10},{10,6},{6,2},{2,0},{1,5},{5,9},... | collective-permute-start | bytes 392 | tf_op jit(solution)/shard_map/ppermute | solution.py:193
  57.4 21.2 %collective-permute-start.13 = (s32[32]{0:T(128)S(1)}, s32[32]{0:T(128)S(1)}, u32[]{:S(2)}, u32[]{:S(2)}) collective-permute-start(s32[32]{0:T(128)S(1)} %collective-permute-done.9.refs_2_), channel_id=1, source_target_pairs={{4,0},{8,4},{12,8},{14,12},{10,14},{6,10},{2,6},{0,2},{5,1},{9,5},... | collective-permute-start | bytes 392 | tf_op jit(solution)/shard_map/ppermute | solution.py:194
  78.7 10.5 %collective-permute-start.18 = (bf16[6,2,128,128]{3,2,1,0:T(8,128)(2,1)S(1)}, bf16[6,2,128,128]{3,2,1,0:T(8,128)(2,1)S(1)}, u32[]{:S(2)}, u32[]{:S(2)}) collective-permute-start(bf16[6,2,128,128]{3,2,1,0:T(8,128)(2,1)S(1)} %slice.15), channel_id=1, source_target_pairs={{4,0},{8,4},{12,8},{14,12},{10,14},{6,10},{2,6},{0,2},{5,1},{9,5},... | collective-permute-start | bytes 1179656 | tf_op jit(solution)/shard_map/ppermute | solution.py:225
  79.2 10.0 %collective-permute-start.17 = (bf16[6,2,128,128]{3,2,1,0:T(8,128)(2,1)S(1)}, bf16[6,2,128,128]{3,2,1,0:T(8,128)(2,1)S(1)}, u32[]{:S(2)}, u32[]{:S(2)}) collective-permute-start(bf16[6,2,128,128]{3,2,1,0:T(8,128)(2,1)S(1)} %slice.14), channel_id=1, source_target_pairs={{0,4},{4,8},{8,12},{12,14},{14,10},{10,6},{6,2},{2,0},{1,5},{5,9},... | collective-permute-start | bytes 1179656 | tf_op jit(solution)/shard_map/ppermute | solution.py:222
  80.8 8.3 %collective-permute-start.14 = (s32[32]{0:T(128)S(1)}, s32[32]{0:T(128)S(1)}, u32[]{:S(2)}, u32[]{:S(2)}) collective-permute-start(s32[32]{0:T(128)S(1)} %collective-permute-done.11.refs_1_), channel_id=1, source_target_pairs={{0,4},{4,8},{8,12},{12,14},{14,10},{10,6},{6,2},{2,0},{1,5},{5,9},... | collective-permute-start | bytes 392 | tf_op jit(solution)/shard_map/ppermute | solution.py:228
  82.4 11.0 %collective-permute-start.16 = (bf16[2,2,128,128]{3,2,1,0:T(8,128)(2,1)S(1)}, bf16[2,2,128,128]{3,2,1,0:T(8,128)(2,1)S(1)}, u32[]{:S(2)}, u32[]{:S(2)}) collective-permute-start(bf16[2,2,128,128]{3,2,1,0:T(8,128)(2,1)S(1)} %slice.13), channel_id=1, source_target_pairs={{4,0},{8,4},{12,8},{14,12},{10,14},{6,10},{2,6},{0,2},{5,1},{9,5},... | collective-permute-start | bytes 393224 | tf_op jit(solution)/shard_map/ppermute | solution.py:225
  82.9 10.6 %collective-permute-start.15 = (bf16[2,2,128,128]{3,2,1,0:T(8,128)(2,1)S(1)}, bf16[2,2,128,128]{3,2,1,0:T(8,128)(2,1)S(1)}, u32[]{:S(2)}, u32[]{:S(2)}) collective-permute-start(bf16[2,2,128,128]{3,2,1,0:T(8,128)(2,1)S(1)} %slice.12), channel_id=1, source_target_pairs={{0,4},{4,8},{8,12},{12,14},{14,10},{10,6},{6,2},{2,0},{1,5},{5,9},... | collective-permute-start | bytes 393224 | tf_op jit(solution)/shard_map/ppermute | solution.py:222

commit v2 on v1

v2 whole, which is shorter than its diff:
```python
import functools

import jax
import jax.numpy as jnp
import numpy as np
from jax import lax
from jax.experimental import pallas as pl
from jax.experimental.pallas import tpu as pltpu
from jax.sharding import PartitionSpec as P

BJ = 8
NOTE_ROWS = 16
VMEM_LIMIT = 20 * 1024 * 1024


def ring_order(n):
    if n == 8:
        return (0, 2, 4, 6, 7, 5, 3, 1)
    return tuple(range(n))


def densify_kernel(col_ref, own_index, other_index, own_ref, other_ref, dense_ref):
    source = pl.program_id(0)
    first = pl.program_id(1) * own_ref.shape[0]
    blk = own_ref.shape[-1]
    slots = own_ref.shape[1]
    for k in range(own_ref.shape[0]):
        stored = [
            jnp.where(source == 0, own_ref[k, t], other_ref[k, t]).astype(jnp.float32)
            for t in range(slots)
        ]
        at = [(first + k) * slots + t for t in range(slots)]
        columns = [jnp.where(source == 0, own_index[i], other_index[i]) for i in at]
        for j in range(BJ):
            total = jnp.zeros((blk, blk), jnp.float32)
            for t in range(slots):
                total = total + jnp.where(columns[t] == j, stored[t], 0.0)
            dense_ref[0, k, :, j * blk : (j + 1) * blk] = total.astype(jnp.bfloat16)


def densify(col, own_index, other_index, own, other, pieces, inner_width):
    slots, blk = own.shape[1], own.shape[-1]
    stored = (inner_width, slots, blk, blk)
    return pl.pallas_call(
        densify_kernel,
        out_shape=jax.ShapeDtypeStruct((2 * pieces, inner_width, blk, BJ * blk), jnp.bfloat16),
        grid_spec=pltpu.PrefetchScalarGridSpec(
            num_scalar_prefetch=3,
            grid=(2, pieces),
            in_specs=[
                pl.BlockSpec(stored, lambda s, g, c, *i: (jnp.where(s == 0, g, pieces - 1), 0, 0, 0)),
                pl.BlockSpec(stored, lambda s, g, c, *i: (jnp.where(s == 0, 0, g), 0, 0, 0)),
            ],
            out_specs=pl.BlockSpec(
                (1, inner_width, blk, BJ * blk),
                lambda s, g, c, *i: (jnp.where(s == 0, c[0], 1 - c[0]) * pieces + g, 0, 0, 0),
            ),
        ),
        compiler_params=pltpu.CompilerParams(vmem_limit_bytes=VMEM_LIMIT),
        name="densify",
        cost_estimate=pl.CostEstimate(flops=0, bytes_accessed=0, transcendentals=0),
    )(col, own_index, other_index, own, other)


def product_kernel(offsets, sides, starts, has_total, step, *refs):
    count = len(offsets)
    index = refs[1 : 1 + count]
    refs = refs[1 + count :]
    left = refs[: count * sides]
    right = refs[count * sides : count * (sides + 1)]
    rest = refs[count * (sides + 1) :]
    out_ref, held = (rest[-2], rest[-1]) if sides == 2 else (rest[-1], None)
    total_ref = rest[0] if has_total else None
    slots, blk = index[0].shape[0], left[0].shape[-1]
    wide = 2 * blk
    g = pl.program_id(0)
    if sides == 2:
        each = pl.num_programs(0) // 2
        second = g >= each
        row0 = jnp.where(second, starts[1] + (g - each) * step, starts[0] + g * step)
    else:
        row0 = starts[0] + g * step
    if sides == 2:
        for m in range(count):

            @pl.when(g < each)
            def _(m=m):
                held[m] = left[m * 2][...]

            @pl.when(g >= each)
            def _(m=m):
                held[m] = left[m * 2 + 1][...]

    for i in range(step):
        factors = []
        for m in range(count):
            inner = [index[m][s, row0 + i] for s in range(slots)]
            parts = []
            for s in range(slots):
                at = slice((i * slots + s) * blk, (i * slots + s + 1) * blk)
                part = left[m][at, :] if sides == 1 else held[m, at, :]
                parts.append(part * jnp.where(inner[s] >= 0, 1.0, 0.0).astype(jnp.bfloat16))
            factors.append((jnp.concatenate(parts, axis=1), [jnp.maximum(k, 0) for k in inner]))
        for c in range(BJ // 2):
            columns = slice(c * wide, (c + 1) * wide)
            total = total_ref[i, :, columns] if has_total else None
            for m in range(count):
                row, inner = factors[m]
                rows_of = jnp.concatenate([right[m][0, k, :, columns] for k in inner], axis=0)
                term = jnp.dot(row, rows_of, preferred_element_type=jnp.float32)
                total = term if total is None else total + term
            out_ref[i, :, columns] = total


def product(cycle, offsets, index, left, right, total, starts, size, rows, step=4):
    count, sides = len(offsets), len(starts)
    slots, blk = index[0].shape[0], left[0][0].shape[-1]
    each = size // step
    inner_width = right.shape[1]

    def of_side(s):
        if s == 0:
            return lambda g, *p: (jnp.minimum(g, each - 1), 0)
        return lambda g, *p: (jnp.maximum(g - each, 0), 0)

    def place(g):
        if sides == 1:
            return starts[0] // step + g
        return jnp.where(g < each, starts[0] // step + g, starts[1] // step + g - each)

    in_specs = [
        pl.BlockSpec((step * slots * blk, blk), of_side(s)) for _ in range(count) for s in range(sides)
    ]
    in_specs += [
        pl.BlockSpec(
            (1, inner_width, blk, BJ * blk), functools.partial(lambda o, g, c, *p: (c[o], 0, 0, 0), o)
        )
        for o in offsets
    ]
    operands = [cycle, *index, *(array for piece in left for array in piece), *([right] * count)]
    aliases = {}
    if total is not None:
        in_specs.append(pl.BlockSpec((step, blk, BJ * blk), lambda g, *p: (place(g), 0, 0)))
        operands.append(total)
        aliases = {len(operands) - 1: 0}
    out_shape = jax.ShapeDtypeStruct((rows, blk, BJ * blk), jnp.float32)
    out_spec = pl.BlockSpec((step, blk, BJ * blk), lambda g, *p: (place(g), 0, 0))
    return pl.pallas_call(
        functools.partial(
            product_kernel, offsets, sides, starts, total is not None, step
        ),
        out_shape=out_shape,
        grid_spec=pltpu.PrefetchScalarGridSpec(
            num_scalar_prefetch=1 + count,
            grid=(each * sides,),
            in_specs=in_specs,
            out_specs=out_spec,
            scratch_shapes=[pltpu.VMEM((count, step * slots * blk, blk), jnp.bfloat16)] * (sides - 1),
        ),
        input_output_aliases=aliases,
        compiler_params=pltpu.CompilerParams(vmem_limit_bytes=VMEM_LIMIT),
        name="product",
        cost_estimate=pl.CostEstimate(flops=0, bytes_accessed=0, transcendentals=0),
    )(*operands)


def finish_kernel(offset, starts, size, cycle, index, low, high, right, total, *refs):
    out_ref, staged, sems = refs[-3:]
    slots, blk = index.shape[0], low.shape[-1]
    wide = 2 * blk
    copies = []
    for half_ref, start in ((low, starts[0]), (high, starts[1])):
        for i in range(size):
            row, at = start + i, len(copies)
            inner = [index[s, row] for s in range(slots)]
            parts = []
            for s in range(slots):
                part = half_ref[(i * slots + s) * blk : (i * slots + s + 1) * blk, :]
                parts.append(part * jnp.where(inner[s] >= 0, 1.0, 0.0).astype(jnp.bfloat16))
            factor = jnp.concatenate(parts, axis=1)
            for c in range(BJ // 2):
                columns = slice(c * wide, (c + 1) * wide)
                rows_of = jnp.concatenate(
                    [right[0, jnp.maximum(k, 0), :, columns] for k in inner], axis=0
                )
                term = jnp.dot(factor, rows_of, preferred_element_type=jnp.float32)
                result = (total[row, :, columns] + term).astype(jnp.bfloat16)
                for j in range(2):
                    staged[at, c * 2 + j] = result[:, j * blk : (j + 1) * blk]
            copies.append(pltpu.make_async_copy(staged.at[at], out_ref.at[row, 0], sems.at[at]))
            copies[-1].start()
    for copy in copies:
        copy.wait()


def finish(cycle, offset, index, low, high, right, total, starts, size, target):
    rows, blk = total.shape[0], total.shape[1]
    inner_width = right.shape[1]
    whole = pl.BlockSpec(memory_space=pltpu.VMEM)
    piece = pl.BlockSpec(
        (1, inner_width, blk, BJ * blk), lambda g, c, *p: (c[offset], 0, 0, 0)
    )
    operands = [cycle, index, low, high, right, total]
    in_specs = [whole, whole, piece, whole]
    aliases = {}
    if target is not None:
        in_specs.append(pl.BlockSpec(memory_space=pl.ANY))
        operands.append(target)
        aliases = {len(operands) - 1: 0}
    return pl.pallas_call(
        functools.partial(finish_kernel, offset, starts, size),
        out_shape=jax.ShapeDtypeStruct((rows, 1, BJ, blk, blk), jnp.bfloat16),
        grid_spec=pltpu.PrefetchScalarGridSpec(
            num_scalar_prefetch=2,
            grid=(1,),
            in_specs=in_specs,
            out_specs=pl.BlockSpec(memory_space=pl.ANY),
            scratch_shapes=[
                pltpu.VMEM((2 * size, BJ, blk, blk), jnp.bfloat16),
                pltpu.SemaphoreType.DMA((2 * size,)),
            ],
        ),
        input_output_aliases=aliases,
        compiler_params=pltpu.CompilerParams(vmem_limit_bytes=VMEM_LIMIT),
        name="finish",
        cost_estimate=pl.CostEstimate(flops=0, bytes_accessed=0, transcendentals=0),
    )(*operands)


def body(a_values, a_index, b_values, b_index):
    n = lax.axis_size("row")
    order = ring_order(n)
    ahead = [(order[q], order[(q + 1) % n]) for q in range(n)]
    back = [(dst, src) for src, dst in ahead]
    whole_steps = n // 2 - 1
    rows, _, slots, blk, _ = a_values.shape
    half = rows // 2

    swap = [(0, 1), (1, 0)]
    flat = a_values.reshape(rows * slots * blk, blk)
    cut = half * slots * blk
    own_index = a_index[:, 0].T
    note = own_index.astype(jnp.bfloat16)
    note = jnp.pad(note, ((0, NOTE_ROWS - slots), (0, blk - rows)))
    low_first, high_second = jnp.concatenate([flat[:cut], note]), flat[cut:]
    high_first, low_second = jnp.concatenate([flat[cut:], note]), flat[:cut]

    def read_note(message):
        return message[-NOTE_ROWS:][:slots, :rows].astype(jnp.int32)

    def move(array, way, name):
        with jax.named_scope(name):
            return lax.ppermute(array, "row", way)

    behind, beyond = [(low_first, high_second)], [(low_second, high_first)]

    def advance():
        low, high = behind[-1]
        far_low, far_high = beyond[-1]
        low, far_high = move(low, ahead, "low_ahead"), move(far_high, back, "high_back")
        high, far_low = move(high, ahead, "high_ahead"), move(far_low, back, "low_back")
        behind.append((low, high))
        beyond.append((far_low, far_high))

    advance()
    col = lax.axis_index("col")
    stored, stored_index = b_values[:, 0], b_index.reshape(-1)
    other = lax.ppermute(stored, "col", swap)
    other_index = lax.ppermute(stored_index, "col", swap)
    inner_width = 2 * stored.shape[0] // n
    right = densify(col[None], stored_index, other_index, stored, other, n // 2, inner_width)

    around = np.array([[order[(order.index(r) + o) % n] for o in range(n)] for r in range(n)])
    cycle = lax.dynamic_index_in_dim(
        jnp.asarray(around, jnp.int32), lax.axis_index("row"), 0, keepdims=False
    )

    def after(done):
        low, far_high, done = lax.optimization_barrier((behind[-1][0], beyond[-1][1], done))
        behind[-1] = (low, behind[-1][1])
        beyond[-1] = (beyond[-1][0], far_high)
        return done


    right = after(right)
    total = None
    for k in range(1, whole_steps + 1):
        offsets, items = (n - k, k), [behind[k], beyond[k]]
        if k == 1:
            offsets, items = (0, *offsets), [behind[0], *items]
        if k < whole_steps:
            advance()
        else:
            small = half // 4
            at = small * slots * blk
            low, high = behind[-1][0], beyond[-1][1]
            large_parts = (
                small,
                half - small,
                move(low[at:], ahead, "far_low_ahead"),
                move(high[at:], back, "far_high_back"),
            )
        index = [read_note(behind[k][0]), read_note(beyond[k][1])]
        if k == 1:
            index.insert(0, own_index)
        total = product(cycle, offsets, index, items, right, total, (0, half), half, rows)
        if k < whole_steps:
            total = after(total)
    low, high = behind[-1][0][:at], beyond[-1][1][:at]
    small_parts = (0, small, move(low, ahead, "last_low_ahead"), move(high, back, "last_high_back"))
    last_parts = [large_parts, small_parts]
    out = None
    far_index = read_note(last_parts[0][2])
    for start, size, low, high in last_parts:
        starts = (start, half + start)
        out = finish(
            cycle, n // 2, far_index, low, high, right, total, starts, size, out
        )
    return out


def solution(mesh):
    placed = (
        P(("groups", "col"), "row", None, None, None),
        P(("groups", "col"), "row", None),
        P(("groups", "col"), "row", None, None, None),
        P(("groups", "col"), "row", None),
    )
    return jax.shard_map(
        body,
        mesh=mesh,
        in_specs=placed,
        out_specs=P(("groups", "col"), "row", None, None, None),
        check_vma=False,
    )
```

time: 95.9 us -> 90.8 us (0.947)
  waiting for transfers between devices: 36.4 us -> 32.6 us
  Pallas kernels: 29 us -> 26.5 us
  other arithmetic: 0 us -> 2.34 us
  local copies, waits for them, and re-layouts: 10.7 us -> 9.04 us
    pallas_call x5 -> x3, Pallas kernels: 23.1 us -> 14.4 us  [product(): pl.pallas_call(functools.partial(product_kernel, offsets, sides, starts,...]
    pallas_call x0 -> x2, Pallas kernels: none -> 4.41 us  [finish(): pl.pallas_call(functools.partial(finish_kernel, offset, starts, size), ou...]
    ppermute x17 -> x16, waiting for transfers between devices: 36.4 us -> 32.6 us  [move(): return lax.ppermute(array, 'row', way)]
    unnamed x10 -> x13, local copies, waits for them, and re-layouts: 9.74 us -> 6.76 us
    pallas_call x1, Pallas kernels: 5.9 us -> 7.71 us  [densify(): pl.pallas_call(densify_kernel, out_shape=jax.ShapeDtypeStruct((2 * pieces...]
    slice x4 -> x5, local copies, waits for them, and re-layouts: 0.07 us -> 1.49 us  [the longest x1 1.42 us: body(): high_first, low_second = (jnp.concatenate([flat[cut:], note]), flat[:cut])]
    convert_element_type x0 -> x7, other arithmetic: none -> 1.39 us  [the longest x6 0.71 us: read_note(): return message[-NOTE_ROWS:][:slots, :rows].astype(jnp.int32)]
    ppermute x17 -> x16, starting transfers between devices: 18.6 us -> 19.1 us  [move(): return lax.ppermute(array, 'row', way)]
  transfers between devices with their start and end apart: 19 -> 18, of which waited for: 6 -> 12; matrix products, arithmetic and copies ran while one was open for 3% -> 5% of each run, Pallas kernels for 28% -> 27%
where the time goes in v2:
time: 90.8 us; the launch traced here: 90.5 us
  waiting for transfers between devices  32.6 us (36%)
  Pallas kernels  26.5 us (29%)
  starting transfers between devices  19.8 us (22%)
  local copies, waits for them, and re-layouts  9.04 us (10%)
  other arithmetic  2.34 us (3%)
    ppermute x16, waiting for transfers between devices, move(): return lax.ppermute(array, 'row', way)  32.6 us
    ppermute x16, starting transfers between devices, move(): return lax.ppermute(array, 'row', way)  19.1 us
    pallas_call x3, Pallas kernels, product(): pl.pallas_call(functools.partial(product_kernel, offsets, sides, starts,...  14.4 us
    pallas_call x1, Pallas kernels, densify(): pl.pallas_call(densify_kernel, out_shape=jax.ShapeDtypeStruct((2 * pieces...  7.71 us
    unnamed x13, local copies, waits for them, and re-layouts  6.76 us
    pallas_call x2, Pallas kernels, finish(): pl.pallas_call(functools.partial(finish_kernel, offset, starts, size), ou...  4.41 us
  transfers between devices with their start and end apart: 18, of which 12 were waited for; matrix products, arithmetic and copies ran while one was open for 5% of the time, Pallas kernels for 27%

profile of v2, /device:TPU:0, one launch (start us, length us, event | category | flops | bytes accessed | tf_op | source)
XLA Modules:
  0.0 90.5 jit_solution(12622654047793310169)
XLA Ops:
  3.5 2.6 %collective-permute-start = (bf16[2064,128]{1,0:T(8,128)(2,1)S(1)}, bf16[2064,128]{1,0:T(8,128)(2,1)}, u32[]{:S(2)}, u32[]{:S(2)}) collective-permute-start(bf16[2064,128]{1,0:T(8,128)(2,1)S(1)} %get-tuple-element.26.refs_4_), channel_id=1, source_target_pairs={{0,4},{4,8},{8,12},{12,14},{14,10},{10,6},{6,2},{2,0},{1,5},{5,9},... | collective-permute-start | bytes 1585160 | tf_op jit(solution)/shard_map/low_ahead/ppermute | solution.py:253
  6.6 1.9 %collective-permute-start.6 = (bf16[2048,128]{1,0:T(8,128)(2,1)S(1)}, bf16[2048,128]{1,0:T(8,128)(2,1)}, u32[]{:S(2)}, u32[]{:S(2)}) collective-permute-start(bf16[2048,128]{1,0:T(8,128)(2,1)S(1)} %bitcast.13), channel_id=1, source_target_pairs={{0,4},{4,8},{8,12},{12,14},{14,10},{10,6},{6,2},{2,0},{1,5},{5,9},... | collective-permute-start | bytes 1572872 | tf_op jit(solution)/shard_map/high_ahead/ppermute | solution.py:253
  9.5 7.7 %densify.1.refs_10_.refs_11_.refs_12_.refs_7_.refs_8_.right = bf16[8,4,128,1024]{3,2,1,0:T(8,128)(2,1)S(1)} custom-call(s32[1]{0:T(128)} %bitcast.5.col_ref, s32[64]{0:T(128)S(1)} %reshape.6.own_index, s32[64]{0:T(128)S(1)} %collective-permute-done.2.other_index, bf16[16,4,128,128]{3,2,1,0:T(8,128)(2,1)S(1)} %bitcast.16, ...), custom_call_target="tpu_custom_call" | custom-call | tf_op jit(solution)/shard_map/densify/pallas_call | solution.py:44
  17.2 3.3 %copy-done = bf16[8,4,128,1024]{3,2,1,0:T(8,128)(2,1)} copy-done((bf16[8,4,128,1024]{3,2,1,0:T(8,128)(2,1)}, bf16[8,4,128,1024]{3,2,1,0:T(8,128)(2,1)S(1)}, u32[]{:S(2)}) %copy-start) | copy-done | bytes 8388632
  21.3 1.6 %collective-permute-start.4 = (bf16[2064,128]{1,0:T(8,128)(2,1)}, bf16[2064,128]{1,0:T(8,128)(2,1)S(1)}, u32[]{:S(2)}, u32[]{:S(2)}) collective-permute-start(bf16[2064,128]{1,0:T(8,128)(2,1)} %collective-permute-done.refs_6_), channel_id=1, source_target_pairs={{0,4},{4,8},{8,12},{12,14},{14,10},{10,6},{6,2},{2,0},{1,5},{5,9},... | collective-permute-start | bytes 1585160 | tf_op jit(solution)/shard_map/low_ahead/ppermute | solution.py:253
  23.3 7.0 %collective-permute-done.6.refs_7_ = bf16[2048,128]{1,0:T(8,128)(2,1)} collective-permute-done((bf16[2048,128]{1,0:T(8,128)(2,1)S(1)}, bf16[2048,128]{1,0:T(8,128)(2,1)}, u32[]{:S(2)}, u32[]{:S(2)}) %collective-permute-start.6) | collective-permute-done | bytes 524320 | tf_op jit(solution)/shard_map/high_ahead/ppermute | solution.py:253
  30.3 2.0 %collective-permute-start.10 = (bf16[2048,128]{1,0:T(8,128)(2,1)}, bf16[2048,128]{1,0:T(8,128)(2,1)S(1)}, u32[]{:S(2)}, u32[]{:S(2)}) collective-permute-start(bf16[2048,128]{1,0:T(8,128)(2,1)} %collective-permute-done.6.refs_7_), channel_id=1, source_target_pairs={{0,4},{4,8},{8,12},{12,14},{14,10},{10,6},{6,2},{2,0},{1,5},{5,9},... | collective-permute-start | bytes 1572872 | tf_op jit(solution)/shard_map/high_ahead/ppermute | solution.py:253
  33.9 3.4 %copy-done.1 = bf16[8,4,128,1024]{3,2,1,0:T(8,128)(2,1)S(1)} copy-done((bf16[8,4,128,1024]{3,2,1,0:T(8,128)(2,1)S(1)}, bf16[8,4,128,1024]{3,2,1,0:T(8,128)(2,1)}, u32[]{:S(2)}) %copy-start.1) | copy-done | bytes 8388632
  37.3 6.3 %product.3.refs_9_ = f32[16,128,1024]{2,1,0:T(8,128)S(1)} custom-call(s32[8]{0:T(128)S(1)} %dynamic-slice_bitcast_fusion.refs_0_.cycle, s32[2,16]{1,0:T(2,128)S(1)} %bitcast.17, s32[2,16]{1,0:T(2,128)S(1)} %get-tuple-element.28.refs_2_, s32[2,16]{1,0:T(2,128)S(1)} %get-tuple-element.27.refs_3_, bf16[2064,128]{1,0:T(8,128)(2,1)S(1)} %get-tuple-element.26.refs_4_, ...), custom_call_target="tpu_custom_call" | custom-call | tf_op jit(solution)/shard_map/product/pallas_call | solution.py:148
  43.7 1.9 %collective-permute-start.8 = (bf16[2064,128]{1,0:T(8,128)(2,1)S(1)}, bf16[2064,128]{1,0:T(8,128)(2,1)S(1)}, u32[]{:S(2)}, u32[]{:S(2)}) collective-permute-start(bf16[2064,128]{1,0:T(8,128)(2,1)S(1)} %collective-permute-done.4.refs_3_), channel_id=1, source_target_pairs={{0,4},{4,8},{8,12},{12,14},{14,10},{10,6},{6,2},{2,0},{1,5},{5,9},... | collective-permute-start | bytes 1585160 | tf_op jit(solution)/shard_map/low_ahead/ppermute | solution.py:253
  45.8 7.0 %collective-permute-done.10.refs_4_ = bf16[2048,128]{1,0:T(8,128)(2,1)S(1)} collective-permute-done((bf16[2048,128]{1,0:T(8,128)(2,1)}, bf16[2048,128]{1,0:T(8,128)(2,1)S(1)}, u32[]{:S(2)}, u32[]{:S(2)}) %collective-permute-start.10) | collective-permute-done | bytes 524320 | tf_op jit(solution)/shard_map/high_ahead/ppermute | solution.py:253
  52.7 2.0 %collective-permute-start.15 = (bf16[2048,128]{1,0:T(8,128)(2,1)S(1)}, bf16[2048,128]{1,0:T(8,128)(2,1)S(1)}, u32[]{:S(2)}, u32[]{:S(2)}) collective-permute-start(bf16[2048,128]{1,0:T(8,128)(2,1)S(1)} %collective-permute-done.10.refs_4_), channel_id=1, source_target_pairs={{0,4},{4,8},{8,12},{12,14},{14,10},{10,6},{6,2},{2,0},{1,5},{5,9},... | collective-permute-start | bytes 1572872 | tf_op jit(solution)/shard_map/high_ahead/ppermute | solution.py:253
  55.0 4.0 %product.4.refs_9_ = f32[16,128,1024]{2,1,0:T(8,128)S(1)} custom-call(s32[8]{0:T(128)S(1)} %dynamic-slice_bitcast_fusion.refs_0_.cycle, s32[2,16]{1,0:T(2,128)S(1)} %slice_convert_fusion.4.refs_1_, s32[2,16]{1,0:T(2,128)S(1)} %slice_convert_fusion.3.refs_2_, bf16[2064,128]{1,0:T(8,128)(2,1)S(1)} %collective-permute-done.4.refs_3_, ...), custom_call_target="tpu_custom_call", output_to_operand_aliasing={{}: (9, {})} | custom-call | tf_op jit(solution)/shard_map/product/pallas_call | solution.py:148
  59.0 5.0 %collective-permute-done.8.refs_3_ = bf16[2064,128]{1,0:T(8,128)(2,1)S(1)} collective-permute-done((bf16[2064,128]{1,0:T(8,128)(2,1)S(1)}, bf16[2064,128]{1,0:T(8,128)(2,1)S(1)}, u32[]{:S(2)}, u32[]{:S(2)}) %collective-permute-start.8) | collective-permute-done | bytes 528416 | tf_op jit(solution)/shard_map/low_ahead/ppermute | solution.py:253
  64.0 2.3 %collective-permute-done.9.refs_6_ = bf16[2064,128]{1,0:T(8,128)(2,1)S(1)} collective-permute-done((bf16[2064,128]{1,0:T(8,128)(2,1)S(1)}, bf16[2064,128]{1,0:T(8,128)(2,1)S(1)}, u32[]{:S(2)}, u32[]{:S(2)}) %collective-permute-start.9) | collective-permute-done | bytes 528416 | tf_op jit(solution)/shard_map/high_back/ppermute | solution.py:253
  66.4 1.6 %collective-permute-start.12 = (bf16[1552,128]{1,0:T(8,128)(2,1)S(1)}, bf16[1552,128]{1,0:T(8,128)(2,1)S(1)}, u32[]{:S(2)}, u32[]{:S(2)}) collective-permute-start(bf16[1552,128]{1,0:T(8,128)(2,1)S(1)} %slice.69), channel_id=1, source_target_pairs={{0,4},{4,8},{8,12},{12,14},{14,10},{10,6},{6,2},{2,0},{1,5},{5,9},... | collective-permute-start | bytes 1191944 | tf_op jit(solution)/shard_map/far_low_ahead/ppermute | solution.py:253
  68.5 1.6 %collective-permute-start.13 = (bf16[512,128]{1,0:T(8,128)(2,1)S(1)}, bf16[512,128]{1,0:T(8,128)(2,1)S(1)}, u32[]{:S(2)}, u32[]{:S(2)}) collective-permute-start(bf16[512,128]{1,0:T(8,128)(2,1)S(1)} %slice.71), channel_id=1, source_target_pairs={{0,4},{4,8},{8,12},{12,14},{14,10},{10,6},{6,2},{2,0},{1,5},{5,9},... | collective-permute-start | bytes 393224 | tf_op jit(solution)/shard_map/last_low_ahead/ppermute | solution.py:253
  70.1 5.2 %collective-permute-done.15.refs_4_ = bf16[2048,128]{1,0:T(8,128)(2,1)S(1)} collective-permute-done((bf16[2048,128]{1,0:T(8,128)(2,1)S(1)}, bf16[2048,128]{1,0:T(8,128)(2,1)S(1)}, u32[]{:S(2)}, u32[]{:S(2)}) %collective-permute-start.15) | collective-permute-done | bytes 524320 | tf_op jit(solution)/shard_map/high_ahead/ppermute | solution.py:253
  75.3 1.9 %collective-permute-start.14 = (bf16[512,128]{1,0:T(8,128)(2,1)S(1)}, bf16[512,128]{1,0:T(8,128)(2,1)S(1)}, u32[]{:S(2)}, u32[]{:S(2)}) collective-permute-start(bf16[512,128]{1,0:T(8,128)(2,1)S(1)} %slice.72), channel_id=1, source_target_pairs={{4,0},{8,4},{12,8},{14,12},{10,14},{6,10},{2,6},{0,2},{5,1},{9,5},... | collective-permute-start | bytes 393224 | tf_op jit(solution)/shard_map/last_high_back/ppermute | solution.py:253
  77.5 4.1 %product.5.total = f32[16,128,1024]{2,1,0:T(8,128)S(1)} custom-call(s32[8]{0:T(128)S(1)} %dynamic-slice_bitcast_fusion.refs_0_.cycle, s32[2,16]{1,0:T(2,128)S(1)} %slice_convert_fusion.2.refs_1_, s32[2,16]{1,0:T(2,128)S(1)} %slice_convert_fusion.1.refs_2_, bf16[2064,128]{1,0:T(8,128)(2,1)S(1)} %collective-permute-done.8.refs_3_, ...), custom_call_target="tpu_custom_call", output_to_operand_aliasing={{}: (9, {})} | custom-call | tf_op jit(solution)/shard_map/product/pallas_call | solution.py:148
  81.6 2.2 %collective-permute-done.12.low = bf16[1552,128]{1,0:T(8,128)(2,1)S(1)} collective-permute-done((bf16[1552,128]{1,0:T(8,128)(2,1)S(1)}, bf16[1552,128]{1,0:T(8,128)(2,1)S(1)}, u32[]{:S(2)}, u32[]{:S(2)}) %collective-permute-start.12) | collective-permute-done | bytes 397344 | tf_op jit(solution)/shard_map/far_low_ahead/ppermute | solution.py:253
  83.8 2.2 %collective-permute-done.17.high = bf16[1552,128]{1,0:T(8,128)(2,1)S(1)} collective-permute-done((bf16[1552,128]{1,0:T(8,128)(2,1)S(1)}, bf16[1552,128]{1,0:T(8,128)(2,1)S(1)}, u32[]{:S(2)}, u32[]{:S(2)}) %collective-permute-start.17) | collective-permute-done | bytes 397344 | tf_op jit(solution)/shard_map/far_high_back/ppermute | solution.py:253
  86.0 2.6 %finish.2.refs_0_ = bf16[16,1,8,128,128]{4,3,2,1,0:T(8,128)(2,1)} custom-call(s32[8]{0:T(128)S(1)} %dynamic-slice_bitcast_fusion.refs_0_.cycle, s32[2,16]{1,0:T(2,128)S(1)} %slice_convert_fusion.index, bf16[1552,128]{1,0:T(8,128)(2,1)S(1)} %collective-permute-done.12.low, bf16[1552,128]{1,0:T(8,128)(2,1)S(1)} %collective-permute-done.17.high, ...), custom_call_target="tpu_custom_call" | custom-call | tf_op jit(solution)/shard_map/finish/pallas_call | solution.py:210
  88.7 1.8 %finish.3 = bf16[16,1,8,128,128]{4,3,2,1,0:T(8,128)(2,1)} custom-call(s32[8]{0:T(128)S(1)} %dynamic-slice_bitcast_fusion.refs_0_.cycle, s32[2,16]{1,0:T(2,128)S(1)} %slice_convert_fusion.index, bf16[512,128]{1,0:T(8,128)(2,1)S(1)} %collective-permute-done.13.low, bf16[512,128]{1,0:T(8,128)(2,1)S(1)} %collective-permute-done.14.high, ...), custom_call_target="tpu_custom_call", output_to_operand_aliasing={{}: (6, {})} | custom-call | tf_op jit(solution)/shard_map/finish/pallas_call | solution.py:210
  (46 shorter events, 9.3 us)
Async XLA Ops:
  0.0 9.4 %collective-permute-start.3 = (bf16[16,4,128,128]{3,2,1,0:T(8,128)(2,1)}, bf16[16,4,128,128]{3,2,1,0:T(8,128)(2,1)}, u32[]{:S(2)}, u32[]{:S(2)}) collective-permute-start(bf16[16,4,128,128]{3,2,1,0:T(8,128)(2,1)} %bitcast.15), channel_id=1, source_target_pairs={{0,1},{1,0},{2,3},{3,2},{4,5},{5,4},{6,7},{7,6},{8,9},{9,8},{10,11... | collective-permute-start | bytes 6291464 | tf_op jit(solution)/shard_map/ppermute | solution.py:268
  1.1 5.0 %copy-start.5 = (s32[16,1,4]{0,2,1:T(4,128)S(1)}, s32[16,1,4]{0,2,1:T(4,128)}, u32[]{:S(2)}) copy-start(s32[16,1,4]{0,2,1:T(4,128)} %param.8) | copy-start | bytes 772
  1.1 8.3 %copy-start.2 = (bf16[16,1,4,128,128]{4,3,2,1,0:T(8,128)(2,1)S(1)}, bf16[16,1,4,128,128]{4,3,2,1,0:T(8,128)(2,1)}, u32[]{:S(2)}) copy-start(bf16[16,1,4,128,128]{4,3,2,1,0:T(8,128)(2,1)} %param.7) | copy-start | bytes 6291460
  2.6 1.0 %copy-start.4 = (bf16[8,1,2,128,128]{4,3,2,1,0:T(8,128)(2,1)}, bf16[8,1,2,128,128]{4,3,2,1,0:T(8,128)(2,1)S(1)}, u32[]{:S(2)}) copy-start(bf16[8,1,2,128,128]{4,3,2,1,0:T(8,128)(2,1)S(1)} %get-tuple-element.24) | copy-start | bytes 1572868
  3.5 16.9 %collective-permute-start = (bf16[2064,128]{1,0:T(8,128)(2,1)S(1)}, bf16[2064,128]{1,0:T(8,128)(2,1)}, u32[]{:S(2)}, u32[]{:S(2)}) collective-permute-start(bf16[2064,128]{1,0:T(8,128)(2,1)S(1)} %get-tuple-element.26.refs_4_), channel_id=1, source_target_pairs={{0,4},{4,8},{8,12},{12,14},{14,10},{10,6},{6,2},{2,0},{1,5},{5,9},... | collective-permute-start | bytes 1585160 | tf_op jit(solution)/shard_map/low_ahead/ppermute | solution.py:253
  6.1 15.2 %collective-permute-start.1 = (bf16[2064,128]{1,0:T(8,128)(2,1)}, bf16[2064,128]{1,0:T(8,128)(2,1)}, u32[]{:S(2)}, u32[]{:S(2)}) collective-permute-start(bf16[2064,128]{1,0:T(8,128)(2,1)} %get-tuple-element.25), channel_id=1, source_target_pairs={{4,0},{8,4},{12,8},{14,12},{10,14},{6,10},{2,6},{0,2},{5,1},{9,5},... | collective-permute-start | bytes 1585160 | tf_op jit(solution)/shard_map/high_back/ppermute | solution.py:253
  6.3 2.2 %collective-permute-start.2 = (s32[64]{0:T(128)S(1)}, s32[64]{0:T(128)S(1)}, u32[]{:S(2)}, u32[]{:S(2)}) collective-permute-start(s32[64]{0:T(128)S(1)} %reshape.6.own_index), channel_id=1, source_target_pairs={{0,1},{1,0},{2,3},{3,2},{4,5},{5,4},{6,7},{7,6},{8,9},{9,8},{10,11... | collective-permute-start | bytes 776 | tf_op jit(solution)/shard_map/ppermute | solution.py:269
  6.6 23.7 %collective-permute-start.6 = (bf16[2048,128]{1,0:T(8,128)(2,1)S(1)}, bf16[2048,128]{1,0:T(8,128)(2,1)}, u32[]{:S(2)}, u32[]{:S(2)}) collective-permute-start(bf16[2048,128]{1,0:T(8,128)(2,1)S(1)} %bitcast.13), channel_id=1, source_target_pairs={{0,4},{4,8},{8,12},{12,14},{14,10},{10,6},{6,2},{2,0},{1,5},{5,9},... | collective-permute-start | bytes 1572872 | tf_op jit(solution)/shard_map/high_ahead/ppermute | solution.py:253
  8.4 24.1 %collective-permute-start.7 = (bf16[2048,128]{1,0:T(8,128)(2,1)}, bf16[2048,128]{1,0:T(8,128)(2,1)}, u32[]{:S(2)}, u32[]{:S(2)}) collective-permute-start(bf16[2048,128]{1,0:T(8,128)(2,1)} %bitcast.19), channel_id=1, source_target_pairs={{4,0},{8,4},{12,8},{14,12},{10,14},{6,10},{2,6},{0,2},{5,1},{9,5},... | collective-permute-start | bytes 1572872 | tf_op jit(solution)/shard_map/low_back/ppermute | solution.py:253
  9.5 24.4 %copy-start.3 = (s32[16,1,2]{0,2,1:T(2,128)S(1)}, s32[16,1,2]{0,2,1:T(2,128)}, u32[]{:S(2)}) copy-start(s32[16,1,2]{0,2,1:T(2,128)} %param.6) | copy-start | bytes 388
  17.2 3.3 %copy-start = (bf16[8,4,128,1024]{3,2,1,0:T(8,128)(2,1)}, bf16[8,4,128,1024]{3,2,1,0:T(8,128)(2,1)S(1)}, u32[]{:S(2)}) copy-start(bf16[8,4,128,1024]{3,2,1,0:T(8,128)(2,1)S(1)} %densify.1.refs_10_.refs_11_.refs_12_.refs_7_.refs_8_.right) | copy-start | bytes 25165828
  21.3 22.3 %collective-permute-start.4 = (bf16[2064,128]{1,0:T(8,128)(2,1)}, bf16[2064,128]{1,0:T(8,128)(2,1)S(1)}, u32[]{:S(2)}, u32[]{:S(2)}) collective-permute-start(bf16[2064,128]{1,0:T(8,128)(2,1)} %collective-permute-done.refs_6_), channel_id=1, source_target_pairs={{0,4},{4,8},{8,12},{12,14},{14,10},{10,6},{6,2},{2,0},{1,5},{5,9},... | collective-permute-start | bytes 1585160 | tf_op jit(solution)/shard_map/low_ahead/ppermute | solution.py:253
  22.9 20.9 %collective-permute-start.5 = (bf16[2064,128]{1,0:T(8,128)(2,1)}, bf16[2064,128]{1,0:T(8,128)(2,1)S(1)}, u32[]{:S(2)}, u32[]{:S(2)}) collective-permute-start(bf16[2064,128]{1,0:T(8,128)(2,1)} %collective-permute-done.1.refs_9_), channel_id=1, source_target_pairs={{4,0},{8,4},{12,8},{14,12},{10,14},{6,10},{2,6},{0,2},{5,1},{9,5},... | collective-permute-start | bytes 1585160 | tf_op jit(solution)/shard_map/high_back/ppermute | solution.py:253
  30.3 22.5 %collective-permute-start.10 = (bf16[2048,128]{1,0:T(8,128)(2,1)}, bf16[2048,128]{1,0:T(8,128)(2,1)S(1)}, u32[]{:S(2)}, u32[]{:S(2)}) collective-permute-start(bf16[2048,128]{1,0:T(8,128)(2,1)} %collective-permute-done.6.refs_7_), channel_id=1, source_target_pairs={{0,4},{4,8},{8,12},{12,14},{14,10},{10,6},{6,2},{2,0},{1,5},{5,9},... | collective-permute-start | bytes 1572872 | tf_op jit(solution)/shard_map/high_ahead/ppermute | solution.py:253
  32.5 22.5 %collective-permute-start.11 = (bf16[2048,128]{1,0:T(8,128)(2,1)}, bf16[2048,128]{1,0:T(8,128)(2,1)S(1)}, u32[]{:S(2)}, u32[]{:S(2)}) collective-permute-start(bf16[2048,128]{1,0:T(8,128)(2,1)} %collective-permute-done.7.refs_8_), channel_id=1, source_target_pairs={{4,0},{8,4},{12,8},{14,12},{10,14},{6,10},{2,6},{0,2},{5,1},{9,5},... | collective-permute-start | bytes 1572872 | tf_op jit(solution)/shard_map/low_back/ppermute | solution.py:253
  33.9 3.4 %copy-start.1 = (bf16[8,4,128,1024]{3,2,1,0:T(8,128)(2,1)S(1)}, bf16[8,4,128,1024]{3,2,1,0:T(8,128)(2,1)}, u32[]{:S(2)}) copy-start(bf16[8,4,128,1024]{3,2,1,0:T(8,128)(2,1)} %copy-done) | copy-start | bytes 25165828
  43.7 20.3 %collective-permute-start.8 = (bf16[2064,128]{1,0:T(8,128)(2,1)S(1)}, bf16[2064,128]{1,0:T(8,128)(2,1)S(1)}, u32[]{:S(2)}, u32[]{:S(2)}) collective-permute-start(bf16[2064,128]{1,0:T(8,128)(2,1)S(1)} %collective-permute-done.4.refs_3_), channel_id=1, source_target_pairs={{0,4},{4,8},{8,12},{12,14},{14,10},{10,6},{6,2},{2,0},{1,5},{5,9},... | collective-permute-start | bytes 1585160 | tf_op jit(solution)/shard_map/low_ahead/ppermute | solution.py:253
  45.6 20.6 %collective-permute-start.9 = (bf16[2064,128]{1,0:T(8,128)(2,1)S(1)}, bf16[2064,128]{1,0:T(8,128)(2,1)S(1)}, u32[]{:S(2)}, u32[]{:S(2)}) collective-permute-start(bf16[2064,128]{1,0:T(8,128)(2,1)S(1)} %collective-permute-done.5.refs_6_), channel_id=1, source_target_pairs={{4,0},{8,4},{12,8},{14,12},{10,14},{6,10},{2,6},{0,2},{5,1},{9,5},... | collective-permute-start | bytes 1585160 | tf_op jit(solution)/shard_map/high_back/ppermute | solution.py:253
  52.7 22.6 %collective-permute-start.15 = (bf16[2048,128]{1,0:T(8,128)(2,1)S(1)}, bf16[2048,128]{1,0:T(8,128)(2,1)S(1)}, u32[]{:S(2)}, u32[]{:S(2)}) collective-permute-start(bf16[2048,128]{1,0:T(8,128)(2,1)S(1)} %collective-permute-done.10.refs_4_), channel_id=1, source_target_pairs={{0,4},{4,8},{8,12},{12,14},{14,10},{10,6},{6,2},{2,0},{1,5},{5,9},... | collective-permute-start | bytes 1572872 | tf_op jit(solution)/shard_map/high_ahead/ppermute | solution.py:253
  55.0 22.6 %collective-permute-start.16 = (bf16[2048,128]{1,0:T(8,128)(2,1)S(1)}, bf16[2048,128]{1,0:T(8,128)(2,1)S(1)}, u32[]{:S(2)}, u32[]{:S(2)}) collective-permute-start(bf16[2048,128]{1,0:T(8,128)(2,1)S(1)} %collective-permute-done.11.refs_5_), channel_id=1, source_target_pairs={{4,0},{8,4},{12,8},{14,12},{10,14},{6,10},{2,6},{0,2},{5,1},{9,5},... | collective-permute-start | bytes 1572872 | tf_op jit(solution)/shard_map/low_back/ppermute | solution.py:253
  66.4 17.4 %collective-permute-start.12 = (bf16[1552,128]{1,0:T(8,128)(2,1)S(1)}, bf16[1552,128]{1,0:T(8,128)(2,1)S(1)}, u32[]{:S(2)}, u32[]{:S(2)}) collective-permute-start(bf16[1552,128]{1,0:T(8,128)(2,1)S(1)} %slice.69), channel_id=1, source_target_pairs={{0,4},{4,8},{8,12},{12,14},{14,10},{10,6},{6,2},{2,0},{1,5},{5,9},... | collective-permute-start | bytes 1191944 | tf_op jit(solution)/shard_map/far_low_ahead/ppermute | solution.py:253
  68.0 18.0 %collective-permute-start.17 = (bf16[1552,128]{1,0:T(8,128)(2,1)S(1)}, bf16[1552,128]{1,0:T(8,128)(2,1)S(1)}, u32[]{:S(2)}, u32[]{:S(2)}) collective-permute-start(bf16[1552,128]{1,0:T(8,128)(2,1)S(1)} %slice.75), channel_id=1, source_target_pairs={{4,0},{8,4},{12,8},{14,12},{10,14},{6,10},{2,6},{0,2},{5,1},{9,5},... | collective-permute-start | bytes 1191944 | tf_op jit(solution)/shard_map/far_high_back/ppermute | solution.py:253
  68.5 20.2 %collective-permute-start.13 = (bf16[512,128]{1,0:T(8,128)(2,1)S(1)}, bf16[512,128]{1,0:T(8,128)(2,1)S(1)}, u32[]{:S(2)}, u32[]{:S(2)}) collective-permute-start(bf16[512,128]{1,0:T(8,128)(2,1)S(1)} %slice.71), channel_id=1, source_target_pairs={{0,4},{4,8},{8,12},{12,14},{14,10},{10,6},{6,2},{2,0},{1,5},{5,9},... | collective-permute-start | bytes 393224 | tf_op jit(solution)/shard_map/last_low_ahead/ppermute | solution.py:253
  75.3 13.4 %collective-permute-start.14 = (bf16[512,128]{1,0:T(8,128)(2,1)S(1)}, bf16[512,128]{1,0:T(8,128)(2,1)S(1)}, u32[]{:S(2)}, u32[]{:S(2)}) collective-permute-start(bf16[512,128]{1,0:T(8,128)(2,1)S(1)} %slice.72), channel_id=1, source_target_pairs={{4,0},{8,4},{12,8},{14,12},{10,14},{6,10},{2,6},{0,2},{5,1},{9,5},... | collective-permute-start | bytes 393224 | tf_op jit(solution)/shard_map/last_high_back/ppermute | solution.py:253

commit v3 on v2

--- a/solution.py
+++ b/solution.py
@@ -227,6 +227,47 @@
     )(*operands)
 
 
+def pack_kernel(flat_ref, index_hbm, low_ref, high_ref, index_ref, wide_ref, sems):
+    cut = flat_ref.shape[0] // 2
+    index_copy = pltpu.make_async_copy(index_hbm, index_ref, sems.at[2])
+    index_copy.start()
+    copies = [
+        pltpu.make_async_copy(
+            flat_ref.at[pl.ds(h * cut, cut)], half_ref.at[pl.ds(0, cut)], sems.at[h]
+        )
+        for h, half_ref in enumerate((low_ref, high_ref))
+    ]
+    for copy in copies:
+        copy.start()
+    index_copy.wait()
+    wide_ref[...] = jnp.zeros(wide_ref.shape, jnp.float32)
+    wide_ref[: index_ref.shape[0], : index_ref.shape[1]] = index_ref[...].astype(jnp.float32)
+    note = wide_ref[...].astype(jnp.bfloat16)
+    for half_ref in (low_ref, high_ref):
+        half_ref[cut:] = note
+    for copy in copies:
+        copy.wait()
+
+
+def pack(flat, index):
+    size, blk = flat.shape
+    half = jax.ShapeDtypeStruct((size // 2 + NOTE_ROWS, blk), jnp.bfloat16)
+    return pl.pallas_call(
+        pack_kernel,
+        out_shape=(half, half),
+        in_specs=[pl.BlockSpec(memory_space=pl.ANY)] * 2,
+        out_specs=[pl.BlockSpec(memory_space=pltpu.VMEM)] * 2,
+        scratch_shapes=[
+            pltpu.VMEM(index.shape, jnp.int32),
+            pltpu.VMEM((NOTE_ROWS, blk), jnp.float32),
+            pltpu.SemaphoreType.DMA((3,)),
+        ],
+        compiler_params=pltpu.CompilerParams(vmem_limit_bytes=VMEM_LIMIT),
+        name="pack",
+        cost_estimate=pl.CostEstimate(flops=0, bytes_accessed=0, transcendentals=0),
+    )(*(pltpu.with_memory_space_constraint(x, pltpu.HBM) for x in (flat, index)))
+
+
 def body(a_values, a_index, b_values, b_index):
     n = lax.axis_size("row")
     order = ring_order(n)
@@ -240,10 +281,8 @@
     flat = a_values.reshape(rows * slots * blk, blk)
     cut = half * slots * blk
     own_index = a_index[:, 0].T
-    note = own_index.astype(jnp.bfloat16)
-    note = jnp.pad(note, ((0, NOTE_ROWS - slots), (0, blk - rows)))
-    low_first, high_second = jnp.concatenate([flat[:cut], note]), flat[cut:]
-    high_first, low_second = jnp.concatenate([flat[cut:], note]), flat[:cut]
+    low_first, high_first = pack(flat, own_index)
+    low_second, high_second = flat[:cut], flat[cut:]
 
     def read_note(message):
         return message[-NOTE_ROWS:][:slots, :rows].astype(jnp.int32)
@@ -264,8 +303,9 @@
 
     advance()
     col = lax.axis_index("col")
-    stored, stored_index = b_values[:, 0], b_index.reshape(-1)
-    other = lax.ppermute(stored, "col", swap)
+    stored = b_values[:, 0]
+    other, stored_index = lax.optimization_barrier((lax.ppermute(stored, "col", swap), b_index))
+    stored_index = stored_index.reshape(-1)
     other_index = lax.ppermute(stored_index, "col", swap)
     inner_width = 2 * stored.shape[0] // n
     right = densify(col[None], stored_index, other_index, stored, other, n // 2, inner_width)
@@ -282,7 +322,6 @@
         return done
 
 
-    right = after(right)
     total = None
     for k in range(1, whole_steps + 1):
         offsets, items = (n - k, k), [behind[k], beyond[k]]

time: 90.8 us -> 89.9 us (0.990)
  local copies, waits for them, and re-layouts: 9.04 us -> 5.29 us
  waiting for transfers between devices: 32.6 us -> 35.1 us
  Pallas kernels: 26.5 us -> 28.1 us
  starting transfers between devices: 19.8 us -> 18.8 us
    unnamed x13 -> x8, local copies, waits for them, and re-layouts: 6.76 us -> 1.6 us
    pallas_call x0 -> x1, Pallas kernels: none -> 2.03 us  [pack(): pl.pallas_call(pack_kernel, out_shape=(half, half), in_specs=[pl.BlockSpe...]
    ppermute x16, waiting for transfers between devices: 32.6 us -> 34.7 us  [move(): return lax.ppermute(array, 'row', way)]
    pallas_call x1, Pallas kernels: 7.71 us -> 5.9 us  [densify(): pl.pallas_call(densify_kernel, out_shape=jax.ShapeDtypeStruct((2 * pieces...]
    pallas_call x3, Pallas kernels: 14.4 us -> 15.8 us  [product(): pl.pallas_call(functools.partial(product_kernel, offsets, sides, starts,...]
    convert_element_type x6, other arithmetic: 0.71 us -> 2.05 us  [read_note(): return message[-NOTE_ROWS:][:slots, :rows].astype(jnp.int32)]
    concatenate x1 -> x0, other arithmetic: 0.95 us -> none  [body(): high_first, low_second = (jnp.concatenate([flat[cut:], note]), flat[:cut])]
  transfers between devices with their start and end apart: 18 -> 18, of which waited for: 12 -> 12; matrix products, arithmetic and copies ran while one was open for 5% -> 6% of each run, Pallas kernels for 27% -> 29%
where the time goes in v3:
time: 89.9 us; the launch traced here: 89.5 us
  waiting for transfers between devices  35.1 us (39%)
  Pallas kernels  28.1 us (31%)
  starting transfers between devices  18.8 us (21%)
  local copies, waits for them, and re-layouts  5.29 us (6%)
  other arithmetic  2.05 us (2%)
    ppermute x16, waiting for transfers between devices, move(): return lax.ppermute(array, 'row', way)  34.7 us
    ppermute x16, starting transfers between devices, move(): return lax.ppermute(array, 'row', way)  18.3 us
    pallas_call x3, Pallas kernels, product(): pl.pallas_call(functools.partial(product_kernel, offsets, sides, starts,...  15.8 us
    pallas_call x1, Pallas kernels, densify(): pl.pallas_call(densify_kernel, out_shape=jax.ShapeDtypeStruct((2 * pieces...  5.9 us
    pallas_call x2, Pallas kernels, finish(): pl.pallas_call(functools.partial(finish_kernel, offset, starts, size), ou...  4.36 us
    slice x1, local copies, waits for them, and re-layouts, body(): low_second, high_second = (flat[:cut], flat[cut:])  2.08 us
    convert_element_type x6, other arithmetic, read_note(): return message[-NOTE_ROWS:][:slots, :rows].astype(jnp.int32)  2.05 us
    pallas_call x1, Pallas kernels, pack(): pl.pallas_call(pack_kernel, out_shape=(half, half), in_specs=[pl.BlockSpe...  2.03 us
  transfers between devices with their start and end apart: 18, of which 12 were waited for; matrix products, arithmetic and copies ran while one was open for 6% of the time, Pallas kernels for 29%

profile of v3, /device:TPU:0, one launch (start us, length us, event | category | flops | bytes accessed | tf_op | source)
XLA Modules:
  0.0 89.5 jit_solution(15012134295548320335)
XLA Ops:
  0.5 2.0 %pack.1 = (bf16[2064,128]{1,0:T(8,128)(2,1)S(1)}, bf16[2064,128]{1,0:T(8,128)(2,1)}) custom-call(bf16[4096,128]{1,0:T(8,128)(2,1)} %bitcast.18, s32[2,16]{1,0:T(2,128)} %bitcast.16), custom_call_target="tpu_custom_call" | custom-call | tf_op jit(solution)/shard_map/pack/pallas_call | solution.py:255
  2.5 2.6 %collective-permute-start = (bf16[2064,128]{1,0:T(8,128)(2,1)S(1)}, bf16[2064,128]{1,0:T(8,128)(2,1)}, u32[]{:S(2)}, u32[]{:S(2)}) collective-permute-start(bf16[2064,128]{1,0:T(8,128)(2,1)S(1)} %get-tuple-element.15.refs_4_), channel_id=1, source_target_pairs={{0,4},{4,8},{8,12},{12,14},{14,10},{10,6},{6,2},{2,0},{1,5},{5,9},... | collective-permute-start | bytes 1585160 | tf_op jit(solution)/shard_map/low_ahead/ppermute | solution.py:292
  5.2 2.1 %fusion = (bf16[8,1,2,128,128]{4,3,2,1,0:T(8,128)(2,1)}, bf16[8,1,2,128,128]{4,3,2,1,0:T(8,128)(2,1)S(1)}) fusion(bf16[16,1,2,128,128]{4,3,2,1,0:T(8,128)(2,1)} %param.5), kind=kLoop, calls=%fused_computation.8 | loop fusion | bytes 2097152 | tf_op jit(solution)/shard_map/slice | solution.py:285
  7.2 2.0 %collective-permute-start.4 = (bf16[2048,128]{1,0:T(8,128)(2,1)S(1)}, bf16[2048,128]{1,0:T(8,128)(2,1)}, u32[]{:S(2)}, u32[]{:S(2)}) collective-permute-start(bf16[2048,128]{1,0:T(8,128)(2,1)S(1)} %bitcast.14), channel_id=1, source_target_pairs={{0,4},{4,8},{8,12},{12,14},{14,10},{10,6},{6,2},{2,0},{1,5},{5,9},... | collective-permute-start | bytes 1572872 | tf_op jit(solution)/shard_map/high_ahead/ppermute | solution.py:292
  9.3 8.8 %collective-permute-done.refs_6_ = bf16[2064,128]{1,0:T(8,128)(2,1)} collective-permute-done((bf16[2064,128]{1,0:T(8,128)(2,1)S(1)}, bf16[2064,128]{1,0:T(8,128)(2,1)}, u32[]{:S(2)}, u32[]{:S(2)}) %collective-permute-start) | collective-permute-done | bytes 528416 | tf_op jit(solution)/shard_map/low_ahead/ppermute | solution.py:292
  18.1 2.0 %collective-permute-start.1 = (bf16[2064,128]{1,0:T(8,128)(2,1)}, bf16[2064,128]{1,0:T(8,128)(2,1)S(1)}, u32[]{:S(2)}, u32[]{:S(2)}) collective-permute-start(bf16[2064,128]{1,0:T(8,128)(2,1)} %collective-permute-done.refs_6_), channel_id=1, source_target_pairs={{0,4},{4,8},{8,12},{12,14},{14,10},{10,6},{6,2},{2,0},{1,5},{5,9},... | collective-permute-start | bytes 1585160 | tf_op jit(solution)/shard_map/low_ahead/ppermute | solution.py:292
  21.0 8.3 %collective-permute-done.4.refs_7_ = bf16[2048,128]{1,0:T(8,128)(2,1)} collective-permute-done((bf16[2048,128]{1,0:T(8,128)(2,1)S(1)}, bf16[2048,128]{1,0:T(8,128)(2,1)}, u32[]{:S(2)}, u32[]{:S(2)}) %collective-permute-start.4) | collective-permute-done | bytes 524320 | tf_op jit(solution)/shard_map/high_ahead/ppermute | solution.py:292
  29.3 2.0 %collective-permute-start.10 = (bf16[2048,128]{1,0:T(8,128)(2,1)}, bf16[2048,128]{1,0:T(8,128)(2,1)}, u32[]{:S(2)}, u32[]{:S(2)}) collective-permute-start(bf16[2048,128]{1,0:T(8,128)(2,1)} %collective-permute-done.4.refs_7_), channel_id=1, source_target_pairs={{0,4},{4,8},{8,12},{12,14},{14,10},{10,6},{6,2},{2,0},{1,5},{5,9},... | collective-permute-start | bytes 1572872 | tf_op jit(solution)/shard_map/high_ahead/ppermute | solution.py:292
  34.3 1.6 %copy-done = bf16[16,1,4,128,128]{4,3,2,1,0:T(8,128)(2,1)S(1)} copy-done((bf16[16,1,4,128,128]{4,3,2,1,0:T(8,128)(2,1)S(1)}, bf16[16,1,4,128,128]{4,3,2,1,0:T(8,128)(2,1)}, u32[]{:S(2)}) %copy-start) | copy-done | bytes 2097176
  35.9 5.9 %densify.1.refs_10_.refs_11_.refs_12_.refs_7_.refs_8_.right = bf16[8,4,128,1024]{3,2,1,0:T(8,128)(2,1)S(1)} custom-call(s32[1]{0:T(128)} %bitcast.7.col_ref, s32[64]{0:T(128)S(1)} %reshape.9.own_index, s32[64]{0:T(128)S(1)} %collective-permute-done.7.other_index, bf16[16,4,128,128]{3,2,1,0:T(8,128)(2,1)S(1)} %bitcast.13, ...), custom_call_target="tpu_custom_call" | custom-call | tf_op jit(solution)/shard_map/densify/pallas_call | solution.py:44
  41.8 6.4 %product.3.refs_9_ = f32[16,128,1024]{2,1,0:T(8,128)S(1)} custom-call(s32[8]{0:T(128)S(1)} %dynamic-slice_bitcast_fusion.refs_0_.cycle, s32[2,16]{1,0:T(2,128)S(1)} %bitcast.17, s32[2,16]{1,0:T(2,128)S(1)} %slice_convert_fusion.2.refs_2_, s32[2,16]{1,0:T(2,128)S(1)} %slice_convert_fusion.1.refs_3_, bf16[2064,128]{1,0:T(8,128)(2,1)S(1)} %copy-done.2, ...), custom_call_target="tpu_custom_call" | custom-call | tf_op jit(solution)/shard_map/product/pallas_call | solution.py:148
  48.2 2.1 %collective-permute-start.8 = (bf16[2064,128]{1,0:T(8,128)(2,1)S(1)}, bf16[2064,128]{1,0:T(8,128)(2,1)S(1)}, u32[]{:S(2)}, u32[]{:S(2)}) collective-permute-start(bf16[2064,128]{1,0:T(8,128)(2,1)S(1)} %collective-permute-done.1.refs_3_), channel_id=1, source_target_pairs={{0,4},{4,8},{8,12},{12,14},{14,10},{10,6},{6,2},{2,0},{1,5},{5,9},... | collective-permute-start | bytes 1585160 | tf_op jit(solution)/shard_map/low_ahead/ppermute | solution.py:292
  51.9 1.8 %collective-permute-start.15 = (bf16[2048,128]{1,0:T(8,128)(2,1)}, bf16[2048,128]{1,0:T(8,128)(2,1)S(1)}, u32[]{:S(2)}, u32[]{:S(2)}) collective-permute-start(bf16[2048,128]{1,0:T(8,128)(2,1)} %collective-permute-done.10.refs_4_), channel_id=1, source_target_pairs={{0,4},{4,8},{8,12},{12,14},{14,10},{10,6},{6,2},{2,0},{1,5},{5,9},... | collective-permute-start | bytes 1572872 | tf_op jit(solution)/shard_map/high_ahead/ppermute | solution.py:292
  54.6 5.4 %product.4.refs_9_ = f32[16,128,1024]{2,1,0:T(8,128)S(1)} custom-call(s32[8]{0:T(128)S(1)} %dynamic-slice_bitcast_fusion.refs_0_.cycle, s32[2,16]{1,0:T(2,128)S(1)} %get-tuple-element.28.refs_1_, s32[2,16]{1,0:T(2,128)S(1)} %get-tuple-element.27.refs_2_, bf16[2064,128]{1,0:T(8,128)(2,1)S(1)} %collective-permute-done.1.refs_3_, ...), custom_call_target="tpu_custom_call", output_to_operand_aliasing={{}: (9, {})} | custom-call | tf_op jit(solution)/shard_map/product/pallas_call | solution.py:148
  59.9 3.3 %collective-permute-done.8.refs_3_ = bf16[2064,128]{1,0:T(8,128)(2,1)S(1)} collective-permute-done((bf16[2064,128]{1,0:T(8,128)(2,1)S(1)}, bf16[2064,128]{1,0:T(8,128)(2,1)S(1)}, u32[]{:S(2)}, u32[]{:S(2)}) %collective-permute-start.8) | collective-permute-done | bytes 528416 | tf_op jit(solution)/shard_map/low_ahead/ppermute | solution.py:292
  63.2 2.2 %collective-permute-done.9.refs_6_ = bf16[2064,128]{1,0:T(8,128)(2,1)S(1)} collective-permute-done((bf16[2064,128]{1,0:T(8,128)(2,1)}, bf16[2064,128]{1,0:T(8,128)(2,1)S(1)}, u32[]{:S(2)}, u32[]{:S(2)}) %collective-permute-start.9) | collective-permute-done | bytes 528416 | tf_op jit(solution)/shard_map/high_back/ppermute | solution.py:292
  65.5 1.6 %collective-permute-start.12 = (bf16[1552,128]{1,0:T(8,128)(2,1)S(1)}, bf16[1552,128]{1,0:T(8,128)(2,1)S(1)}, u32[]{:S(2)}, u32[]{:S(2)}) collective-permute-start(bf16[1552,128]{1,0:T(8,128)(2,1)S(1)} %slice.67), channel_id=1, source_target_pairs={{0,4},{4,8},{8,12},{12,14},{14,10},{10,6},{6,2},{2,0},{1,5},{5,9},... | collective-permute-start | bytes 1191944 | tf_op jit(solution)/shard_map/far_low_ahead/ppermute | solution.py:292
  69.2 5.3 %collective-permute-done.15.refs_4_ = bf16[2048,128]{1,0:T(8,128)(2,1)S(1)} collective-permute-done((bf16[2048,128]{1,0:T(8,128)(2,1)}, bf16[2048,128]{1,0:T(8,128)(2,1)S(1)}, u32[]{:S(2)}, u32[]{:S(2)}) %collective-permute-start.15) | collective-permute-done | bytes 524320 | tf_op jit(solution)/shard_map/high_ahead/ppermute | solution.py:292
  74.5 1.9 %collective-permute-start.14 = (bf16[512,128]{1,0:T(8,128)(2,1)S(1)}, bf16[512,128]{1,0:T(8,128)(2,1)S(1)}, u32[]{:S(2)}, u32[]{:S(2)}) collective-permute-start(bf16[512,128]{1,0:T(8,128)(2,1)S(1)} %slice.70), channel_id=1, source_target_pairs={{4,0},{8,4},{12,8},{14,12},{10,14},{6,10},{2,6},{0,2},{5,1},{9,5},... | collective-permute-start | bytes 393224 | tf_op jit(solution)/shard_map/last_high_back/ppermute | solution.py:292
  76.6 4.1 %product.5.total = f32[16,128,1024]{2,1,0:T(8,128)S(1)} custom-call(s32[8]{0:T(128)S(1)} %dynamic-slice_bitcast_fusion.refs_0_.cycle, s32[2,16]{1,0:T(2,128)S(1)} %slice_convert_fusion.4.refs_1_, s32[2,16]{1,0:T(2,128)S(1)} %slice_convert_fusion.3.refs_2_, bf16[2064,128]{1,0:T(8,128)(2,1)S(1)} %collective-permute-done.8.refs_3_, ...), custom_call_target="tpu_custom_call", output_to_operand_aliasing={{}: (9, {})} | custom-call | tf_op jit(solution)/shard_map/product/pallas_call | solution.py:148
  80.7 2.3 %collective-permute-done.12.low = bf16[1552,128]{1,0:T(8,128)(2,1)S(1)} collective-permute-done((bf16[1552,128]{1,0:T(8,128)(2,1)S(1)}, bf16[1552,128]{1,0:T(8,128)(2,1)S(1)}, u32[]{:S(2)}, u32[]{:S(2)}) %collective-permute-start.12) | collective-permute-done | bytes 397344 | tf_op jit(solution)/shard_map/far_low_ahead/ppermute | solution.py:292
  83.0 2.2 %collective-permute-done.17.high = bf16[1552,128]{1,0:T(8,128)(2,1)S(1)} collective-permute-done((bf16[1552,128]{1,0:T(8,128)(2,1)S(1)}, bf16[1552,128]{1,0:T(8,128)(2,1)S(1)}, u32[]{:S(2)}, u32[]{:S(2)}) %collective-permute-start.17) | collective-permute-done | bytes 397344 | tf_op jit(solution)/shard_map/far_high_back/ppermute | solution.py:292
  85.1 2.6 %finish.2.refs_0_ = bf16[16,1,8,128,128]{4,3,2,1,0:T(8,128)(2,1)} custom-call(s32[8]{0:T(128)S(1)} %dynamic-slice_bitcast_fusion.refs_0_.cycle, s32[2,16]{1,0:T(2,128)S(1)} %slice_convert_fusion.index, bf16[1552,128]{1,0:T(8,128)(2,1)S(1)} %collective-permute-done.12.low, bf16[1552,128]{1,0:T(8,128)(2,1)S(1)} %collective-permute-done.17.high, ...), custom_call_target="tpu_custom_call" | custom-call | tf_op jit(solution)/shard_map/finish/pallas_call | solution.py:210
  87.7 1.8 %finish.3 = bf16[16,1,8,128,128]{4,3,2,1,0:T(8,128)(2,1)} custom-call(s32[8]{0:T(128)S(1)} %dynamic-slice_bitcast_fusion.refs_0_.cycle, s32[2,16]{1,0:T(2,128)S(1)} %slice_convert_fusion.index, bf16[512,128]{1,0:T(8,128)(2,1)S(1)} %collective-permute-done.13.low, bf16[512,128]{1,0:T(8,128)(2,1)S(1)} %collective-permute-done.14.high, ...), custom_call_target="tpu_custom_call", output_to_operand_aliasing={{}: (6, {})} | custom-call | tf_op jit(solution)/shard_map/finish/pallas_call | solution.py:210
  (41 shorter events, 9.3 us)
Async XLA Ops:
  0.0 41.8 %copy-start.3 = (s32[16,1,2]{0,2,1:T(2,128)S(1)}, s32[16,1,2]{0,2,1:T(2,128)}, u32[]{:S(2)}) copy-start(s32[16,1,2]{0,2,1:T(2,128)} %param.6) | copy-start | bytes 388
  0.0 32.2 %collective-permute-start.6 = (bf16[16,4,128,128]{3,2,1,0:T(8,128)(2,1)}, bf16[16,4,128,128]{3,2,1,0:T(8,128)(2,1)S(1)}, u32[]{:S(2)}, u32[]{:S(2)}) collective-permute-start(bf16[16,4,128,128]{3,2,1,0:T(8,128)(2,1)} %bitcast.12), channel_id=1, source_target_pairs={{0,1},{1,0},{2,3},{3,2},{4,5},{5,4},{6,7},{7,6},{8,9},{9,8},{10,11... | collective-permute-start | bytes 6291464 | tf_op jit(solution)/shard_map/ppermute | solution.py:307
  2.5 6.8 %copy-start.1 = (bf16[2064,128]{1,0:T(8,128)(2,1)}, bf16[2064,128]{1,0:T(8,128)(2,1)S(1)}, u32[]{:S(2)}) copy-start(bf16[2064,128]{1,0:T(8,128)(2,1)S(1)} %get-tuple-element.15.refs_4_) | copy-start | bytes 1585156
  2.5 15.6 %collective-permute-start = (bf16[2064,128]{1,0:T(8,128)(2,1)S(1)}, bf16[2064,128]{1,0:T(8,128)(2,1)}, u32[]{:S(2)}, u32[]{:S(2)}) collective-permute-start(bf16[2064,128]{1,0:T(8,128)(2,1)S(1)} %get-tuple-element.15.refs_4_), channel_id=1, source_target_pairs={{0,4},{4,8},{8,12},{12,14},{14,10},{10,6},{6,2},{2,0},{1,5},{5,9},... | collective-permute-start | bytes 1585160 | tf_op jit(solution)/shard_map/low_ahead/ppermute | solution.py:292
  5.1 15.2 %collective-permute-start.2 = (bf16[2064,128]{1,0:T(8,128)(2,1)}, bf16[2064,128]{1,0:T(8,128)(2,1)}, u32[]{:S(2)}, u32[]{:S(2)}) collective-permute-start(bf16[2064,128]{1,0:T(8,128)(2,1)} %get-tuple-element.16), channel_id=1, source_target_pairs={{4,0},{8,4},{12,8},{14,12},{10,14},{6,10},{2,6},{0,2},{5,1},{9,5},... | collective-permute-start | bytes 1585160 | tf_op jit(solution)/shard_map/high_back/ppermute | solution.py:292
  7.2 22.1 %collective-permute-start.4 = (bf16[2048,128]{1,0:T(8,128)(2,1)S(1)}, bf16[2048,128]{1,0:T(8,128)(2,1)}, u32[]{:S(2)}, u32[]{:S(2)}) collective-permute-start(bf16[2048,128]{1,0:T(8,128)(2,1)S(1)} %bitcast.14), channel_id=1, source_target_pairs={{0,4},{4,8},{8,12},{12,14},{14,10},{10,6},{6,2},{2,0},{1,5},{5,9},... | collective-permute-start | bytes 1572872 | tf_op jit(solution)/shard_map/high_ahead/ppermute | solution.py:292
  9.2 22.3 %collective-permute-start.5 = (bf16[2048,128]{1,0:T(8,128)(2,1)}, bf16[2048,128]{1,0:T(8,128)(2,1)}, u32[]{:S(2)}, u32[]{:S(2)}) collective-permute-start(bf16[2048,128]{1,0:T(8,128)(2,1)} %bitcast.6), channel_id=1, source_target_pairs={{4,0},{8,4},{12,8},{14,12},{10,14},{6,10},{2,6},{0,2},{5,1},{9,5},... | collective-permute-start | bytes 1572872 | tf_op jit(solution)/shard_map/low_back/ppermute | solution.py:292
  18.1 30.1 %collective-permute-start.1 = (bf16[2064,128]{1,0:T(8,128)(2,1)}, bf16[2064,128]{1,0:T(8,128)(2,1)S(1)}, u32[]{:S(2)}, u32[]{:S(2)}) collective-permute-start(bf16[2064,128]{1,0:T(8,128)(2,1)} %collective-permute-done.refs_6_), channel_id=1, source_target_pairs={{0,4},{4,8},{8,12},{12,14},{14,10},{10,6},{6,2},{2,0},{1,5},{5,9},... | collective-permute-start | bytes 1585160 | tf_op jit(solution)/shard_map/low_ahead/ppermute | solution.py:292
  20.3 27.9 %collective-permute-start.3 = (bf16[2064,128]{1,0:T(8,128)(2,1)}, bf16[2064,128]{1,0:T(8,128)(2,1)}, u32[]{:S(2)}, u32[]{:S(2)}) collective-permute-start(bf16[2064,128]{1,0:T(8,128)(2,1)} %collective-permute-done.2.refs_9_), channel_id=1, source_target_pairs={{4,0},{8,4},{12,8},{14,12},{10,14},{6,10},{2,6},{0,2},{5,1},{9,5},... | collective-permute-start | bytes 1585160 | tf_op jit(solution)/shard_map/high_back/ppermute | solution.py:292
  29.3 22.6 %collective-permute-start.10 = (bf16[2048,128]{1,0:T(8,128)(2,1)}, bf16[2048,128]{1,0:T(8,128)(2,1)}, u32[]{:S(2)}, u32[]{:S(2)}) collective-permute-start(bf16[2048,128]{1,0:T(8,128)(2,1)} %collective-permute-done.4.refs_7_), channel_id=1, source_target_pairs={{0,4},{4,8},{8,12},{12,14},{14,10},{10,6},{6,2},{2,0},{1,5},{5,9},... | collective-permute-start | bytes 1572872 | tf_op jit(solution)/shard_map/high_ahead/ppermute | solution.py:292
  31.5 22.1 %collective-permute-start.11 = (bf16[2048,128]{1,0:T(8,128)(2,1)}, bf16[2048,128]{1,0:T(8,128)(2,1)}, u32[]{:S(2)}, u32[]{:S(2)}) collective-permute-start(bf16[2048,128]{1,0:T(8,128)(2,1)} %collective-permute-done.5.refs_8_), channel_id=1, source_target_pairs={{4,0},{8,4},{12,8},{14,12},{10,14},{6,10},{2,6},{0,2},{5,1},{9,5},... | collective-permute-start | bytes 1572872 | tf_op jit(solution)/shard_map/low_back/ppermute | solution.py:292
  33.1 1.2 %collective-permute-start.7 = (s32[64]{0:T(128)S(1)}, s32[64]{0:T(128)S(1)}, u32[]{:S(2)}, u32[]{:S(2)}) collective-permute-start(s32[64]{0:T(128)S(1)} %reshape.9.own_index), channel_id=1, source_target_pairs={{0,1},{1,0},{2,3},{3,2},{4,5},{5,4},{6,7},{7,6},{8,9},{9,8},{10,11... | collective-permute-start | bytes 776 | tf_op jit(solution)/shard_map/ppermute | solution.py:309
  34.3 1.6 %copy-start = (bf16[16,1,4,128,128]{4,3,2,1,0:T(8,128)(2,1)S(1)}, bf16[16,1,4,128,128]{4,3,2,1,0:T(8,128)(2,1)}, u32[]{:S(2)}) copy-start(bf16[16,1,4,128,128]{4,3,2,1,0:T(8,128)(2,1)} %param.7) | copy-start | bytes 6291460
  35.9 5.9 %copy-start.2 = (bf16[2064,128]{1,0:T(8,128)(2,1)S(1)}, bf16[2064,128]{1,0:T(8,128)(2,1)}, u32[]{:S(2)}) copy-start(bf16[2064,128]{1,0:T(8,128)(2,1)} %copy-done.1) | copy-start | bytes 1585156
  48.2 15.0 %collective-permute-start.8 = (bf16[2064,128]{1,0:T(8,128)(2,1)S(1)}, bf16[2064,128]{1,0:T(8,128)(2,1)S(1)}, u32[]{:S(2)}, u32[]{:S(2)}) collective-permute-start(bf16[2064,128]{1,0:T(8,128)(2,1)S(1)} %collective-permute-done.1.refs_3_), channel_id=1, source_target_pairs={{0,4},{4,8},{8,12},{12,14},{14,10},{10,6},{6,2},{2,0},{1,5},{5,9},... | collective-permute-start | bytes 1585160 | tf_op jit(solution)/shard_map/low_ahead/ppermute | solution.py:292
  50.3 15.1 %collective-permute-start.9 = (bf16[2064,128]{1,0:T(8,128)(2,1)}, bf16[2064,128]{1,0:T(8,128)(2,1)S(1)}, u32[]{:S(2)}, u32[]{:S(2)}) collective-permute-start(bf16[2064,128]{1,0:T(8,128)(2,1)} %collective-permute-done.3.refs_6_), channel_id=1, source_target_pairs={{4,0},{8,4},{12,8},{14,12},{10,14},{6,10},{2,6},{0,2},{5,1},{9,5},... | collective-permute-start | bytes 1585160 | tf_op jit(solution)/shard_map/high_back/ppermute | solution.py:292
  51.9 22.6 %collective-permute-start.15 = (bf16[2048,128]{1,0:T(8,128)(2,1)}, bf16[2048,128]{1,0:T(8,128)(2,1)S(1)}, u32[]{:S(2)}, u32[]{:S(2)}) collective-permute-start(bf16[2048,128]{1,0:T(8,128)(2,1)} %collective-permute-done.10.refs_4_), channel_id=1, source_target_pairs={{0,4},{4,8},{8,12},{12,14},{14,10},{10,6},{6,2},{2,0},{1,5},{5,9},... | collective-permute-start | bytes 1572872 | tf_op jit(solution)/shard_map/high_ahead/ppermute | solution.py:292
  53.7 23.0 %collective-permute-start.16 = (bf16[2048,128]{1,0:T(8,128)(2,1)}, bf16[2048,128]{1,0:T(8,128)(2,1)S(1)}, u32[]{:S(2)}, u32[]{:S(2)}) collective-permute-start(bf16[2048,128]{1,0:T(8,128)(2,1)} %collective-permute-done.11.refs_5_), channel_id=1, source_target_pairs={{4,0},{8,4},{12,8},{14,12},{10,14},{6,10},{2,6},{0,2},{5,1},{9,5},... | collective-permute-start | bytes 1572872 | tf_op jit(solution)/shard_map/low_back/ppermute | solution.py:292
  65.5 17.5 %collective-permute-start.12 = (bf16[1552,128]{1,0:T(8,128)(2,1)S(1)}, bf16[1552,128]{1,0:T(8,128)(2,1)S(1)}, u32[]{:S(2)}, u32[]{:S(2)}) collective-permute-start(bf16[1552,128]{1,0:T(8,128)(2,1)S(1)} %slice.67), channel_id=1, source_target_pairs={{0,4},{4,8},{8,12},{12,14},{14,10},{10,6},{6,2},{2,0},{1,5},{5,9},... | collective-permute-start | bytes 1191944 | tf_op jit(solution)/shard_map/far_low_ahead/ppermute | solution.py:292
  67.1 18.0 %collective-permute-start.17 = (bf16[1552,128]{1,0:T(8,128)(2,1)S(1)}, bf16[1552,128]{1,0:T(8,128)(2,1)S(1)}, u32[]{:S(2)}, u32[]{:S(2)}) collective-permute-start(bf16[1552,128]{1,0:T(8,128)(2,1)S(1)} %slice.73), channel_id=1, source_target_pairs={{4,0},{8,4},{12,8},{14,12},{10,14},{6,10},{2,6},{0,2},{5,1},{9,5},... | collective-permute-start | bytes 1191944 | tf_op jit(solution)/shard_map/far_high_back/ppermute | solution.py:292
  67.6 20.1 %collective-permute-start.13 = (bf16[512,128]{1,0:T(8,128)(2,1)S(1)}, bf16[512,128]{1,0:T(8,128)(2,1)S(1)}, u32[]{:S(2)}, u32[]{:S(2)}) collective-permute-start(bf16[512,128]{1,0:T(8,128)(2,1)S(1)} %slice.69), channel_id=1, source_target_pairs={{0,4},{4,8},{8,12},{12,14},{14,10},{10,6},{6,2},{2,0},{1,5},{5,9},... | collective-permute-start | bytes 393224 | tf_op jit(solution)/shard_map/last_low_ahead/ppermute | solution.py:292
  74.5 13.3 %collective-permute-start.14 = (bf16[512,128]{1,0:T(8,128)(2,1)S(1)}, bf16[512,128]{1,0:T(8,128)(2,1)S(1)}, u32[]{:S(2)}, u32[]{:S(2)}) collective-permute-start(bf16[512,128]{1,0:T(8,128)(2,1)S(1)} %slice.70), channel_id=1, source_target_pairs={{4,0},{8,4},{12,8},{14,12},{10,14},{6,10},{2,6},{0,2},{5,1},{9,5},... | collective-permute-start | bytes 393224 | tf_op jit(solution)/shard_map/last_high_back/ppermute | solution.py:292

commit v4 on v3

--- a/solution.py
+++ b/solution.py
@@ -164,64 +164,56 @@
     )(*operands)
 
 
-def finish_kernel(offset, starts, size, cycle, index, low, high, right, total, *refs):
+def finish_kernel(parts, offset, cycle_ref, index_ref, right, total, *refs):
     out_ref, staged, sems = refs[-3:]
-    slots, blk = index.shape[0], low.shape[-1]
+    arrays = refs[: len(refs) - 3]
+    slots, blk = index_ref.shape[0], right.shape[2]
     wide = 2 * blk
+    index, piece = index_ref[...], cycle_ref[...][0, offset]
     copies = []
-    for half_ref, start in ((low, starts[0]), (high, starts[1])):
-        for i in range(size):
-            row, at = start + i, len(copies)
-            inner = [index[s, row] for s in range(slots)]
-            parts = []
-            for s in range(slots):
-                part = half_ref[(i * slots + s) * blk : (i * slots + s + 1) * blk, :]
-                parts.append(part * jnp.where(inner[s] >= 0, 1.0, 0.0).astype(jnp.bfloat16))
-            factor = jnp.concatenate(parts, axis=1)
-            for c in range(BJ // 2):
-                columns = slice(c * wide, (c + 1) * wide)
-                rows_of = jnp.concatenate(
-                    [right[0, jnp.maximum(k, 0), :, columns] for k in inner], axis=0
-                )
-                term = jnp.dot(factor, rows_of, preferred_element_type=jnp.float32)
-                result = (total[row, :, columns] + term).astype(jnp.bfloat16)
-                for j in range(2):
-                    staged[at, c * 2 + j] = result[:, j * blk : (j + 1) * blk]
-            copies.append(pltpu.make_async_copy(staged.at[at], out_ref.at[row, 0], sems.at[at]))
-            copies[-1].start()
+    for at, (row, places) in enumerate(parts):
+        inner = [index[s, row] for s in range(slots)]
+        factor = []
+        for s, (array, start) in enumerate(places):
+            filled = jnp.where(inner[s] >= 0, 1.0, 0.0).astype(jnp.bfloat16)
+            factor.append(arrays[array][start : start + blk, :] * filled)
+        factor = jnp.concatenate(factor, axis=1)
+        for c in range(BJ // 2):
+            columns = slice(c * wide, (c + 1) * wide)
+            rows_of = jnp.concatenate(
+                [right[piece, jnp.maximum(k, 0), :, columns] for k in inner], axis=0
+            )
+            term = jnp.dot(factor, rows_of, preferred_element_type=jnp.float32)
+            result = (total[row, :, columns] + term).astype(jnp.bfloat16)
+            for j in range(2):
+                staged[at, c * 2 + j] = result[:, j * blk : (j + 1) * blk]
+        copies.append(pltpu.make_async_copy(staged.at[at], out_ref.at[row, 0], sems.at[at]))
+        copies[-1].start()
     for copy in copies:
         copy.wait()
 
 
-def finish(cycle, offset, index, low, high, right, total, starts, size, target):
+def finish(parts, cycle, offset, index, right, total, arrays, target):
     rows, blk = total.shape[0], total.shape[1]
-    inner_width = right.shape[1]
     whole = pl.BlockSpec(memory_space=pltpu.VMEM)
-    piece = pl.BlockSpec(
-        (1, inner_width, blk, BJ * blk), lambda g, c, *p: (c[offset], 0, 0, 0)
-    )
-    operands = [cycle, index, low, high, right, total]
-    in_specs = [whole, whole, piece, whole]
+    operands = [cycle[None], index, right, total, *arrays]
+    in_specs = [whole] * len(operands)
     aliases = {}
     if target is not None:
         in_specs.append(pl.BlockSpec(memory_space=pl.ANY))
         operands.append(target)
         aliases = {len(operands) - 1: 0}
     return pl.pallas_call(
-        functools.partial(finish_kernel, offset, starts, size),
+        functools.partial(finish_kernel, parts, offset),
         out_shape=jax.ShapeDtypeStruct((rows, 1, BJ, blk, blk), jnp.bfloat16),
-        grid_spec=pltpu.PrefetchScalarGridSpec(
-            num_scalar_prefetch=2,
-            grid=(1,),
-            in_specs=in_specs,
-            out_specs=pl.BlockSpec(memory_space=pl.ANY),
-            scratch_shapes=[
-                pltpu.VMEM((2 * size, BJ, blk, blk), jnp.bfloat16),
-                pltpu.SemaphoreType.DMA((2 * size,)),
-            ],
-        ),
+        in_specs=in_specs,
+        out_specs=pl.BlockSpec(memory_space=pl.ANY),
+        scratch_shapes=[
+            pltpu.VMEM((len(parts), BJ, blk, blk), jnp.bfloat16),
+            pltpu.SemaphoreType.DMA((len(parts),)),
+        ],
         input_output_aliases=aliases,
-        compiler_params=pltpu.CompilerParams(vmem_limit_bytes=VMEM_LIMIT),
+        compiler_params=pltpu.CompilerParams(vmem_limit_bytes=VMEM_LIMIT // 2),
         name="finish",
         cost_estimate=pl.CostEstimate(flops=0, bytes_accessed=0, transcendentals=0),
     )(*operands)
@@ -350,11 +342,14 @@
     last_parts = [large_parts, small_parts]
     out = None
     far_index = read_note(last_parts[0][2])
+    per_row = slots * blk
     for start, size, low, high in last_parts:
-        starts = (start, half + start)
-        out = finish(
-            cycle, n // 2, far_index, low, high, right, total, starts, size, out
-        )
+        parts = [
+            (h * half + start + i, [(h, i * per_row + s * blk) for s in range(slots)])
+            for h in range(2)
+            for i in range(size)
+        ]
+        out = finish(parts, cycle, n // 2, far_index, right, total, [low, high], out)
     return out
 
 

time: 89.9 us -> 89 us (0.990)
  Pallas kernels: 28.1 us -> 27.2 us
where the time goes in v4:
time: 89 us; the launch traced here: 88.7 us
  waiting for transfers between devices  35.1 us (39%)
  Pallas kernels  27.2 us (31%)
  starting transfers between devices  18.8 us (21%)
  local copies, waits for them, and re-layouts  5.29 us (6%)
  other arithmetic  2.03 us (2%)
    ppermute x16, waiting for transfers between devices, move(): return lax.ppermute(array, 'row', way)  34.7 us
    ppermute x16, starting transfers between devices, move(): return lax.ppermute(array, 'row', way)  18.3 us
    pallas_call x3, Pallas kernels, product(): pl.pallas_call(functools.partial(product_kernel, offsets, sides, starts,...  15.8 us
    pallas_call x1, Pallas kernels, densify(): pl.pallas_call(densify_kernel, out_shape=jax.ShapeDtypeStruct((2 * pieces...  5.9 us
    pallas_call x2, Pallas kernels, finish(): pl.pallas_call(functools.partial(finish_kernel, parts, offset), out_shape...  3.5 us
    slice x1, local copies, waits for them, and re-layouts, body(): low_second, high_second = (flat[:cut], flat[cut:])  2.08 us
    pallas_call x1, Pallas kernels, pack(): pl.pallas_call(pack_kernel, out_shape=(half, half), in_specs=[pl.BlockSpe...  2.03 us
    convert_element_type x6, other arithmetic, read_note(): return message[-NOTE_ROWS:][:slots, :rows].astype(jnp.int32)  2.03 us
  transfers between devices with their start and end apart: 18, of which 12 were waited for; matrix products, arithmetic and copies ran while one was open for 6% of the time, Pallas kernels for 29%

profile of v4, /device:TPU:0, one launch (start us, length us, event | category | flops | bytes accessed | tf_op | source)
XLA Modules:
  0.0 88.7 jit_solution(7544649933778554148)
XLA Ops:
  0.5 2.0 %pack.1 = (bf16[2064,128]{1,0:T(8,128)(2,1)S(1)}, bf16[2064,128]{1,0:T(8,128)(2,1)}) custom-call(bf16[4096,128]{1,0:T(8,128)(2,1)} %bitcast.18, s32[2,16]{1,0:T(2,128)} %bitcast.16), custom_call_target="tpu_custom_call" | custom-call | tf_op jit(solution)/shard_map/pack/pallas_call | solution.py:247
  2.5 2.6 %collective-permute-start = (bf16[2064,128]{1,0:T(8,128)(2,1)S(1)}, bf16[2064,128]{1,0:T(8,128)(2,1)}, u32[]{:S(2)}, u32[]{:S(2)}) collective-permute-start(bf16[2064,128]{1,0:T(8,128)(2,1)S(1)} %get-tuple-element.15.refs_4_), channel_id=1, source_target_pairs={{0,4},{4,8},{8,12},{12,14},{14,10},{10,6},{6,2},{2,0},{1,5},{5,9},... | collective-permute-start | bytes 1585160 | tf_op jit(solution)/shard_map/low_ahead/ppermute | solution.py:284
  5.2 2.1 %fusion.1 = (bf16[8,1,2,128,128]{4,3,2,1,0:T(8,128)(2,1)}, bf16[8,1,2,128,128]{4,3,2,1,0:T(8,128)(2,1)S(1)}) fusion(bf16[16,1,2,128,128]{4,3,2,1,0:T(8,128)(2,1)} %param.5), kind=kLoop, calls=%fused_computation.9 | loop fusion | bytes 2097152 | tf_op jit(solution)/shard_map/slice | solution.py:277
  7.2 2.0 %collective-permute-start.4 = (bf16[2048,128]{1,0:T(8,128)(2,1)S(1)}, bf16[2048,128]{1,0:T(8,128)(2,1)}, u32[]{:S(2)}, u32[]{:S(2)}) collective-permute-start(bf16[2048,128]{1,0:T(8,128)(2,1)S(1)} %bitcast.14), channel_id=1, source_target_pairs={{0,4},{4,8},{8,12},{12,14},{14,10},{10,6},{6,2},{2,0},{1,5},{5,9},... | collective-permute-start | bytes 1572872 | tf_op jit(solution)/shard_map/high_ahead/ppermute | solution.py:284
  9.3 8.8 %collective-permute-done.refs_6_ = bf16[2064,128]{1,0:T(8,128)(2,1)} collective-permute-done((bf16[2064,128]{1,0:T(8,128)(2,1)S(1)}, bf16[2064,128]{1,0:T(8,128)(2,1)}, u32[]{:S(2)}, u32[]{:S(2)}) %collective-permute-start) | collective-permute-done | bytes 528416 | tf_op jit(solution)/shard_map/low_ahead/ppermute | solution.py:284
  18.1 2.0 %collective-permute-start.1 = (bf16[2064,128]{1,0:T(8,128)(2,1)}, bf16[2064,128]{1,0:T(8,128)(2,1)S(1)}, u32[]{:S(2)}, u32[]{:S(2)}) collective-permute-start(bf16[2064,128]{1,0:T(8,128)(2,1)} %collective-permute-done.refs_6_), channel_id=1, source_target_pairs={{0,4},{4,8},{8,12},{12,14},{14,10},{10,6},{6,2},{2,0},{1,5},{5,9},... | collective-permute-start | bytes 1585160 | tf_op jit(solution)/shard_map/low_ahead/ppermute | solution.py:284
  21.0 8.3 %collective-permute-done.4.refs_7_ = bf16[2048,128]{1,0:T(8,128)(2,1)} collective-permute-done((bf16[2048,128]{1,0:T(8,128)(2,1)S(1)}, bf16[2048,128]{1,0:T(8,128)(2,1)}, u32[]{:S(2)}, u32[]{:S(2)}) %collective-permute-start.4) | collective-permute-done | bytes 524320 | tf_op jit(solution)/shard_map/high_ahead/ppermute | solution.py:284
  29.3 2.0 %collective-permute-start.10 = (bf16[2048,128]{1,0:T(8,128)(2,1)}, bf16[2048,128]{1,0:T(8,128)(2,1)}, u32[]{:S(2)}, u32[]{:S(2)}) collective-permute-start(bf16[2048,128]{1,0:T(8,128)(2,1)} %collective-permute-done.4.refs_7_), channel_id=1, source_target_pairs={{0,4},{4,8},{8,12},{12,14},{14,10},{10,6},{6,2},{2,0},{1,5},{5,9},... | collective-permute-start | bytes 1572872 | tf_op jit(solution)/shard_map/high_ahead/ppermute | solution.py:284
  34.3 1.6 %copy-done = bf16[16,1,4,128,128]{4,3,2,1,0:T(8,128)(2,1)S(1)} copy-done((bf16[16,1,4,128,128]{4,3,2,1,0:T(8,128)(2,1)S(1)}, bf16[16,1,4,128,128]{4,3,2,1,0:T(8,128)(2,1)}, u32[]{:S(2)}) %copy-start) | copy-done | bytes 2097176
  35.8 5.9 %densify.1.refs_10_.refs_11_.refs_12_.refs_7_.refs_8_.right = bf16[8,4,128,1024]{3,2,1,0:T(8,128)(2,1)S(1)} custom-call(s32[1]{0:T(128)} %bitcast.7.col_ref, s32[64]{0:T(128)S(1)} %reshape.9.own_index, s32[64]{0:T(128)S(1)} %collective-permute-done.7.other_index, bf16[16,4,128,128]{3,2,1,0:T(8,128)(2,1)S(1)} %bitcast.13, ...), custom_call_target="tpu_custom_call" | custom-call | tf_op jit(solution)/shard_map/densify/pallas_call | solution.py:44
  41.8 6.4 %product.3.refs_9_ = f32[16,128,1024]{2,1,0:T(8,128)S(1)} custom-call(s32[8]{0:T(128)S(1)} %get-tuple-element.27.refs_0_, s32[2,16]{1,0:T(2,128)S(1)} %bitcast.17, s32[2,16]{1,0:T(2,128)S(1)} %slice_convert_fusion.2.refs_2_, s32[2,16]{1,0:T(2,128)S(1)} %slice_convert_fusion.1.refs_3_, bf16[2064,128]{1,0:T(8,128)(2,1)S(1)} %copy-done.2, ...), custom_call_target="tpu_custom_call" | custom-call | tf_op jit(solution)/shard_map/product/pallas_call | solution.py:148
  48.2 2.1 %collective-permute-start.8 = (bf16[2064,128]{1,0:T(8,128)(2,1)S(1)}, bf16[2064,128]{1,0:T(8,128)(2,1)S(1)}, u32[]{:S(2)}, u32[]{:S(2)}) collective-permute-start(bf16[2064,128]{1,0:T(8,128)(2,1)S(1)} %collective-permute-done.1.refs_3_), channel_id=1, source_target_pairs={{0,4},{4,8},{8,12},{12,14},{14,10},{10,6},{6,2},{2,0},{1,5},{5,9},... | collective-permute-start | bytes 1585160 | tf_op jit(solution)/shard_map/low_ahead/ppermute | solution.py:284
  51.9 1.8 %collective-permute-start.13 = (bf16[2048,128]{1,0:T(8,128)(2,1)}, bf16[2048,128]{1,0:T(8,128)(2,1)S(1)}, u32[]{:S(2)}, u32[]{:S(2)}) collective-permute-start(bf16[2048,128]{1,0:T(8,128)(2,1)} %collective-permute-done.10.refs_4_), channel_id=1, source_target_pairs={{0,4},{4,8},{8,12},{12,14},{14,10},{10,6},{6,2},{2,0},{1,5},{5,9},... | collective-permute-start | bytes 1572872 | tf_op jit(solution)/shard_map/high_ahead/ppermute | solution.py:284
  54.6 5.4 %product.4.refs_9_ = f32[16,128,1024]{2,1,0:T(8,128)S(1)} custom-call(s32[8]{0:T(128)S(1)} %get-tuple-element.27.refs_0_, s32[2,16]{1,0:T(2,128)S(1)} %get-tuple-element.30.refs_1_, s32[2,16]{1,0:T(2,128)S(1)} %get-tuple-element.29.refs_2_, bf16[2064,128]{1,0:T(8,128)(2,1)S(1)} %collective-permute-done.1.refs_3_, ...), custom_call_target="tpu_custom_call", output_to_operand_aliasing={{}: (9, {})} | custom-call | tf_op jit(solution)/shard_map/product/pallas_call | solution.py:148
  59.9 3.3 %collective-permute-done.8.refs_3_ = bf16[2064,128]{1,0:T(8,128)(2,1)S(1)} collective-permute-done((bf16[2064,128]{1,0:T(8,128)(2,1)S(1)}, bf16[2064,128]{1,0:T(8,128)(2,1)S(1)}, u32[]{:S(2)}, u32[]{:S(2)}) %collective-permute-start.8) | collective-permute-done | bytes 528416 | tf_op jit(solution)/shard_map/low_ahead/ppermute | solution.py:284
  63.2 2.2 %collective-permute-done.9.refs_6_ = bf16[2064,128]{1,0:T(8,128)(2,1)S(1)} collective-permute-done((bf16[2064,128]{1,0:T(8,128)(2,1)}, bf16[2064,128]{1,0:T(8,128)(2,1)S(1)}, u32[]{:S(2)}, u32[]{:S(2)}) %collective-permute-start.9) | collective-permute-done | bytes 528416 | tf_op jit(solution)/shard_map/high_back/ppermute | solution.py:284
  65.5 1.6 %collective-permute-start.12 = (bf16[1552,128]{1,0:T(8,128)(2,1)S(1)}, bf16[1552,128]{1,0:T(8,128)(2,1)S(1)}, u32[]{:S(2)}, u32[]{:S(2)}) collective-permute-start(bf16[1552,128]{1,0:T(8,128)(2,1)S(1)} %slice.67), channel_id=1, source_target_pairs={{0,4},{4,8},{8,12},{12,14},{14,10},{10,6},{6,2},{2,0},{1,5},{5,9},... | collective-permute-start | bytes 1191944 | tf_op jit(solution)/shard_map/far_low_ahead/ppermute | solution.py:284
  67.6 1.6 %collective-permute-start.15 = (bf16[512,128]{1,0:T(8,128)(2,1)S(1)}, bf16[512,128]{1,0:T(8,128)(2,1)S(1)}, u32[]{:S(2)}, u32[]{:S(2)}) collective-permute-start(bf16[512,128]{1,0:T(8,128)(2,1)S(1)} %slice.71), channel_id=1, source_target_pairs={{0,4},{4,8},{8,12},{12,14},{14,10},{10,6},{6,2},{2,0},{1,5},{5,9},... | collective-permute-start | bytes 393224 | tf_op jit(solution)/shard_map/last_low_ahead/ppermute | solution.py:284
  69.1 5.3 %collective-permute-done.13.refs_4_ = bf16[2048,128]{1,0:T(8,128)(2,1)S(1)} collective-permute-done((bf16[2048,128]{1,0:T(8,128)(2,1)}, bf16[2048,128]{1,0:T(8,128)(2,1)S(1)}, u32[]{:S(2)}, u32[]{:S(2)}) %collective-permute-start.13) | collective-permute-done | bytes 524320 | tf_op jit(solution)/shard_map/high_ahead/ppermute | solution.py:284
  74.4 1.9 %collective-permute-start.16 = (bf16[512,128]{1,0:T(8,128)(2,1)S(1)}, bf16[512,128]{1,0:T(8,128)(2,1)S(1)}, u32[]{:S(2)}, u32[]{:S(2)}) collective-permute-start(bf16[512,128]{1,0:T(8,128)(2,1)S(1)} %slice.72), channel_id=1, source_target_pairs={{4,0},{8,4},{12,8},{14,12},{10,14},{6,10},{2,6},{0,2},{5,1},{9,5},... | collective-permute-start | bytes 393224 | tf_op jit(solution)/shard_map/last_high_back/ppermute | solution.py:284
  76.6 4.1 %product.5.total = f32[16,128,1024]{2,1,0:T(8,128)S(1)} custom-call(s32[8]{0:T(128)S(1)} %get-tuple-element.27.refs_0_, s32[2,16]{1,0:T(2,128)S(1)} %slice_convert_fusion.4.refs_1_, s32[2,16]{1,0:T(2,128)S(1)} %slice_convert_fusion.3.refs_2_, bf16[2064,128]{1,0:T(8,128)(2,1)S(1)} %collective-permute-done.8.refs_3_, ...), custom_call_target="tpu_custom_call", output_to_operand_aliasing={{}: (9, {})} | custom-call | tf_op jit(solution)/shard_map/product/pallas_call | solution.py:148
  80.7 2.3 %collective-permute-done.12.refs_0_ = bf16[1552,128]{1,0:T(8,128)(2,1)S(1)} collective-permute-done((bf16[1552,128]{1,0:T(8,128)(2,1)S(1)}, bf16[1552,128]{1,0:T(8,128)(2,1)S(1)}, u32[]{:S(2)}, u32[]{:S(2)}) %collective-permute-start.12) | collective-permute-done | bytes 397344 | tf_op jit(solution)/shard_map/far_low_ahead/ppermute | solution.py:284
  83.0 2.2 %collective-permute-done.17.refs_1_ = bf16[1552,128]{1,0:T(8,128)(2,1)S(1)} collective-permute-done((bf16[1552,128]{1,0:T(8,128)(2,1)S(1)}, bf16[1552,128]{1,0:T(8,128)(2,1)S(1)}, u32[]{:S(2)}, u32[]{:S(2)}) %collective-permute-start.17) | collective-permute-done | bytes 397344 | tf_op jit(solution)/shard_map/far_high_back/ppermute | solution.py:284
  85.1 2.1 %finish.2.refs_2_ = bf16[16,1,8,128,128]{4,3,2,1,0:T(8,128)(2,1)} custom-call(s32[1,8]{1,0:T(1,128)S(1)} %get-tuple-element.28.cycle_ref, s32[2,16]{1,0:T(2,128)S(1)} %slice_convert_fusion.index_ref, bf16[8,4,128,1024]{3,2,1,0:T(8,128)(2,1)S(1)} %densify.1.refs_10_.refs_11_.refs_12_.refs_7_.refs_8_.right, f32[16,128,1024]{2,1,0:T(8,128)S(1)} %product.5.total, ...), custom_call_target="tpu_custom_call" | custom-call | tf_op jit(solution)/shard_map/finish/pallas_call | solution.py:206
  (41 shorter events, 9.1 us)
Async XLA Ops:
  0.0 41.8 %copy-start.3 = (s32[16,1,2]{0,2,1:T(2,128)S(1)}, s32[16,1,2]{0,2,1:T(2,128)}, u32[]{:S(2)}) copy-start(s32[16,1,2]{0,2,1:T(2,128)} %param.6) | copy-start | bytes 388
  0.0 32.2 %collective-permute-start.6 = (bf16[16,4,128,128]{3,2,1,0:T(8,128)(2,1)}, bf16[16,4,128,128]{3,2,1,0:T(8,128)(2,1)S(1)}, u32[]{:S(2)}, u32[]{:S(2)}) collective-permute-start(bf16[16,4,128,128]{3,2,1,0:T(8,128)(2,1)} %bitcast.12), channel_id=1, source_target_pairs={{0,1},{1,0},{2,3},{3,2},{4,5},{5,4},{6,7},{7,6},{8,9},{9,8},{10,11... | collective-permute-start | bytes 6291464 | tf_op jit(solution)/shard_map/ppermute | solution.py:299
  2.5 6.8 %copy-start.1 = (bf16[2064,128]{1,0:T(8,128)(2,1)}, bf16[2064,128]{1,0:T(8,128)(2,1)S(1)}, u32[]{:S(2)}) copy-start(bf16[2064,128]{1,0:T(8,128)(2,1)S(1)} %get-tuple-element.15.refs_4_) | copy-start | bytes 1585156
  2.5 15.6 %collective-permute-start = (bf16[2064,128]{1,0:T(8,128)(2,1)S(1)}, bf16[2064,128]{1,0:T(8,128)(2,1)}, u32[]{:S(2)}, u32[]{:S(2)}) collective-permute-start(bf16[2064,128]{1,0:T(8,128)(2,1)S(1)} %get-tuple-element.15.refs_4_), channel_id=1, source_target_pairs={{0,4},{4,8},{8,12},{12,14},{14,10},{10,6},{6,2},{2,0},{1,5},{5,9},... | collective-permute-start | bytes 1585160 | tf_op jit(solution)/shard_map/low_ahead/ppermute | solution.py:284
  5.1 15.2 %collective-permute-start.2 = (bf16[2064,128]{1,0:T(8,128)(2,1)}, bf16[2064,128]{1,0:T(8,128)(2,1)}, u32[]{:S(2)}, u32[]{:S(2)}) collective-permute-start(bf16[2064,128]{1,0:T(8,128)(2,1)} %get-tuple-element.16), channel_id=1, source_target_pairs={{4,0},{8,4},{12,8},{14,12},{10,14},{6,10},{2,6},{0,2},{5,1},{9,5},... | collective-permute-start | bytes 1585160 | tf_op jit(solution)/shard_map/high_back/ppermute | solution.py:284
  7.2 22.1 %collective-permute-start.4 = (bf16[2048,128]{1,0:T(8,128)(2,1)S(1)}, bf16[2048,128]{1,0:T(8,128)(2,1)}, u32[]{:S(2)}, u32[]{:S(2)}) collective-permute-start(bf16[2048,128]{1,0:T(8,128)(2,1)S(1)} %bitcast.14), channel_id=1, source_target_pairs={{0,4},{4,8},{8,12},{12,14},{14,10},{10,6},{6,2},{2,0},{1,5},{5,9},... | collective-permute-start | bytes 1572872 | tf_op jit(solution)/shard_map/high_ahead/ppermute | solution.py:284
  9.2 22.3 %collective-permute-start.5 = (bf16[2048,128]{1,0:T(8,128)(2,1)}, bf16[2048,128]{1,0:T(8,128)(2,1)}, u32[]{:S(2)}, u32[]{:S(2)}) collective-permute-start(bf16[2048,128]{1,0:T(8,128)(2,1)} %bitcast.6), channel_id=1, source_target_pairs={{4,0},{8,4},{12,8},{14,12},{10,14},{6,10},{2,6},{0,2},{5,1},{9,5},... | collective-permute-start | bytes 1572872 | tf_op jit(solution)/shard_map/low_back/ppermute | solution.py:284
  18.1 30.1 %collective-permute-start.1 = (bf16[2064,128]{1,0:T(8,128)(2,1)}, bf16[2064,128]{1,0:T(8,128)(2,1)S(1)}, u32[]{:S(2)}, u32[]{:S(2)}) collective-permute-start(bf16[2064,128]{1,0:T(8,128)(2,1)} %collective-permute-done.refs_6_), channel_id=1, source_target_pairs={{0,4},{4,8},{8,12},{12,14},{14,10},{10,6},{6,2},{2,0},{1,5},{5,9},... | collective-permute-start | bytes 1585160 | tf_op jit(solution)/shard_map/low_ahead/ppermute | solution.py:284
  20.3 27.9 %collective-permute-start.3 = (bf16[2064,128]{1,0:T(8,128)(2,1)}, bf16[2064,128]{1,0:T(8,128)(2,1)}, u32[]{:S(2)}, u32[]{:S(2)}) collective-permute-start(bf16[2064,128]{1,0:T(8,128)(2,1)} %collective-permute-done.2.refs_9_), channel_id=1, source_target_pairs={{4,0},{8,4},{12,8},{14,12},{10,14},{6,10},{2,6},{0,2},{5,1},{9,5},... | collective-permute-start | bytes 1585160 | tf_op jit(solution)/shard_map/high_back/ppermute | solution.py:284
  29.3 22.6 %collective-permute-start.10 = (bf16[2048,128]{1,0:T(8,128)(2,1)}, bf16[2048,128]{1,0:T(8,128)(2,1)}, u32[]{:S(2)}, u32[]{:S(2)}) collective-permute-start(bf16[2048,128]{1,0:T(8,128)(2,1)} %collective-permute-done.4.refs_7_), channel_id=1, source_target_pairs={{0,4},{4,8},{8,12},{12,14},{14,10},{10,6},{6,2},{2,0},{1,5},{5,9},... | collective-permute-start | bytes 1572872 | tf_op jit(solution)/shard_map/high_ahead/ppermute | solution.py:284
  31.5 22.1 %collective-permute-start.11 = (bf16[2048,128]{1,0:T(8,128)(2,1)}, bf16[2048,128]{1,0:T(8,128)(2,1)}, u32[]{:S(2)}, u32[]{:S(2)}) collective-permute-start(bf16[2048,128]{1,0:T(8,128)(2,1)} %collective-permute-done.5.refs_8_), channel_id=1, source_target_pairs={{4,0},{8,4},{12,8},{14,12},{10,14},{6,10},{2,6},{0,2},{5,1},{9,5},... | collective-permute-start | bytes 1572872 | tf_op jit(solution)/shard_map/low_back/ppermute | solution.py:284
  33.1 1.2 %collective-permute-start.7 = (s32[64]{0:T(128)S(1)}, s32[64]{0:T(128)S(1)}, u32[]{:S(2)}, u32[]{:S(2)}) collective-permute-start(s32[64]{0:T(128)S(1)} %reshape.9.own_index), channel_id=1, source_target_pairs={{0,1},{1,0},{2,3},{3,2},{4,5},{5,4},{6,7},{7,6},{8,9},{9,8},{10,11... | collective-permute-start | bytes 776 | tf_op jit(solution)/shard_map/ppermute | solution.py:301
  34.3 1.6 %copy-start = (bf16[16,1,4,128,128]{4,3,2,1,0:T(8,128)(2,1)S(1)}, bf16[16,1,4,128,128]{4,3,2,1,0:T(8,128)(2,1)}, u32[]{:S(2)}) copy-start(bf16[16,1,4,128,128]{4,3,2,1,0:T(8,128)(2,1)} %param.7) | copy-start | bytes 6291460
  35.8 5.9 %copy-start.2 = (bf16[2064,128]{1,0:T(8,128)(2,1)S(1)}, bf16[2064,128]{1,0:T(8,128)(2,1)}, u32[]{:S(2)}) copy-start(bf16[2064,128]{1,0:T(8,128)(2,1)} %copy-done.1) | copy-start | bytes 1585156
  48.2 15.0 %collective-permute-start.8 = (bf16[2064,128]{1,0:T(8,128)(2,1)S(1)}, bf16[2064,128]{1,0:T(8,128)(2,1)S(1)}, u32[]{:S(2)}, u32[]{:S(2)}) collective-permute-start(bf16[2064,128]{1,0:T(8,128)(2,1)S(1)} %collective-permute-done.1.refs_3_), channel_id=1, source_target_pairs={{0,4},{4,8},{8,12},{12,14},{14,10},{10,6},{6,2},{2,0},{1,5},{5,9},... | collective-permute-start | bytes 1585160 | tf_op jit(solution)/shard_map/low_ahead/ppermute | solution.py:284
  50.3 15.1 %collective-permute-start.9 = (bf16[2064,128]{1,0:T(8,128)(2,1)}, bf16[2064,128]{1,0:T(8,128)(2,1)S(1)}, u32[]{:S(2)}, u32[]{:S(2)}) collective-permute-start(bf16[2064,128]{1,0:T(8,128)(2,1)} %collective-permute-done.3.refs_6_), channel_id=1, source_target_pairs={{4,0},{8,4},{12,8},{14,12},{10,14},{6,10},{2,6},{0,2},{5,1},{9,5},... | collective-permute-start | bytes 1585160 | tf_op jit(solution)/shard_map/high_back/ppermute | solution.py:284
  51.9 22.6 %collective-permute-start.13 = (bf16[2048,128]{1,0:T(8,128)(2,1)}, bf16[2048,128]{1,0:T(8,128)(2,1)S(1)}, u32[]{:S(2)}, u32[]{:S(2)}) collective-permute-start(bf16[2048,128]{1,0:T(8,128)(2,1)} %collective-permute-done.10.refs_4_), channel_id=1, source_target_pairs={{0,4},{4,8},{8,12},{12,14},{14,10},{10,6},{6,2},{2,0},{1,5},{5,9},... | collective-permute-start | bytes 1572872 | tf_op jit(solution)/shard_map/high_ahead/ppermute | solution.py:284
  53.7 23.0 %collective-permute-start.14 = (bf16[2048,128]{1,0:T(8,128)(2,1)}, bf16[2048,128]{1,0:T(8,128)(2,1)S(1)}, u32[]{:S(2)}, u32[]{:S(2)}) collective-permute-start(bf16[2048,128]{1,0:T(8,128)(2,1)} %collective-permute-done.11.refs_5_), channel_id=1, source_target_pairs={{4,0},{8,4},{12,8},{14,12},{10,14},{6,10},{2,6},{0,2},{5,1},{9,5},... | collective-permute-start | bytes 1572872 | tf_op jit(solution)/shard_map/low_back/ppermute | solution.py:284
  65.5 17.5 %collective-permute-start.12 = (bf16[1552,128]{1,0:T(8,128)(2,1)S(1)}, bf16[1552,128]{1,0:T(8,128)(2,1)S(1)}, u32[]{:S(2)}, u32[]{:S(2)}) collective-permute-start(bf16[1552,128]{1,0:T(8,128)(2,1)S(1)} %slice.67), channel_id=1, source_target_pairs={{0,4},{4,8},{8,12},{12,14},{14,10},{10,6},{6,2},{2,0},{1,5},{5,9},... | collective-permute-start | bytes 1191944 | tf_op jit(solution)/shard_map/far_low_ahead/ppermute | solution.py:284
  67.1 18.0 %collective-permute-start.17 = (bf16[1552,128]{1,0:T(8,128)(2,1)S(1)}, bf16[1552,128]{1,0:T(8,128)(2,1)S(1)}, u32[]{:S(2)}, u32[]{:S(2)}) collective-permute-start(bf16[1552,128]{1,0:T(8,128)(2,1)S(1)} %slice.73), channel_id=1, source_target_pairs={{4,0},{8,4},{12,8},{14,12},{10,14},{6,10},{2,6},{0,2},{5,1},{9,5},... | collective-permute-start | bytes 1191944 | tf_op jit(solution)/shard_map/far_high_back/ppermute | solution.py:284
  67.6 19.7 %collective-permute-start.15 = (bf16[512,128]{1,0:T(8,128)(2,1)S(1)}, bf16[512,128]{1,0:T(8,128)(2,1)S(1)}, u32[]{:S(2)}, u32[]{:S(2)}) collective-permute-start(bf16[512,128]{1,0:T(8,128)(2,1)S(1)} %slice.71), channel_id=1, source_target_pairs={{0,4},{4,8},{8,12},{12,14},{14,10},{10,6},{6,2},{2,0},{1,5},{5,9},... | collective-permute-start | bytes 393224 | tf_op jit(solution)/shard_map/last_low_ahead/ppermute | solution.py:284
  74.4 12.8 %collective-permute-start.16 = (bf16[512,128]{1,0:T(8,128)(2,1)S(1)}, bf16[512,128]{1,0:T(8,128)(2,1)S(1)}, u32[]{:S(2)}, u32[]{:S(2)}) collective-permute-start(bf16[512,128]{1,0:T(8,128)(2,1)S(1)} %slice.72), channel_id=1, source_target_pairs={{4,0},{8,4},{12,8},{14,12},{10,14},{6,10},{2,6},{0,2},{5,1},{9,5},... | collective-permute-start | bytes 393224 | tf_op jit(solution)/shard_map/last_high_back/ppermute | solution.py:284

commit v5 on v4

--- a/solution.py
+++ b/solution.py
@@ -243,7 +243,7 @@
 
 def pack(flat, index):
     size, blk = flat.shape
-    half = jax.ShapeDtypeStruct((size // 2 + NOTE_ROWS, blk), jnp.bfloat16)
+    half = pltpu.VMEM((size // 2 + NOTE_ROWS, blk), jnp.bfloat16)
     return pl.pallas_call(
         pack_kernel,
         out_shape=(half, half),
@@ -318,7 +318,7 @@
     for k in range(1, whole_steps + 1):
         offsets, items = (n - k, k), [behind[k], beyond[k]]
         if k == 1:
-            offsets, items = (0, *offsets), [behind[0], *items]
+            offsets, items = (0, *offsets), [(behind[0][0], beyond[0][1]), *items]
         if k < whole_steps:
             advance()
         else:

time: 89 us -> 87.8 us (0.987)
  Pallas kernels: 27.2 us -> 25.8 us
  transfers between devices with their start and end apart: 18 -> 18, of which waited for: 12 -> 10; matrix products, arithmetic and copies ran while one was open for 6% -> 6% of each run, Pallas kernels for 29% -> 28%
where the time goes in v5:
time: 87.8 us; the launch traced here: 87.5 us
  waiting for transfers between devices  35.5 us (40%)
  Pallas kernels  25.8 us (29%)
  starting transfers between devices  19.1 us (22%)
  local copies, waits for them, and re-layouts  5.51 us (6%)
  other arithmetic  1.37 us (2%)
    ppermute x16, waiting for transfers between devices, move(): return lax.ppermute(array, 'row', way)  35.1 us
    ppermute x16, starting transfers between devices, move(): return lax.ppermute(array, 'row', way)  18.6 us
    pallas_call x3, Pallas kernels, product(): pl.pallas_call(functools.partial(product_kernel, offsets, sides, starts,...  15.2 us
    pallas_call x1, Pallas kernels, densify(): pl.pallas_call(densify_kernel, out_shape=jax.ShapeDtypeStruct((2 * pieces...  5.9 us
    pallas_call x2, Pallas kernels, finish(): pl.pallas_call(functools.partial(finish_kernel, parts, offset), out_shape...  3.47 us
    slice x1, local copies, waits for them, and re-layouts, body(): low_second, high_second = (flat[:cut], flat[cut:])  2.28 us
  transfers between devices with their start and end apart: 18, of which 10 were waited for; matrix products, arithmetic and copies ran while one was open for 6% of the time, Pallas kernels for 28%

profile of v5, /device:TPU:0, one launch (start us, length us, event | category | flops | bytes accessed | tf_op | source)
XLA Modules:
  0.0 87.5 jit_solution(15017759362306441765)
XLA Ops:
  0.5 1.2 %pack.1 = (bf16[2064,128]{1,0:T(8,128)(2,1)S(1)}, bf16[2064,128]{1,0:T(8,128)(2,1)S(1)}) custom-call(bf16[4096,128]{1,0:T(8,128)(2,1)} %bitcast.16, s32[2,16]{1,0:T(2,128)} %bitcast.14), custom_call_target="tpu_custom_call" | custom-call | tf_op jit(solution)/shard_map/pack/pallas_call | solution.py:247
  1.7 2.6 %collective-permute-start.2 = (bf16[2064,128]{1,0:T(8,128)(2,1)S(1)}, bf16[2064,128]{1,0:T(8,128)(2,1)}, u32[]{:S(2)}, u32[]{:S(2)}) collective-permute-start(bf16[2064,128]{1,0:T(8,128)(2,1)S(1)} %get-tuple-element.16.refs_5_), channel_id=1, source_target_pairs={{4,0},{8,4},{12,8},{14,12},{10,14},{6,10},{2,6},{0,2},{5,1},{9,5},... | collective-permute-start | bytes 1585160 | tf_op jit(solution)/shard_map/high_back/ppermute | solution.py:284
  4.4 2.3 %fusion.1 = (bf16[8,1,2,128,128]{4,3,2,1,0:T(8,128)(2,1)}, bf16[8,1,2,128,128]{4,3,2,1,0:T(8,128)(2,1)}) fusion(bf16[16,1,2,128,128]{4,3,2,1,0:T(8,128)(2,1)} %param.5), kind=kLoop, calls=%fused_computation.9 | loop fusion | bytes 2097152 | tf_op jit(solution)/shard_map/slice | solution.py:277
  6.7 2.0 %collective-permute-start.4 = (bf16[2048,128]{1,0:T(8,128)(2,1)}, bf16[2048,128]{1,0:T(8,128)(2,1)}, u32[]{:S(2)}, u32[]{:S(2)}) collective-permute-start(bf16[2048,128]{1,0:T(8,128)(2,1)} %bitcast.5), channel_id=1, source_target_pairs={{0,4},{4,8},{8,12},{12,14},{14,10},{10,6},{6,2},{2,0},{1,5},{5,9},... | collective-permute-start | bytes 1572872 | tf_op jit(solution)/shard_map/high_ahead/ppermute | solution.py:284
  8.7 10.5 %collective-permute-done.refs_6_ = bf16[2064,128]{1,0:T(8,128)(2,1)} collective-permute-done((bf16[2064,128]{1,0:T(8,128)(2,1)S(1)}, bf16[2064,128]{1,0:T(8,128)(2,1)}, u32[]{:S(2)}, u32[]{:S(2)}) %collective-permute-start) | collective-permute-done | bytes 528416 | tf_op jit(solution)/shard_map/low_ahead/ppermute | solution.py:284
  19.3 1.9 %collective-permute-start.3 = (bf16[2064,128]{1,0:T(8,128)(2,1)}, bf16[2064,128]{1,0:T(8,128)(2,1)S(1)}, u32[]{:S(2)}, u32[]{:S(2)}) collective-permute-start(bf16[2064,128]{1,0:T(8,128)(2,1)} %collective-permute-done.2.refs_9_), channel_id=1, source_target_pairs={{4,0},{8,4},{12,8},{14,12},{10,14},{6,10},{2,6},{0,2},{5,1},{9,5},... | collective-permute-start | bytes 1585160 | tf_op jit(solution)/shard_map/high_back/ppermute | solution.py:284
  22.0 8.5 %collective-permute-done.4.refs_7_ = bf16[2048,128]{1,0:T(8,128)(2,1)} collective-permute-done((bf16[2048,128]{1,0:T(8,128)(2,1)}, bf16[2048,128]{1,0:T(8,128)(2,1)}, u32[]{:S(2)}, u32[]{:S(2)}) %collective-permute-start.4) | collective-permute-done | bytes 524320 | tf_op jit(solution)/shard_map/high_ahead/ppermute | solution.py:284
  30.6 1.9 %collective-permute-start.11 = (bf16[2048,128]{1,0:T(8,128)(2,1)}, bf16[2048,128]{1,0:T(8,128)(2,1)}, u32[]{:S(2)}, u32[]{:S(2)}) collective-permute-start(bf16[2048,128]{1,0:T(8,128)(2,1)} %collective-permute-done.5.refs_8_), channel_id=1, source_target_pairs={{4,0},{8,4},{12,8},{14,12},{10,14},{6,10},{2,6},{0,2},{5,1},{9,5},... | collective-permute-start | bytes 1572872 | tf_op jit(solution)/shard_map/low_back/ppermute | solution.py:284
  35.2 1.6 %copy-done = bf16[16,1,4,128,128]{4,3,2,1,0:T(8,128)(2,1)S(1)} copy-done((bf16[16,1,4,128,128]{4,3,2,1,0:T(8,128)(2,1)S(1)}, bf16[16,1,4,128,128]{4,3,2,1,0:T(8,128)(2,1)}, u32[]{:S(2)}) %copy-start) | copy-done | bytes 2097176
  36.8 5.9 %densify.1.refs_10_.refs_11_.refs_12_.refs_7_.refs_8_.right = bf16[8,4,128,1024]{3,2,1,0:T(8,128)(2,1)S(1)} custom-call(s32[1]{0:T(128)} %bitcast.7.col_ref, s32[64]{0:T(128)S(1)} %reshape.9.own_index, s32[64]{0:T(128)S(1)} %collective-permute-done.7.other_index, bf16[16,4,128,128]{3,2,1,0:T(8,128)(2,1)S(1)} %bitcast.13, ...), custom_call_target="tpu_custom_call" | custom-call | tf_op jit(solution)/shard_map/densify/pallas_call | solution.py:44
  42.8 6.3 %product.3.refs_9_ = f32[16,128,1024]{2,1,0:T(8,128)S(1)} custom-call(s32[8]{0:T(128)S(1)} %get-tuple-element.27.refs_0_, s32[2,16]{1,0:T(2,128)S(1)} %bitcast.15, s32[2,16]{1,0:T(2,128)S(1)} %slice_convert_fusion.2.refs_2_, s32[2,16]{1,0:T(2,128)S(1)} %slice_convert_fusion.1.refs_3_, bf16[2064,128]{1,0:T(8,128)(2,1)S(1)} %copy-done.2, ...), custom_call_target="tpu_custom_call" | custom-call | tf_op jit(solution)/shard_map/product/pallas_call | solution.py:148
  49.2 1.9 %collective-permute-start.9 = (bf16[2064,128]{1,0:T(8,128)(2,1)S(1)}, bf16[2064,128]{1,0:T(8,128)(2,1)S(1)}, u32[]{:S(2)}, u32[]{:S(2)}) collective-permute-start(bf16[2064,128]{1,0:T(8,128)(2,1)S(1)} %collective-permute-done.3.refs_6_), channel_id=1, source_target_pairs={{4,0},{8,4},{12,8},{14,12},{10,14},{6,10},{2,6},{0,2},{5,1},{9,5},... | collective-permute-start | bytes 1585160 | tf_op jit(solution)/shard_map/high_back/ppermute | solution.py:284
  51.1 1.5 %collective-permute-done.10.refs_4_ = bf16[2048,128]{1,0:T(8,128)(2,1)} collective-permute-done((bf16[2048,128]{1,0:T(8,128)(2,1)}, bf16[2048,128]{1,0:T(8,128)(2,1)}, u32[]{:S(2)}, u32[]{:S(2)}) %collective-permute-start.10) | collective-permute-done | bytes 524320 | tf_op jit(solution)/shard_map/high_ahead/ppermute | solution.py:284
  53.1 1.5 %collective-permute-start.14 = (bf16[2048,128]{1,0:T(8,128)(2,1)}, bf16[2048,128]{1,0:T(8,128)(2,1)S(1)}, u32[]{:S(2)}, u32[]{:S(2)}) collective-permute-start(bf16[2048,128]{1,0:T(8,128)(2,1)} %collective-permute-done.11.refs_5_), channel_id=1, source_target_pairs={{4,0},{8,4},{12,8},{14,12},{10,14},{6,10},{2,6},{0,2},{5,1},{9,5},... | collective-permute-start | bytes 1572872 | tf_op jit(solution)/shard_map/low_back/ppermute | solution.py:284
  54.6 5.1 %product.4.refs_9_ = f32[16,128,1024]{2,1,0:T(8,128)S(1)} custom-call(s32[8]{0:T(128)S(1)} %get-tuple-element.27.refs_0_, s32[2,16]{1,0:T(2,128)S(1)} %get-tuple-element.30.refs_1_, s32[2,16]{1,0:T(2,128)S(1)} %get-tuple-element.29.refs_2_, bf16[2064,128]{1,0:T(8,128)(2,1)S(1)} %collective-permute-done.1.refs_3_, ...), custom_call_target="tpu_custom_call", output_to_operand_aliasing={{}: (9, {})} | custom-call | tf_op jit(solution)/shard_map/product/pallas_call | solution.py:148
  59.7 4.3 %collective-permute-done.8.refs_3_ = bf16[2064,128]{1,0:T(8,128)(2,1)S(1)} collective-permute-done((bf16[2064,128]{1,0:T(8,128)(2,1)S(1)}, bf16[2064,128]{1,0:T(8,128)(2,1)S(1)}, u32[]{:S(2)}, u32[]{:S(2)}) %collective-permute-start.8) | collective-permute-done | bytes 528416 | tf_op jit(solution)/shard_map/low_ahead/ppermute | solution.py:284
  64.2 2.1 %collective-permute-start.12 = (bf16[1552,128]{1,0:T(8,128)(2,1)S(1)}, bf16[1552,128]{1,0:T(8,128)(2,1)S(1)}, u32[]{:S(2)}, u32[]{:S(2)}) collective-permute-start(bf16[1552,128]{1,0:T(8,128)(2,1)S(1)} %slice.67), channel_id=1, source_target_pairs={{0,4},{4,8},{8,12},{12,14},{14,10},{10,6},{6,2},{2,0},{1,5},{5,9},... | collective-permute-start | bytes 1191944 | tf_op jit(solution)/shard_map/far_low_ahead/ppermute | solution.py:284
  66.3 2.0 %collective-permute-start.15 = (bf16[512,128]{1,0:T(8,128)(2,1)S(1)}, bf16[512,128]{1,0:T(8,128)(2,1)S(1)}, u32[]{:S(2)}, u32[]{:S(2)}) collective-permute-start(bf16[512,128]{1,0:T(8,128)(2,1)S(1)} %slice.71), channel_id=1, source_target_pairs={{0,4},{4,8},{8,12},{12,14},{14,10},{10,6},{6,2},{2,0},{1,5},{5,9},... | collective-permute-start | bytes 393224 | tf_op jit(solution)/shard_map/last_low_ahead/ppermute | solution.py:284
  68.3 6.9 %collective-permute-done.13.refs_4_ = bf16[2048,128]{1,0:T(8,128)(2,1)S(1)} collective-permute-done((bf16[2048,128]{1,0:T(8,128)(2,1)}, bf16[2048,128]{1,0:T(8,128)(2,1)S(1)}, u32[]{:S(2)}, u32[]{:S(2)}) %collective-permute-start.13) | collective-permute-done | bytes 524320 | tf_op jit(solution)/shard_map/high_ahead/ppermute | solution.py:284
  75.2 1.6 %collective-permute-start.16 = (bf16[512,128]{1,0:T(8,128)(2,1)S(1)}, bf16[512,128]{1,0:T(8,128)(2,1)S(1)}, u32[]{:S(2)}, u32[]{:S(2)}) collective-permute-start(bf16[512,128]{1,0:T(8,128)(2,1)S(1)} %slice.72), channel_id=1, source_target_pairs={{4,0},{8,4},{12,8},{14,12},{10,14},{6,10},{2,6},{0,2},{5,1},{9,5},... | collective-permute-start | bytes 393224 | tf_op jit(solution)/shard_map/last_high_back/ppermute | solution.py:284
  76.8 3.9 %product.5.total = f32[16,128,1024]{2,1,0:T(8,128)S(1)} custom-call(s32[8]{0:T(128)S(1)} %get-tuple-element.27.refs_0_, s32[2,16]{1,0:T(2,128)S(1)} %slice_convert_fusion.4.refs_1_, s32[2,16]{1,0:T(2,128)S(1)} %slice_convert_fusion.3.refs_2_, bf16[2064,128]{1,0:T(8,128)(2,1)S(1)} %collective-permute-done.8.refs_3_, ...), custom_call_target="tpu_custom_call", output_to_operand_aliasing={{}: (9, {})} | custom-call | tf_op jit(solution)/shard_map/product/pallas_call | solution.py:148
  80.7 3.0 %collective-permute-done.12.refs_0_ = bf16[1552,128]{1,0:T(8,128)(2,1)S(1)} collective-permute-done((bf16[1552,128]{1,0:T(8,128)(2,1)S(1)}, bf16[1552,128]{1,0:T(8,128)(2,1)S(1)}, u32[]{:S(2)}, u32[]{:S(2)}) %collective-permute-start.12) | collective-permute-done | bytes 397344 | tf_op jit(solution)/shard_map/far_low_ahead/ppermute | solution.py:284
  83.8 2.1 %finish.2.refs_2_ = bf16[16,1,8,128,128]{4,3,2,1,0:T(8,128)(2,1)} custom-call(s32[1,8]{1,0:T(1,128)S(1)} %get-tuple-element.28.cycle_ref, s32[2,16]{1,0:T(2,128)S(1)} %slice_convert_fusion.index_ref, bf16[8,4,128,1024]{3,2,1,0:T(8,128)(2,1)S(1)} %densify.1.refs_10_.refs_11_.refs_12_.refs_7_.refs_8_.right, f32[16,128,1024]{2,1,0:T(8,128)S(1)} %product.5.total, ...), custom_call_target="tpu_custom_call" | custom-call | tf_op jit(solution)/shard_map/finish/pallas_call | solution.py:206
  86.1 1.4 %finish.3 = bf16[16,1,8,128,128]{4,3,2,1,0:T(8,128)(2,1)} custom-call(s32[1,8]{1,0:T(1,128)S(1)} %get-tuple-element.28.cycle_ref, s32[2,16]{1,0:T(2,128)S(1)} %slice_convert_fusion.index_ref, bf16[8,4,128,1024]{3,2,1,0:T(8,128)(2,1)S(1)} %densify.1.refs_10_.refs_11_.refs_12_.refs_7_.refs_8_.right, ...), custom_call_target="tpu_custom_call", output_to_operand_aliasing={{}: (6, {})} | custom-call | tf_op jit(solution)/shard_map/finish/pallas_call | solution.py:206
  (45 shorter events, 5.4 us)
Async XLA Ops:
  0.0 42.7 %copy-start.5 = (s32[16,1,2]{0,2,1:T(2,128)S(1)}, s32[16,1,2]{0,2,1:T(2,128)}, u32[]{:S(2)}) copy-start(s32[16,1,2]{0,2,1:T(2,128)} %param.6) | copy-start | bytes 388
  0.0 33.2 %collective-permute-start.6 = (bf16[16,4,128,128]{3,2,1,0:T(8,128)(2,1)}, bf16[16,4,128,128]{3,2,1,0:T(8,128)(2,1)S(1)}, u32[]{:S(2)}, u32[]{:S(2)}) collective-permute-start(bf16[16,4,128,128]{3,2,1,0:T(8,128)(2,1)} %bitcast.12), channel_id=1, source_target_pairs={{0,1},{1,0},{2,3},{3,2},{4,5},{5,4},{6,7},{7,6},{8,9},{9,8},{10,11... | collective-permute-start | bytes 6291464 | tf_op jit(solution)/shard_map/ppermute | solution.py:299
  1.7 7.0 %copy-start.1 = (bf16[2064,128]{1,0:T(8,128)(2,1)}, bf16[2064,128]{1,0:T(8,128)(2,1)S(1)}, u32[]{:S(2)}) copy-start(bf16[2064,128]{1,0:T(8,128)(2,1)S(1)} %get-tuple-element.15.refs_4_) | copy-start | bytes 1585156
  1.7 17.6 %copy-start.3 = (bf16[2064,128]{1,0:T(8,128)(2,1)}, bf16[2064,128]{1,0:T(8,128)(2,1)S(1)}, u32[]{:S(2)}) copy-start(bf16[2064,128]{1,0:T(8,128)(2,1)S(1)} %get-tuple-element.16.refs_5_) | copy-start | bytes 1585156
  1.7 17.6 %collective-permute-start.2 = (bf16[2064,128]{1,0:T(8,128)(2,1)S(1)}, bf16[2064,128]{1,0:T(8,128)(2,1)}, u32[]{:S(2)}, u32[]{:S(2)}) collective-permute-start(bf16[2064,128]{1,0:T(8,128)(2,1)S(1)} %get-tuple-element.16.refs_5_), channel_id=1, source_target_pairs={{4,0},{8,4},{12,8},{14,12},{10,14},{6,10},{2,6},{0,2},{5,1},{9,5},... | collective-permute-start | bytes 1585160 | tf_op jit(solution)/shard_map/high_back/ppermute | solution.py:284
  4.3 15.0 %collective-permute-start = (bf16[2064,128]{1,0:T(8,128)(2,1)S(1)}, bf16[2064,128]{1,0:T(8,128)(2,1)}, u32[]{:S(2)}, u32[]{:S(2)}) collective-permute-start(bf16[2064,128]{1,0:T(8,128)(2,1)S(1)} %get-tuple-element.15.refs_4_), channel_id=1, source_target_pairs={{0,4},{4,8},{8,12},{12,14},{14,10},{10,6},{6,2},{2,0},{1,5},{5,9},... | collective-permute-start | bytes 1585160 | tf_op jit(solution)/shard_map/low_ahead/ppermute | solution.py:284
  6.7 23.8 %collective-permute-start.4 = (bf16[2048,128]{1,0:T(8,128)(2,1)}, bf16[2048,128]{1,0:T(8,128)(2,1)}, u32[]{:S(2)}, u32[]{:S(2)}) collective-permute-start(bf16[2048,128]{1,0:T(8,128)(2,1)} %bitcast.5), channel_id=1, source_target_pairs={{0,4},{4,8},{8,12},{12,14},{14,10},{10,6},{6,2},{2,0},{1,5},{5,9},... | collective-permute-start | bytes 1572872 | tf_op jit(solution)/shard_map/high_ahead/ppermute | solution.py:284
  8.7 21.9 %collective-permute-start.5 = (bf16[2048,128]{1,0:T(8,128)(2,1)}, bf16[2048,128]{1,0:T(8,128)(2,1)}, u32[]{:S(2)}, u32[]{:S(2)}) collective-permute-start(bf16[2048,128]{1,0:T(8,128)(2,1)} %bitcast.6), channel_id=1, source_target_pairs={{4,0},{8,4},{12,8},{14,12},{10,14},{6,10},{2,6},{0,2},{5,1},{9,5},... | collective-permute-start | bytes 1572872 | tf_op jit(solution)/shard_map/low_back/ppermute | solution.py:284
  19.3 29.8 %collective-permute-start.1 = (bf16[2064,128]{1,0:T(8,128)(2,1)}, bf16[2064,128]{1,0:T(8,128)(2,1)S(1)}, u32[]{:S(2)}, u32[]{:S(2)}) collective-permute-start(bf16[2064,128]{1,0:T(8,128)(2,1)} %collective-permute-done.refs_6_), channel_id=1, source_target_pairs={{0,4},{4,8},{8,12},{12,14},{14,10},{10,6},{6,2},{2,0},{1,5},{5,9},... | collective-permute-start | bytes 1585160 | tf_op jit(solution)/shard_map/low_ahead/ppermute | solution.py:284
  19.3 29.7 %collective-permute-start.3 = (bf16[2064,128]{1,0:T(8,128)(2,1)}, bf16[2064,128]{1,0:T(8,128)(2,1)S(1)}, u32[]{:S(2)}, u32[]{:S(2)}) collective-permute-start(bf16[2064,128]{1,0:T(8,128)(2,1)} %collective-permute-done.2.refs_9_), channel_id=1, source_target_pairs={{4,0},{8,4},{12,8},{14,12},{10,14},{6,10},{2,6},{0,2},{5,1},{9,5},... | collective-permute-start | bytes 1585160 | tf_op jit(solution)/shard_map/high_back/ppermute | solution.py:284
  30.5 22.1 %collective-permute-start.10 = (bf16[2048,128]{1,0:T(8,128)(2,1)}, bf16[2048,128]{1,0:T(8,128)(2,1)}, u32[]{:S(2)}, u32[]{:S(2)}) collective-permute-start(bf16[2048,128]{1,0:T(8,128)(2,1)} %collective-permute-done.4.refs_7_), channel_id=1, source_target_pairs={{0,4},{4,8},{8,12},{12,14},{14,10},{10,6},{6,2},{2,0},{1,5},{5,9},... | collective-permute-start | bytes 1572872 | tf_op jit(solution)/shard_map/high_ahead/ppermute | solution.py:284
  30.6 22.6 %collective-permute-start.11 = (bf16[2048,128]{1,0:T(8,128)(2,1)}, bf16[2048,128]{1,0:T(8,128)(2,1)}, u32[]{:S(2)}, u32[]{:S(2)}) collective-permute-start(bf16[2048,128]{1,0:T(8,128)(2,1)} %collective-permute-done.5.refs_8_), channel_id=1, source_target_pairs={{4,0},{8,4},{12,8},{14,12},{10,14},{6,10},{2,6},{0,2},{5,1},{9,5},... | collective-permute-start | bytes 1572872 | tf_op jit(solution)/shard_map/low_back/ppermute | solution.py:284
  34.0 1.2 %collective-permute-start.7 = (s32[64]{0:T(128)S(1)}, s32[64]{0:T(128)S(1)}, u32[]{:S(2)}, u32[]{:S(2)}) collective-permute-start(s32[64]{0:T(128)S(1)} %reshape.9.own_index), channel_id=1, source_target_pairs={{0,1},{1,0},{2,3},{3,2},{4,5},{5,4},{6,7},{7,6},{8,9},{9,8},{10,11... | collective-permute-start | bytes 776 | tf_op jit(solution)/shard_map/ppermute | solution.py:301
  35.2 1.6 %copy-start = (bf16[16,1,4,128,128]{4,3,2,1,0:T(8,128)(2,1)S(1)}, bf16[16,1,4,128,128]{4,3,2,1,0:T(8,128)(2,1)}, u32[]{:S(2)}) copy-start(bf16[16,1,4,128,128]{4,3,2,1,0:T(8,128)(2,1)} %param.7) | copy-start | bytes 6291460
  36.8 5.9 %copy-start.2 = (bf16[2064,128]{1,0:T(8,128)(2,1)S(1)}, bf16[2064,128]{1,0:T(8,128)(2,1)}, u32[]{:S(2)}) copy-start(bf16[2064,128]{1,0:T(8,128)(2,1)} %copy-done.1) | copy-start | bytes 1585156
  36.8 5.9 %copy-start.4 = (bf16[2064,128]{1,0:T(8,128)(2,1)S(1)}, bf16[2064,128]{1,0:T(8,128)(2,1)}, u32[]{:S(2)}) copy-start(bf16[2064,128]{1,0:T(8,128)(2,1)} %copy-done.3) | copy-start | bytes 1585156
  49.1 14.9 %collective-permute-start.8 = (bf16[2064,128]{1,0:T(8,128)(2,1)S(1)}, bf16[2064,128]{1,0:T(8,128)(2,1)S(1)}, u32[]{:S(2)}, u32[]{:S(2)}) collective-permute-start(bf16[2064,128]{1,0:T(8,128)(2,1)S(1)} %collective-permute-done.1.refs_3_), channel_id=1, source_target_pairs={{0,4},{4,8},{8,12},{12,14},{14,10},{10,6},{6,2},{2,0},{1,5},{5,9},... | collective-permute-start | bytes 1585160 | tf_op jit(solution)/shard_map/low_ahead/ppermute | solution.py:284
  49.2 14.9 %collective-permute-start.9 = (bf16[2064,128]{1,0:T(8,128)(2,1)S(1)}, bf16[2064,128]{1,0:T(8,128)(2,1)S(1)}, u32[]{:S(2)}, u32[]{:S(2)}) collective-permute-start(bf16[2064,128]{1,0:T(8,128)(2,1)S(1)} %collective-permute-done.3.refs_6_), channel_id=1, source_target_pairs={{4,0},{8,4},{12,8},{14,12},{10,14},{6,10},{2,6},{0,2},{5,1},{9,5},... | collective-permute-start | bytes 1585160 | tf_op jit(solution)/shard_map/high_back/ppermute | solution.py:284
  52.6 22.6 %collective-permute-start.13 = (bf16[2048,128]{1,0:T(8,128)(2,1)}, bf16[2048,128]{1,0:T(8,128)(2,1)S(1)}, u32[]{:S(2)}, u32[]{:S(2)}) collective-permute-start(bf16[2048,128]{1,0:T(8,128)(2,1)} %collective-permute-done.10.refs_4_), channel_id=1, source_target_pairs={{0,4},{4,8},{8,12},{12,14},{14,10},{10,6},{6,2},{2,0},{1,5},{5,9},... | collective-permute-start | bytes 1572872 | tf_op jit(solution)/shard_map/high_ahead/ppermute | solution.py:284
  53.1 23.6 %collective-permute-start.14 = (bf16[2048,128]{1,0:T(8,128)(2,1)}, bf16[2048,128]{1,0:T(8,128)(2,1)S(1)}, u32[]{:S(2)}, u32[]{:S(2)}) collective-permute-start(bf16[2048,128]{1,0:T(8,128)(2,1)} %collective-permute-done.11.refs_5_), channel_id=1, source_target_pairs={{4,0},{8,4},{12,8},{14,12},{10,14},{6,10},{2,6},{0,2},{5,1},{9,5},... | collective-permute-start | bytes 1572872 | tf_op jit(solution)/shard_map/low_back/ppermute | solution.py:284
  64.2 19.6 %collective-permute-start.12 = (bf16[1552,128]{1,0:T(8,128)(2,1)S(1)}, bf16[1552,128]{1,0:T(8,128)(2,1)S(1)}, u32[]{:S(2)}, u32[]{:S(2)}) collective-permute-start(bf16[1552,128]{1,0:T(8,128)(2,1)S(1)} %slice.67), channel_id=1, source_target_pairs={{0,4},{4,8},{8,12},{12,14},{14,10},{10,6},{6,2},{2,0},{1,5},{5,9},... | collective-permute-start | bytes 1191944 | tf_op jit(solution)/shard_map/far_low_ahead/ppermute | solution.py:284
  66.2 17.6 %collective-permute-start.17 = (bf16[1552,128]{1,0:T(8,128)(2,1)S(1)}, bf16[1552,128]{1,0:T(8,128)(2,1)S(1)}, u32[]{:S(2)}, u32[]{:S(2)}) collective-permute-start(bf16[1552,128]{1,0:T(8,128)(2,1)S(1)} %slice.73), channel_id=1, source_target_pairs={{4,0},{8,4},{12,8},{14,12},{10,14},{6,10},{2,6},{0,2},{5,1},{9,5},... | collective-permute-start | bytes 1191944 | tf_op jit(solution)/shard_map/far_high_back/ppermute | solution.py:284
  66.3 19.9 %collective-permute-start.15 = (bf16[512,128]{1,0:T(8,128)(2,1)S(1)}, bf16[512,128]{1,0:T(8,128)(2,1)S(1)}, u32[]{:S(2)}, u32[]{:S(2)}) collective-permute-start(bf16[512,128]{1,0:T(8,128)(2,1)S(1)} %slice.71), channel_id=1, source_target_pairs={{0,4},{4,8},{8,12},{12,14},{14,10},{10,6},{6,2},{2,0},{1,5},{5,9},... | collective-permute-start | bytes 393224 | tf_op jit(solution)/shard_map/last_low_ahead/ppermute | solution.py:284
  75.2 10.9 %collective-permute-start.16 = (bf16[512,128]{1,0:T(8,128)(2,1)S(1)}, bf16[512,128]{1,0:T(8,128)(2,1)S(1)}, u32[]{:S(2)}, u32[]{:S(2)}) collective-permute-start(bf16[512,128]{1,0:T(8,128)(2,1)S(1)} %slice.72), channel_id=1, source_target_pairs={{4,0},{8,4},{12,8},{14,12},{10,14},{6,10},{2,6},{0,2},{5,1},{9,5},... | collective-permute-start | bytes 393224 | tf_op jit(solution)/shard_map/last_high_back/ppermute | solution.py:284

commit v6 on v5

--- a/solution.py
+++ b/solution.py
@@ -322,34 +322,32 @@
         if k < whole_steps:
             advance()
         else:
-            small = half // 4
-            at = small * slots * blk
+            per_row = slots * blk
+            small, other_small = half // 4, 3 * half // 8
             low, high = behind[-1][0], beyond[-1][1]
-            large_parts = (
-                small,
-                half - small,
-                move(low[at:], ahead, "far_low_ahead"),
-                move(high[at:], back, "far_high_back"),
-            )
+            large_low = move(low[small * per_row :], ahead, "far_low_ahead")
+            large_high = move(high[other_small * per_row : cut], back, "far_high_back")
         index = [read_note(behind[k][0]), read_note(beyond[k][1])]
         if k == 1:
             index.insert(0, own_index)
         total = product(cycle, offsets, index, items, right, total, (0, half), half, rows)
         if k < whole_steps:
             total = after(total)
-    low, high = behind[-1][0][:at], beyond[-1][1][:at]
-    small_parts = (0, small, move(low, ahead, "last_low_ahead"), move(high, back, "last_high_back"))
-    last_parts = [large_parts, small_parts]
-    out = None
-    far_index = read_note(last_parts[0][2])
-    per_row = slots * blk
-    for start, size, low, high in last_parts:
-        parts = [
-            (h * half + start + i, [(h, i * per_row + s * blk) for s in range(slots)])
-            for h in range(2)
-            for i in range(size)
+    low, high = behind[-1][0][: small * per_row], beyond[-1][1][: other_small * per_row]
+    small_low, small_high = move(low, ahead, "last_low_ahead"), move(high, back, "last_high_back")
+
+    def blocks(array, first, stop, origin):
+        return [
+            (row, [(array, (row - origin) * per_row + s * blk) for s in range(slots)])
+            for row in range(first, stop)
         ]
-        out = finish(parts, cycle, n // 2, far_index, right, total, [low, high], out)
+
+    far, far_index = n // 2, read_note(large_low)
+    split = half + other_small
+    parts = blocks(0, small, half, small) + blocks(1, split, rows, split)
+    out = finish(parts, cycle, far, far_index, right, total, [large_low, large_high], None)
+    parts = blocks(0, 0, small, 0) + blocks(1, half, split, half)
+    out = finish(parts, cycle, far, far_index, right, total, [small_low, small_high], out)
     return out
 
 

time: 87.8 us -> 87.9 us (level)
  starting transfers between devices: 19.1 us -> 17.9 us
  waiting for transfers between devices: 35.5 us -> 36.7 us
    ppermute x16, waiting for transfers between devices: 35.1 us -> 36.3 us  [move(): return lax.ppermute(array, 'row', way)]
    ppermute x16, starting transfers between devices: 18.6 us -> 17.4 us  [move(): return lax.ppermute(array, 'row', way)]
  transfers between devices with their start and end apart: 18 -> 18, of which waited for: 10 -> 9; matrix products, arithmetic and copies ran while one was open for 6% -> 6% of each run, Pallas kernels for 28% -> 28%
where the time goes in v6:
time: 87.9 us; the launch traced here: 87.6 us
  waiting for transfers between devices  36.7 us (42%)
  Pallas kernels  25.9 us (29%)
  starting transfers between devices  17.9 us (20%)
  local copies, waits for them, and re-layouts  5.51 us (6%)
  other arithmetic  1.37 us (2%)
    ppermute x16, waiting for transfers between devices, move(): return lax.ppermute(array, 'row', way)  36.3 us
    ppermute x16, starting transfers between devices, move(): return lax.ppermute(array, 'row', way)  17.4 us
    pallas_call x3, Pallas kernels, product(): pl.pallas_call(functools.partial(product_kernel, offsets, sides, starts,...  15.2 us
    pallas_call x1, Pallas kernels, densify(): pl.pallas_call(densify_kernel, out_shape=jax.ShapeDtypeStruct((2 * pieces...  5.9 us
    pallas_call x2, Pallas kernels, finish(): pl.pallas_call(functools.partial(finish_kernel, parts, offset), out_shape...  3.47 us
    slice x1, local copies, waits for them, and re-layouts, body(): low_second, high_second = (flat[:cut], flat[cut:])  2.28 us
  transfers between devices with their start and end apart: 18, of which 9 were waited for; matrix products, arithmetic and copies ran while one was open for 6% of the time, Pallas kernels for 28%

profile of v6, /device:TPU:0, one launch (start us, length us, event | category | flops | bytes accessed | tf_op | source)
XLA Modules:
  0.0 87.6 jit_solution(4932557760152935964)
XLA Ops:
  0.5 1.2 %pack.1 = (bf16[2064,128]{1,0:T(8,128)(2,1)S(1)}, bf16[2064,128]{1,0:T(8,128)(2,1)S(1)}) custom-call(bf16[4096,128]{1,0:T(8,128)(2,1)} %bitcast.16, s32[2,16]{1,0:T(2,128)} %bitcast.14), custom_call_target="tpu_custom_call" | custom-call | tf_op jit(solution)/shard_map/pack/pallas_call | solution.py:247
  1.7 2.6 %collective-permute-start.2 = (bf16[2064,128]{1,0:T(8,128)(2,1)S(1)}, bf16[2064,128]{1,0:T(8,128)(2,1)}, u32[]{:S(2)}, u32[]{:S(2)}) collective-permute-start(bf16[2064,128]{1,0:T(8,128)(2,1)S(1)} %get-tuple-element.16.refs_5_), channel_id=1, source_target_pairs={{4,0},{8,4},{12,8},{14,12},{10,14},{6,10},{2,6},{0,2},{5,1},{9,5},... | collective-permute-start | bytes 1585160 | tf_op jit(solution)/shard_map/high_back/ppermute | solution.py:284
  4.4 2.3 %fusion.1 = (bf16[8,1,2,128,128]{4,3,2,1,0:T(8,128)(2,1)}, bf16[8,1,2,128,128]{4,3,2,1,0:T(8,128)(2,1)}) fusion(bf16[16,1,2,128,128]{4,3,2,1,0:T(8,128)(2,1)} %param.5), kind=kLoop, calls=%fused_computation.9 | loop fusion | bytes 2097152 | tf_op jit(solution)/shard_map/slice | solution.py:277
  6.7 2.0 %collective-permute-start.4 = (bf16[2048,128]{1,0:T(8,128)(2,1)}, bf16[2048,128]{1,0:T(8,128)(2,1)}, u32[]{:S(2)}, u32[]{:S(2)}) collective-permute-start(bf16[2048,128]{1,0:T(8,128)(2,1)} %bitcast.5), channel_id=1, source_target_pairs={{0,4},{4,8},{8,12},{12,14},{14,10},{10,6},{6,2},{2,0},{1,5},{5,9},... | collective-permute-start | bytes 1572872 | tf_op jit(solution)/shard_map/high_ahead/ppermute | solution.py:284
  8.7 10.5 %collective-permute-done.refs_6_ = bf16[2064,128]{1,0:T(8,128)(2,1)} collective-permute-done((bf16[2064,128]{1,0:T(8,128)(2,1)S(1)}, bf16[2064,128]{1,0:T(8,128)(2,1)}, u32[]{:S(2)}, u32[]{:S(2)}) %collective-permute-start) | collective-permute-done | bytes 528416 | tf_op jit(solution)/shard_map/low_ahead/ppermute | solution.py:284
  19.3 1.9 %collective-permute-start.3 = (bf16[2064,128]{1,0:T(8,128)(2,1)}, bf16[2064,128]{1,0:T(8,128)(2,1)S(1)}, u32[]{:S(2)}, u32[]{:S(2)}) collective-permute-start(bf16[2064,128]{1,0:T(8,128)(2,1)} %collective-permute-done.2.refs_9_), channel_id=1, source_target_pairs={{4,0},{8,4},{12,8},{14,12},{10,14},{6,10},{2,6},{0,2},{5,1},{9,5},... | collective-permute-start | bytes 1585160 | tf_op jit(solution)/shard_map/high_back/ppermute | solution.py:284
  22.0 8.5 %collective-permute-done.4.refs_7_ = bf16[2048,128]{1,0:T(8,128)(2,1)} collective-permute-done((bf16[2048,128]{1,0:T(8,128)(2,1)}, bf16[2048,128]{1,0:T(8,128)(2,1)}, u32[]{:S(2)}, u32[]{:S(2)}) %collective-permute-start.4) | collective-permute-done | bytes 524320 | tf_op jit(solution)/shard_map/high_ahead/ppermute | solution.py:284
  30.6 1.9 %collective-permute-start.11 = (bf16[2048,128]{1,0:T(8,128)(2,1)}, bf16[2048,128]{1,0:T(8,128)(2,1)}, u32[]{:S(2)}, u32[]{:S(2)}) collective-permute-start(bf16[2048,128]{1,0:T(8,128)(2,1)} %collective-permute-done.5.refs_8_), channel_id=1, source_target_pairs={{4,0},{8,4},{12,8},{14,12},{10,14},{6,10},{2,6},{0,2},{5,1},{9,5},... | collective-permute-start | bytes 1572872 | tf_op jit(solution)/shard_map/low_back/ppermute | solution.py:284
  33.2 0.8 copy.10
  35.2 1.6 %copy-done = bf16[16,1,4,128,128]{4,3,2,1,0:T(8,128)(2,1)S(1)} copy-done((bf16[16,1,4,128,128]{4,3,2,1,0:T(8,128)(2,1)S(1)}, bf16[16,1,4,128,128]{4,3,2,1,0:T(8,128)(2,1)}, u32[]{:S(2)}) %copy-start) | copy-done | bytes 2097176
  36.8 5.9 %densify.1.refs_10_.refs_11_.refs_12_.refs_7_.refs_8_.right = bf16[8,4,128,1024]{3,2,1,0:T(8,128)(2,1)S(1)} custom-call(s32[1]{0:T(128)} %bitcast.7.col_ref, s32[64]{0:T(128)S(1)} %reshape.9.own_index, s32[64]{0:T(128)S(1)} %collective-permute-done.7.other_index, bf16[16,4,128,128]{3,2,1,0:T(8,128)(2,1)S(1)} %bitcast.13, ...), custom_call_target="tpu_custom_call" | custom-call | tf_op jit(solution)/shard_map/densify/pallas_call | solution.py:44
  42.8 6.3 %product.3.refs_9_ = f32[16,128,1024]{2,1,0:T(8,128)S(1)} custom-call(s32[8]{0:T(128)S(1)} %get-tuple-element.27.refs_0_, s32[2,16]{1,0:T(2,128)S(1)} %bitcast.15, s32[2,16]{1,0:T(2,128)S(1)} %slice_convert_fusion.2.refs_2_, s32[2,16]{1,0:T(2,128)S(1)} %slice_convert_fusion.1.refs_3_, bf16[2064,128]{1,0:T(8,128)(2,1)S(1)} %copy-done.2, ...), custom_call_target="tpu_custom_call" | custom-call | tf_op jit(solution)/shard_map/product/pallas_call | solution.py:148
  49.2 1.9 %collective-permute-start.9 = (bf16[2064,128]{1,0:T(8,128)(2,1)S(1)}, bf16[2064,128]{1,0:T(8,128)(2,1)S(1)}, u32[]{:S(2)}, u32[]{:S(2)}) collective-permute-start(bf16[2064,128]{1,0:T(8,128)(2,1)S(1)} %collective-permute-done.3.refs_6_), channel_id=1, source_target_pairs={{4,0},{8,4},{12,8},{14,12},{10,14},{6,10},{2,6},{0,2},{5,1},{9,5},... | collective-permute-start | bytes 1585160 | tf_op jit(solution)/shard_map/high_back/ppermute | solution.py:284
  51.1 1.5 %collective-permute-done.10.refs_4_ = bf16[2048,128]{1,0:T(8,128)(2,1)} collective-permute-done((bf16[2048,128]{1,0:T(8,128)(2,1)}, bf16[2048,128]{1,0:T(8,128)(2,1)}, u32[]{:S(2)}, u32[]{:S(2)}) %collective-permute-start.10) | collective-permute-done | bytes 524320 | tf_op jit(solution)/shard_map/high_ahead/ppermute | solution.py:284
  53.1 1.5 %collective-permute-start.14 = (bf16[2048,128]{1,0:T(8,128)(2,1)}, bf16[2048,128]{1,0:T(8,128)(2,1)S(1)}, u32[]{:S(2)}, u32[]{:S(2)}) collective-permute-start(bf16[2048,128]{1,0:T(8,128)(2,1)} %collective-permute-done.11.refs_5_), channel_id=1, source_target_pairs={{4,0},{8,4},{12,8},{14,12},{10,14},{6,10},{2,6},{0,2},{5,1},{9,5},... | collective-permute-start | bytes 1572872 | tf_op jit(solution)/shard_map/low_back/ppermute | solution.py:284
  54.6 5.1 %product.4.refs_9_ = f32[16,128,1024]{2,1,0:T(8,128)S(1)} custom-call(s32[8]{0:T(128)S(1)} %get-tuple-element.27.refs_0_, s32[2,16]{1,0:T(2,128)S(1)} %get-tuple-element.30.refs_1_, s32[2,16]{1,0:T(2,128)S(1)} %get-tuple-element.29.refs_2_, bf16[2064,128]{1,0:T(8,128)(2,1)S(1)} %collective-permute-done.1.refs_3_, ...), custom_call_target="tpu_custom_call", output_to_operand_aliasing={{}: (9, {})} | custom-call | tf_op jit(solution)/shard_map/product/pallas_call | solution.py:148
  59.7 4.3 %collective-permute-done.8.refs_3_ = bf16[2064,128]{1,0:T(8,128)(2,1)S(1)} collective-permute-done((bf16[2064,128]{1,0:T(8,128)(2,1)S(1)}, bf16[2064,128]{1,0:T(8,128)(2,1)S(1)}, u32[]{:S(2)}, u32[]{:S(2)}) %collective-permute-start.8) | collective-permute-done | bytes 528416 | tf_op jit(solution)/shard_map/low_ahead/ppermute | solution.py:284
  64.1 2.1 %collective-permute-start.12 = (bf16[1552,128]{1,0:T(8,128)(2,1)S(1)}, bf16[1552,128]{1,0:T(8,128)(2,1)S(1)}, u32[]{:S(2)}, u32[]{:S(2)}) collective-permute-start(bf16[1552,128]{1,0:T(8,128)(2,1)S(1)} %slice.67), channel_id=1, source_target_pairs={{0,4},{4,8},{8,12},{12,14},{14,10},{10,6},{6,2},{2,0},{1,5},{5,9},... | collective-permute-start | bytes 1191944 | tf_op jit(solution)/shard_map/far_low_ahead/ppermute | solution.py:284
  66.3 2.0 %collective-permute-start.16 = (bf16[768,128]{1,0:T(8,128)(2,1)S(1)}, bf16[768,128]{1,0:T(8,128)(2,1)S(1)}, u32[]{:S(2)}, u32[]{:S(2)}) collective-permute-start(bf16[768,128]{1,0:T(8,128)(2,1)S(1)} %slice.72), channel_id=1, source_target_pairs={{4,0},{8,4},{12,8},{14,12},{10,14},{6,10},{2,6},{0,2},{5,1},{9,5},... | collective-permute-start | bytes 589832 | tf_op jit(solution)/shard_map/last_high_back/ppermute | solution.py:284
  68.3 6.9 %collective-permute-done.13.refs_4_ = bf16[2048,128]{1,0:T(8,128)(2,1)S(1)} collective-permute-done((bf16[2048,128]{1,0:T(8,128)(2,1)}, bf16[2048,128]{1,0:T(8,128)(2,1)S(1)}, u32[]{:S(2)}, u32[]{:S(2)}) %collective-permute-start.13) | collective-permute-done | bytes 524320 | tf_op jit(solution)/shard_map/high_ahead/ppermute | solution.py:284
  75.6 3.9 %product.5.total = f32[16,128,1024]{2,1,0:T(8,128)S(1)} custom-call(s32[8]{0:T(128)S(1)} %get-tuple-element.27.refs_0_, s32[2,16]{1,0:T(2,128)S(1)} %slice_convert_fusion.4.refs_1_, s32[2,16]{1,0:T(2,128)S(1)} %slice_convert_fusion.3.refs_2_, bf16[2064,128]{1,0:T(8,128)(2,1)S(1)} %collective-permute-done.8.refs_3_, ...), custom_call_target="tpu_custom_call", output_to_operand_aliasing={{}: (9, {})} | custom-call | tf_op jit(solution)/shard_map/product/pallas_call | solution.py:148
  79.5 4.2 %collective-permute-done.12.refs_0_ = bf16[1552,128]{1,0:T(8,128)(2,1)S(1)} collective-permute-done((bf16[1552,128]{1,0:T(8,128)(2,1)S(1)}, bf16[1552,128]{1,0:T(8,128)(2,1)S(1)}, u32[]{:S(2)}, u32[]{:S(2)}) %collective-permute-start.12) | collective-permute-done | bytes 397344 | tf_op jit(solution)/shard_map/far_low_ahead/ppermute | solution.py:284
  83.7 2.0 %finish.2.refs_2_ = bf16[16,1,8,128,128]{4,3,2,1,0:T(8,128)(2,1)} custom-call(s32[1,8]{1,0:T(1,128)S(1)} %get-tuple-element.28.cycle_ref, s32[2,16]{1,0:T(2,128)S(1)} %slice_convert_fusion.index_ref, bf16[8,4,128,1024]{3,2,1,0:T(8,128)(2,1)S(1)} %densify.1.refs_10_.refs_11_.refs_12_.refs_7_.refs_8_.right, f32[16,128,1024]{2,1,0:T(8,128)S(1)} %product.5.total, ...), custom_call_target="tpu_custom_call" | custom-call | tf_op jit(solution)/shard_map/finish/pallas_call | solution.py:206
  86.1 1.4 %finish.3 = bf16[16,1,8,128,128]{4,3,2,1,0:T(8,128)(2,1)} custom-call(s32[1,8]{1,0:T(1,128)S(1)} %get-tuple-element.28.cycle_ref, s32[2,16]{1,0:T(2,128)S(1)} %slice_convert_fusion.index_ref, bf16[8,4,128,1024]{3,2,1,0:T(8,128)(2,1)S(1)} %densify.1.refs_10_.refs_11_.refs_12_.refs_7_.refs_8_.right, ...), custom_call_target="tpu_custom_call", output_to_operand_aliasing={{}: (6, {})} | custom-call | tf_op jit(solution)/shard_map/finish/pallas_call | solution.py:206
  (45 shorter events, 5.2 us)
Async XLA Ops:
  0.0 42.7 %copy-start.5 = (s32[16,1,2]{0,2,1:T(2,128)S(1)}, s32[16,1,2]{0,2,1:T(2,128)}, u32[]{:S(2)}) copy-start(s32[16,1,2]{0,2,1:T(2,128)} %param.6) | copy-start | bytes 388
  0.0 33.2 %collective-permute-start.6 = (bf16[16,4,128,128]{3,2,1,0:T(8,128)(2,1)}, bf16[16,4,128,128]{3,2,1,0:T(8,128)(2,1)S(1)}, u32[]{:S(2)}, u32[]{:S(2)}) collective-permute-start(bf16[16,4,128,128]{3,2,1,0:T(8,128)(2,1)} %bitcast.12), channel_id=1, source_target_pairs={{0,1},{1,0},{2,3},{3,2},{4,5},{5,4},{6,7},{7,6},{8,9},{9,8},{10,11... | collective-permute-start | bytes 6291464 | tf_op jit(solution)/shard_map/ppermute | solution.py:299
  1.7 7.0 %copy-start.1 = (bf16[2064,128]{1,0:T(8,128)(2,1)}, bf16[2064,128]{1,0:T(8,128)(2,1)S(1)}, u32[]{:S(2)}) copy-start(bf16[2064,128]{1,0:T(8,128)(2,1)S(1)} %get-tuple-element.15.refs_4_) | copy-start | bytes 1585156
  1.7 17.6 %copy-start.3 = (bf16[2064,128]{1,0:T(8,128)(2,1)}, bf16[2064,128]{1,0:T(8,128)(2,1)S(1)}, u32[]{:S(2)}) copy-start(bf16[2064,128]{1,0:T(8,128)(2,1)S(1)} %get-tuple-element.16.refs_5_) | copy-start | bytes 1585156
  1.7 17.6 %collective-permute-start.2 = (bf16[2064,128]{1,0:T(8,128)(2,1)S(1)}, bf16[2064,128]{1,0:T(8,128)(2,1)}, u32[]{:S(2)}, u32[]{:S(2)}) collective-permute-start(bf16[2064,128]{1,0:T(8,128)(2,1)S(1)} %get-tuple-element.16.refs_5_), channel_id=1, source_target_pairs={{4,0},{8,4},{12,8},{14,12},{10,14},{6,10},{2,6},{0,2},{5,1},{9,5},... | collective-permute-start | bytes 1585160 | tf_op jit(solution)/shard_map/high_back/ppermute | solution.py:284
  4.3 15.0 %collective-permute-start = (bf16[2064,128]{1,0:T(8,128)(2,1)S(1)}, bf16[2064,128]{1,0:T(8,128)(2,1)}, u32[]{:S(2)}, u32[]{:S(2)}) collective-permute-start(bf16[2064,128]{1,0:T(8,128)(2,1)S(1)} %get-tuple-element.15.refs_4_), channel_id=1, source_target_pairs={{0,4},{4,8},{8,12},{12,14},{14,10},{10,6},{6,2},{2,0},{1,5},{5,9},... | collective-permute-start | bytes 1585160 | tf_op jit(solution)/shard_map/low_ahead/ppermute | solution.py:284
  6.7 23.8 %collective-permute-start.4 = (bf16[2048,128]{1,0:T(8,128)(2,1)}, bf16[2048,128]{1,0:T(8,128)(2,1)}, u32[]{:S(2)}, u32[]{:S(2)}) collective-permute-start(bf16[2048,128]{1,0:T(8,128)(2,1)} %bitcast.5), channel_id=1, source_target_pairs={{0,4},{4,8},{8,12},{12,14},{14,10},{10,6},{6,2},{2,0},{1,5},{5,9},... | collective-permute-start | bytes 1572872 | tf_op jit(solution)/shard_map/high_ahead/ppermute | solution.py:284
  8.7 21.9 %collective-permute-start.5 = (bf16[2048,128]{1,0:T(8,128)(2,1)}, bf16[2048,128]{1,0:T(8,128)(2,1)}, u32[]{:S(2)}, u32[]{:S(2)}) collective-permute-start(bf16[2048,128]{1,0:T(8,128)(2,1)} %bitcast.6), channel_id=1, source_target_pairs={{4,0},{8,4},{12,8},{14,12},{10,14},{6,10},{2,6},{0,2},{5,1},{9,5},... | collective-permute-start | bytes 1572872 | tf_op jit(solution)/shard_map/low_back/ppermute | solution.py:284
  19.3 29.8 %collective-permute-start.1 = (bf16[2064,128]{1,0:T(8,128)(2,1)}, bf16[2064,128]{1,0:T(8,128)(2,1)S(1)}, u32[]{:S(2)}, u32[]{:S(2)}) collective-permute-start(bf16[2064,128]{1,0:T(8,128)(2,1)} %collective-permute-done.refs_6_), channel_id=1, source_target_pairs={{0,4},{4,8},{8,12},{12,14},{14,10},{10,6},{6,2},{2,0},{1,5},{5,9},... | collective-permute-start | bytes 1585160 | tf_op jit(solution)/shard_map/low_ahead/ppermute | solution.py:284
  19.3 29.7 %collective-permute-start.3 = (bf16[2064,128]{1,0:T(8,128)(2,1)}, bf16[2064,128]{1,0:T(8,128)(2,1)S(1)}, u32[]{:S(2)}, u32[]{:S(2)}) collective-permute-start(bf16[2064,128]{1,0:T(8,128)(2,1)} %collective-permute-done.2.refs_9_), channel_id=1, source_target_pairs={{4,0},{8,4},{12,8},{14,12},{10,14},{6,10},{2,6},{0,2},{5,1},{9,5},... | collective-permute-start | bytes 1585160 | tf_op jit(solution)/shard_map/high_back/ppermute | solution.py:284
  30.5 22.1 %collective-permute-start.10 = (bf16[2048,128]{1,0:T(8,128)(2,1)}, bf16[2048,128]{1,0:T(8,128)(2,1)}, u32[]{:S(2)}, u32[]{:S(2)}) collective-permute-start(bf16[2048,128]{1,0:T(8,128)(2,1)} %collective-permute-done.4.refs_7_), channel_id=1, source_target_pairs={{0,4},{4,8},{8,12},{12,14},{14,10},{10,6},{6,2},{2,0},{1,5},{5,9},... | collective-permute-start | bytes 1572872 | tf_op jit(solution)/shard_map/high_ahead/ppermute | solution.py:284
  30.6 22.6 %collective-permute-start.11 = (bf16[2048,128]{1,0:T(8,128)(2,1)}, bf16[2048,128]{1,0:T(8,128)(2,1)}, u32[]{:S(2)}, u32[]{:S(2)}) collective-permute-start(bf16[2048,128]{1,0:T(8,128)(2,1)} %collective-permute-done.5.refs_8_), channel_id=1, source_target_pairs={{4,0},{8,4},{12,8},{14,12},{10,14},{6,10},{2,6},{0,2},{5,1},{9,5},... | collective-permute-start | bytes 1572872 | tf_op jit(solution)/shard_map/low_back/ppermute | solution.py:284
  34.0 1.2 %collective-permute-start.7 = (s32[64]{0:T(128)S(1)}, s32[64]{0:T(128)S(1)}, u32[]{:S(2)}, u32[]{:S(2)}) collective-permute-start(s32[64]{0:T(128)S(1)} %reshape.9.own_index), channel_id=1, source_target_pairs={{0,1},{1,0},{2,3},{3,2},{4,5},{5,4},{6,7},{7,6},{8,9},{9,8},{10,11... | collective-permute-start | bytes 776 | tf_op jit(solution)/shard_map/ppermute | solution.py:301
  35.2 1.6 %copy-start = (bf16[16,1,4,128,128]{4,3,2,1,0:T(8,128)(2,1)S(1)}, bf16[16,1,4,128,128]{4,3,2,1,0:T(8,128)(2,1)}, u32[]{:S(2)}) copy-start(bf16[16,1,4,128,128]{4,3,2,1,0:T(8,128)(2,1)} %param.7) | copy-start | bytes 6291460
  36.8 5.9 %copy-start.2 = (bf16[2064,128]{1,0:T(8,128)(2,1)S(1)}, bf16[2064,128]{1,0:T(8,128)(2,1)}, u32[]{:S(2)}) copy-start(bf16[2064,128]{1,0:T(8,128)(2,1)} %copy-done.1) | copy-start | bytes 1585156
  36.8 5.9 %copy-start.4 = (bf16[2064,128]{1,0:T(8,128)(2,1)S(1)}, bf16[2064,128]{1,0:T(8,128)(2,1)}, u32[]{:S(2)}) copy-start(bf16[2064,128]{1,0:T(8,128)(2,1)} %copy-done.3) | copy-start | bytes 1585156
  49.1 14.9 %collective-permute-start.8 = (bf16[2064,128]{1,0:T(8,128)(2,1)S(1)}, bf16[2064,128]{1,0:T(8,128)(2,1)S(1)}, u32[]{:S(2)}, u32[]{:S(2)}) collective-permute-start(bf16[2064,128]{1,0:T(8,128)(2,1)S(1)} %collective-permute-done.1.refs_3_), channel_id=1, source_target_pairs={{0,4},{4,8},{8,12},{12,14},{14,10},{10,6},{6,2},{2,0},{1,5},{5,9},... | collective-permute-start | bytes 1585160 | tf_op jit(solution)/shard_map/low_ahead/ppermute | solution.py:284
  49.2 14.9 %collective-permute-start.9 = (bf16[2064,128]{1,0:T(8,128)(2,1)S(1)}, bf16[2064,128]{1,0:T(8,128)(2,1)S(1)}, u32[]{:S(2)}, u32[]{:S(2)}) collective-permute-start(bf16[2064,128]{1,0:T(8,128)(2,1)S(1)} %collective-permute-done.3.refs_6_), channel_id=1, source_target_pairs={{4,0},{8,4},{12,8},{14,12},{10,14},{6,10},{2,6},{0,2},{5,1},{9,5},... | collective-permute-start | bytes 1585160 | tf_op jit(solution)/shard_map/high_back/ppermute | solution.py:284
  52.6 22.6 %collective-permute-start.13 = (bf16[2048,128]{1,0:T(8,128)(2,1)}, bf16[2048,128]{1,0:T(8,128)(2,1)S(1)}, u32[]{:S(2)}, u32[]{:S(2)}) collective-permute-start(bf16[2048,128]{1,0:T(8,128)(2,1)} %collective-permute-done.10.refs_4_), channel_id=1, source_target_pairs={{0,4},{4,8},{8,12},{12,14},{14,10},{10,6},{6,2},{2,0},{1,5},{5,9},... | collective-permute-start | bytes 1572872 | tf_op jit(solution)/shard_map/high_ahead/ppermute | solution.py:284
  53.1 22.5 %collective-permute-start.14 = (bf16[2048,128]{1,0:T(8,128)(2,1)}, bf16[2048,128]{1,0:T(8,128)(2,1)S(1)}, u32[]{:S(2)}, u32[]{:S(2)}) collective-permute-start(bf16[2048,128]{1,0:T(8,128)(2,1)} %collective-permute-done.11.refs_5_), channel_id=1, source_target_pairs={{4,0},{8,4},{12,8},{14,12},{10,14},{6,10},{2,6},{0,2},{5,1},{9,5},... | collective-permute-start | bytes 1572872 | tf_op jit(solution)/shard_map/low_back/ppermute | solution.py:284
  64.1 19.6 %collective-permute-start.12 = (bf16[1552,128]{1,0:T(8,128)(2,1)S(1)}, bf16[1552,128]{1,0:T(8,128)(2,1)S(1)}, u32[]{:S(2)}, u32[]{:S(2)}) collective-permute-start(bf16[1552,128]{1,0:T(8,128)(2,1)S(1)} %slice.67), channel_id=1, source_target_pairs={{0,4},{4,8},{8,12},{12,14},{14,10},{10,6},{6,2},{2,0},{1,5},{5,9},... | collective-permute-start | bytes 1191944 | tf_op jit(solution)/shard_map/far_low_ahead/ppermute | solution.py:284
  66.2 17.5 %collective-permute-start.17 = (bf16[1280,128]{1,0:T(8,128)(2,1)S(1)}, bf16[1280,128]{1,0:T(8,128)(2,1)S(1)}, u32[]{:S(2)}, u32[]{:S(2)}) collective-permute-start(bf16[1280,128]{1,0:T(8,128)(2,1)S(1)} %slice.73), channel_id=1, source_target_pairs={{4,0},{8,4},{12,8},{14,12},{10,14},{6,10},{2,6},{0,2},{5,1},{9,5},... | collective-permute-start | bytes 983048 | tf_op jit(solution)/shard_map/far_high_back/ppermute | solution.py:284
  66.3 19.8 %collective-permute-start.16 = (bf16[768,128]{1,0:T(8,128)(2,1)S(1)}, bf16[768,128]{1,0:T(8,128)(2,1)S(1)}, u32[]{:S(2)}, u32[]{:S(2)}) collective-permute-start(bf16[768,128]{1,0:T(8,128)(2,1)S(1)} %slice.72), channel_id=1, source_target_pairs={{4,0},{8,4},{12,8},{14,12},{10,14},{6,10},{2,6},{0,2},{5,1},{9,5},... | collective-permute-start | bytes 589832 | tf_op jit(solution)/shard_map/last_high_back/ppermute | solution.py:284
  75.2 10.9 %collective-permute-start.15 = (bf16[512,128]{1,0:T(8,128)(2,1)S(1)}, bf16[512,128]{1,0:T(8,128)(2,1)S(1)}, u32[]{:S(2)}, u32[]{:S(2)}) collective-permute-start(bf16[512,128]{1,0:T(8,128)(2,1)S(1)} %slice.71), channel_id=1, source_target_pairs={{0,4},{4,8},{8,12},{12,14},{14,10},{10,6},{6,2},{2,0},{1,5},{5,9},... | collective-permute-start | bytes 393224 | tf_op jit(solution)/shard_map/last_low_ahead/ppermute | solution.py:284

commit v7 on v5

--- a/solution.py
+++ b/solution.py
@@ -274,6 +274,7 @@
     cut = half * slots * blk
     own_index = a_index[:, 0].T
     low_first, high_first = pack(flat, own_index)
+    low_first, high_first, b_values = lax.optimization_barrier((low_first, high_first, b_values))
     low_second, high_second = flat[:cut], flat[cut:]
 
     def read_note(message):
@@ -329,7 +330,7 @@
                 small,
                 half - small,
                 move(low[at:], ahead, "far_low_ahead"),
-                move(high[at:], back, "far_high_back"),
+                move(high[at:cut], back, "far_high_back"),
             )
         index = [read_note(behind[k][0]), read_note(beyond[k][1])]
         if k == 1:

time: 87.8 us -> 87.9 us (level)
  transfers between devices with their start and end apart: 18 -> 18, of which waited for: 10 -> 9; matrix products, arithmetic and copies ran while one was open for 6% -> 6% of each run, Pallas kernels for 28% -> 27%
where the time goes in v7:
time: 87.9 us; the launch traced here: 87.5 us
  waiting for transfers between devices  35.4 us (40%)
  Pallas kernels  25.9 us (29%)
  starting transfers between devices  19.1 us (22%)
  local copies, waits for them, and re-layouts  5.51 us (6%)
  other arithmetic  1.37 us (2%)
    ppermute x16, waiting for transfers between devices, move(): return lax.ppermute(array, 'row', way)  35 us
    ppermute x16, starting transfers between devices, move(): return lax.ppermute(array, 'row', way)  18.6 us
    pallas_call x3, Pallas kernels, product(): pl.pallas_call(functools.partial(product_kernel, offsets, sides, starts,...  15.2 us
    pallas_call x1, Pallas kernels, densify(): pl.pallas_call(densify_kernel, out_shape=jax.ShapeDtypeStruct((2 * pieces...  5.9 us
    pallas_call x2, Pallas kernels, finish(): pl.pallas_call(functools.partial(finish_kernel, parts, offset), out_shape...  3.46 us
    slice x1, local copies, waits for them, and re-layouts, body(): low_second, high_second = (flat[:cut], flat[cut:])  2.28 us
  transfers between devices with their start and end apart: 18, of which 9 were waited for; matrix products, arithmetic and copies ran while one was open for 6% of the time, Pallas kernels for 27%

profile of v7, /device:TPU:0, one launch (start us, length us, event | category | flops | bytes accessed | tf_op | source)
XLA Modules:
  0.0 87.5 jit_solution(17679449054268071477)
XLA Ops:
  0.0 1.3 %pack.1 = (bf16[2064,128]{1,0:T(8,128)(2,1)S(1)}, bf16[2064,128]{1,0:T(8,128)(2,1)S(1)}) custom-call(bf16[4096,128]{1,0:T(8,128)(2,1)} %bitcast.16, s32[2,16]{1,0:T(2,128)} %bitcast.14), custom_call_target="tpu_custom_call" | custom-call | tf_op jit(solution)/shard_map/pack/pallas_call | solution.py:247
  1.8 2.6 %collective-permute-start.2 = (bf16[2064,128]{1,0:T(8,128)(2,1)S(1)}, bf16[2064,128]{1,0:T(8,128)(2,1)}, u32[]{:S(2)}, u32[]{:S(2)}) collective-permute-start(bf16[2064,128]{1,0:T(8,128)(2,1)S(1)} %get-tuple-element.21.refs_5_), channel_id=1, source_target_pairs={{4,0},{8,4},{12,8},{14,12},{10,14},{6,10},{2,6},{0,2},{5,1},{9,5},... | collective-permute-start | bytes 1585160 | tf_op jit(solution)/shard_map/high_back/ppermute | solution.py:285
  4.5 2.3 %fusion.1 = (bf16[8,1,2,128,128]{4,3,2,1,0:T(8,128)(2,1)}, bf16[8,1,2,128,128]{4,3,2,1,0:T(8,128)(2,1)}) fusion(bf16[16,1,2,128,128]{4,3,2,1,0:T(8,128)(2,1)} %param.5), kind=kLoop, calls=%fused_computation.9 | loop fusion | bytes 2097152 | tf_op jit(solution)/shard_map/slice | solution.py:278
  6.8 1.9 %collective-permute-start.4 = (bf16[2048,128]{1,0:T(8,128)(2,1)}, bf16[2048,128]{1,0:T(8,128)(2,1)}, u32[]{:S(2)}, u32[]{:S(2)}) collective-permute-start(bf16[2048,128]{1,0:T(8,128)(2,1)} %bitcast.5), channel_id=1, source_target_pairs={{0,4},{4,8},{8,12},{12,14},{14,10},{10,6},{6,2},{2,0},{1,5},{5,9},... | collective-permute-start | bytes 1572872 | tf_op jit(solution)/shard_map/high_ahead/ppermute | solution.py:285
  8.8 10.5 %collective-permute-done.refs_6_ = bf16[2064,128]{1,0:T(8,128)(2,1)} collective-permute-done((bf16[2064,128]{1,0:T(8,128)(2,1)S(1)}, bf16[2064,128]{1,0:T(8,128)(2,1)}, u32[]{:S(2)}, u32[]{:S(2)}) %collective-permute-start) | collective-permute-done | bytes 528416 | tf_op jit(solution)/shard_map/low_ahead/ppermute | solution.py:285
  19.5 1.9 %collective-permute-start.3 = (bf16[2064,128]{1,0:T(8,128)(2,1)}, bf16[2064,128]{1,0:T(8,128)(2,1)S(1)}, u32[]{:S(2)}, u32[]{:S(2)}) collective-permute-start(bf16[2064,128]{1,0:T(8,128)(2,1)} %collective-permute-done.2.refs_9_), channel_id=1, source_target_pairs={{4,0},{8,4},{12,8},{14,12},{10,14},{6,10},{2,6},{0,2},{5,1},{9,5},... | collective-permute-start | bytes 1585160 | tf_op jit(solution)/shard_map/high_back/ppermute | solution.py:285
  22.1 8.5 %collective-permute-done.4.refs_7_ = bf16[2048,128]{1,0:T(8,128)(2,1)} collective-permute-done((bf16[2048,128]{1,0:T(8,128)(2,1)}, bf16[2048,128]{1,0:T(8,128)(2,1)}, u32[]{:S(2)}, u32[]{:S(2)}) %collective-permute-start.4) | collective-permute-done | bytes 524320 | tf_op jit(solution)/shard_map/high_ahead/ppermute | solution.py:285
  30.7 1.9 %collective-permute-start.11 = (bf16[2048,128]{1,0:T(8,128)(2,1)}, bf16[2048,128]{1,0:T(8,128)(2,1)}, u32[]{:S(2)}, u32[]{:S(2)}) collective-permute-start(bf16[2048,128]{1,0:T(8,128)(2,1)} %collective-permute-done.5.refs_8_), channel_id=1, source_target_pairs={{4,0},{8,4},{12,8},{14,12},{10,14},{6,10},{2,6},{0,2},{5,1},{9,5},... | collective-permute-start | bytes 1572872 | tf_op jit(solution)/shard_map/low_back/ppermute | solution.py:285
  35.3 1.6 %copy-done = bf16[16,1,4,128,128]{4,3,2,1,0:T(8,128)(2,1)S(1)} copy-done((bf16[16,1,4,128,128]{4,3,2,1,0:T(8,128)(2,1)S(1)}, bf16[16,1,4,128,128]{4,3,2,1,0:T(8,128)(2,1)}, u32[]{:S(2)}) %copy-start) | copy-done | bytes 2097176
  36.9 5.9 %densify.1.refs_10_.refs_11_.refs_12_.refs_7_.refs_8_.right = bf16[8,4,128,1024]{3,2,1,0:T(8,128)(2,1)S(1)} custom-call(s32[1]{0:T(128)} %bitcast.7.col_ref, s32[64]{0:T(128)S(1)} %reshape.9.own_index, s32[64]{0:T(128)S(1)} %collective-permute-done.7.other_index, bf16[16,4,128,128]{3,2,1,0:T(8,128)(2,1)S(1)} %bitcast.13, ...), custom_call_target="tpu_custom_call" | custom-call | tf_op jit(solution)/shard_map/densify/pallas_call | solution.py:44
  42.9 6.3 %product.3.refs_9_ = f32[16,128,1024]{2,1,0:T(8,128)S(1)} custom-call(s32[8]{0:T(128)S(1)} %get-tuple-element.33.refs_0_, s32[2,16]{1,0:T(2,128)S(1)} %bitcast.15, s32[2,16]{1,0:T(2,128)S(1)} %slice_convert_fusion.2.refs_2_, s32[2,16]{1,0:T(2,128)S(1)} %slice_convert_fusion.1.refs_3_, bf16[2064,128]{1,0:T(8,128)(2,1)S(1)} %copy-done.2, ...), custom_call_target="tpu_custom_call" | custom-call | tf_op jit(solution)/shard_map/product/pallas_call | solution.py:148
  49.3 1.9 %collective-permute-start.9 = (bf16[2064,128]{1,0:T(8,128)(2,1)S(1)}, bf16[2064,128]{1,0:T(8,128)(2,1)S(1)}, u32[]{:S(2)}, u32[]{:S(2)}) collective-permute-start(bf16[2064,128]{1,0:T(8,128)(2,1)S(1)} %collective-permute-done.3.refs_6_), channel_id=1, source_target_pairs={{4,0},{8,4},{12,8},{14,12},{10,14},{6,10},{2,6},{0,2},{5,1},{9,5},... | collective-permute-start | bytes 1585160 | tf_op jit(solution)/shard_map/high_back/ppermute | solution.py:285
  51.2 1.3 %collective-permute-done.10.refs_4_ = bf16[2048,128]{1,0:T(8,128)(2,1)} collective-permute-done((bf16[2048,128]{1,0:T(8,128)(2,1)}, bf16[2048,128]{1,0:T(8,128)(2,1)}, u32[]{:S(2)}, u32[]{:S(2)}) %collective-permute-start.10) | collective-permute-done | bytes 524320 | tf_op jit(solution)/shard_map/high_ahead/ppermute | solution.py:285
  53.0 1.6 %collective-permute-start.14 = (bf16[2048,128]{1,0:T(8,128)(2,1)}, bf16[2048,128]{1,0:T(8,128)(2,1)S(1)}, u32[]{:S(2)}, u32[]{:S(2)}) collective-permute-start(bf16[2048,128]{1,0:T(8,128)(2,1)} %collective-permute-done.11.refs_5_), channel_id=1, source_target_pairs={{4,0},{8,4},{12,8},{14,12},{10,14},{6,10},{2,6},{0,2},{5,1},{9,5},... | collective-permute-start | bytes 1572872 | tf_op jit(solution)/shard_map/low_back/ppermute | solution.py:285
  54.6 5.1 %product.4.refs_9_ = f32[16,128,1024]{2,1,0:T(8,128)S(1)} custom-call(s32[8]{0:T(128)S(1)} %get-tuple-element.33.refs_0_, s32[2,16]{1,0:T(2,128)S(1)} %get-tuple-element.36.refs_1_, s32[2,16]{1,0:T(2,128)S(1)} %get-tuple-element.35.refs_2_, bf16[2064,128]{1,0:T(8,128)(2,1)S(1)} %collective-permute-done.1.refs_3_, ...), custom_call_target="tpu_custom_call", output_to_operand_aliasing={{}: (9, {})} | custom-call | tf_op jit(solution)/shard_map/product/pallas_call | solution.py:148
  59.7 4.4 %collective-permute-done.8.refs_3_ = bf16[2064,128]{1,0:T(8,128)(2,1)S(1)} collective-permute-done((bf16[2064,128]{1,0:T(8,128)(2,1)S(1)}, bf16[2064,128]{1,0:T(8,128)(2,1)S(1)}, u32[]{:S(2)}, u32[]{:S(2)}) %collective-permute-start.8) | collective-permute-done | bytes 528416 | tf_op jit(solution)/shard_map/low_ahead/ppermute | solution.py:285
  64.3 2.1 %collective-permute-start.12 = (bf16[1552,128]{1,0:T(8,128)(2,1)S(1)}, bf16[1552,128]{1,0:T(8,128)(2,1)S(1)}, u32[]{:S(2)}, u32[]{:S(2)}) collective-permute-start(bf16[1552,128]{1,0:T(8,128)(2,1)S(1)} %slice.67), channel_id=1, source_target_pairs={{0,4},{4,8},{8,12},{12,14},{14,10},{10,6},{6,2},{2,0},{1,5},{5,9},... | collective-permute-start | bytes 1191944 | tf_op jit(solution)/shard_map/far_low_ahead/ppermute | solution.py:285
  66.4 2.0 %collective-permute-start.15 = (bf16[512,128]{1,0:T(8,128)(2,1)S(1)}, bf16[512,128]{1,0:T(8,128)(2,1)S(1)}, u32[]{:S(2)}, u32[]{:S(2)}) collective-permute-start(bf16[512,128]{1,0:T(8,128)(2,1)S(1)} %slice.71), channel_id=1, source_target_pairs={{0,4},{4,8},{8,12},{12,14},{14,10},{10,6},{6,2},{2,0},{1,5},{5,9},... | collective-permute-start | bytes 393224 | tf_op jit(solution)/shard_map/last_low_ahead/ppermute | solution.py:285
  68.4 6.9 %collective-permute-done.13.refs_4_ = bf16[2048,128]{1,0:T(8,128)(2,1)S(1)} collective-permute-done((bf16[2048,128]{1,0:T(8,128)(2,1)}, bf16[2048,128]{1,0:T(8,128)(2,1)S(1)}, u32[]{:S(2)}, u32[]{:S(2)}) %collective-permute-start.13) | collective-permute-done | bytes 524320 | tf_op jit(solution)/shard_map/high_ahead/ppermute | solution.py:285
  75.3 1.6 %collective-permute-start.16 = (bf16[512,128]{1,0:T(8,128)(2,1)S(1)}, bf16[512,128]{1,0:T(8,128)(2,1)S(1)}, u32[]{:S(2)}, u32[]{:S(2)}) collective-permute-start(bf16[512,128]{1,0:T(8,128)(2,1)S(1)} %slice.72), channel_id=1, source_target_pairs={{4,0},{8,4},{12,8},{14,12},{10,14},{6,10},{2,6},{0,2},{5,1},{9,5},... | collective-permute-start | bytes 393224 | tf_op jit(solution)/shard_map/last_high_back/ppermute | solution.py:285
  76.9 3.9 %product.5.total = f32[16,128,1024]{2,1,0:T(8,128)S(1)} custom-call(s32[8]{0:T(128)S(1)} %get-tuple-element.33.refs_0_, s32[2,16]{1,0:T(2,128)S(1)} %slice_convert_fusion.4.refs_1_, s32[2,16]{1,0:T(2,128)S(1)} %slice_convert_fusion.3.refs_2_, bf16[2064,128]{1,0:T(8,128)(2,1)S(1)} %collective-permute-done.8.refs_3_, ...), custom_call_target="tpu_custom_call", output_to_operand_aliasing={{}: (9, {})} | custom-call | tf_op jit(solution)/shard_map/product/pallas_call | solution.py:148
  80.8 3.0 %collective-permute-done.12.refs_0_ = bf16[1552,128]{1,0:T(8,128)(2,1)S(1)} collective-permute-done((bf16[1552,128]{1,0:T(8,128)(2,1)S(1)}, bf16[1552,128]{1,0:T(8,128)(2,1)S(1)}, u32[]{:S(2)}, u32[]{:S(2)}) %collective-permute-start.12) | collective-permute-done | bytes 397344 | tf_op jit(solution)/shard_map/far_low_ahead/ppermute | solution.py:285
  83.8 2.1 %finish.2.refs_2_ = bf16[16,1,8,128,128]{4,3,2,1,0:T(8,128)(2,1)} custom-call(s32[1,8]{1,0:T(1,128)S(1)} %get-tuple-element.34.cycle_ref, s32[2,16]{1,0:T(2,128)S(1)} %slice_convert_fusion.index_ref, bf16[8,4,128,1024]{3,2,1,0:T(8,128)(2,1)S(1)} %densify.1.refs_10_.refs_11_.refs_12_.refs_7_.refs_8_.right, f32[16,128,1024]{2,1,0:T(8,128)S(1)} %product.5.total, ...), custom_call_target="tpu_custom_call" | custom-call | tf_op jit(solution)/shard_map/finish/pallas_call | solution.py:206
  86.1 1.3 %finish.3 = bf16[16,1,8,128,128]{4,3,2,1,0:T(8,128)(2,1)} custom-call(s32[1,8]{1,0:T(1,128)S(1)} %get-tuple-element.34.cycle_ref, s32[2,16]{1,0:T(2,128)S(1)} %slice_convert_fusion.index_ref, bf16[8,4,128,1024]{3,2,1,0:T(8,128)(2,1)S(1)} %densify.1.refs_10_.refs_11_.refs_12_.refs_7_.refs_8_.right, ...), custom_call_target="tpu_custom_call", output_to_operand_aliasing={{}: (6, {})} | custom-call | tf_op jit(solution)/shard_map/finish/pallas_call | solution.py:206
  (45 shorter events, 5.4 us)
Async XLA Ops:
  0.0 42.8 %copy-start.5 = (s32[16,1,2]{0,2,1:T(2,128)S(1)}, s32[16,1,2]{0,2,1:T(2,128)}, u32[]{:S(2)}) copy-start(s32[16,1,2]{0,2,1:T(2,128)} %param.6) | copy-start | bytes 388
  1.3 7.6 %copy-start.1 = (bf16[2064,128]{1,0:T(8,128)(2,1)}, bf16[2064,128]{1,0:T(8,128)(2,1)S(1)}, u32[]{:S(2)}) copy-start(bf16[2064,128]{1,0:T(8,128)(2,1)S(1)} %get-tuple-element.20.refs_4_) | copy-start | bytes 1585156
  1.3 18.2 %copy-start.3 = (bf16[2064,128]{1,0:T(8,128)(2,1)}, bf16[2064,128]{1,0:T(8,128)(2,1)S(1)}, u32[]{:S(2)}) copy-start(bf16[2064,128]{1,0:T(8,128)(2,1)S(1)} %get-tuple-element.21.refs_5_) | copy-start | bytes 1585156
  1.3 32.0 %collective-permute-start.6 = (bf16[16,4,128,128]{3,2,1,0:T(8,128)(2,1)}, bf16[16,4,128,128]{3,2,1,0:T(8,128)(2,1)S(1)}, u32[]{:S(2)}, u32[]{:S(2)}) collective-permute-start(bf16[16,4,128,128]{3,2,1,0:T(8,128)(2,1)} %bitcast.12), channel_id=1, source_target_pairs={{0,1},{1,0},{2,3},{3,2},{4,5},{5,4},{6,7},{7,6},{8,9},{9,8},{10,11... | collective-permute-start | bytes 6291464 | tf_op jit(solution)/shard_map/ppermute | solution.py:300
  1.8 17.7 %collective-permute-start.2 = (bf16[2064,128]{1,0:T(8,128)(2,1)S(1)}, bf16[2064,128]{1,0:T(8,128)(2,1)}, u32[]{:S(2)}, u32[]{:S(2)}) collective-permute-start(bf16[2064,128]{1,0:T(8,128)(2,1)S(1)} %get-tuple-element.21.refs_5_), channel_id=1, source_target_pairs={{4,0},{8,4},{12,8},{14,12},{10,14},{6,10},{2,6},{0,2},{5,1},{9,5},... | collective-permute-start | bytes 1585160 | tf_op jit(solution)/shard_map/high_back/ppermute | solution.py:285
  4.4 15.0 %collective-permute-start = (bf16[2064,128]{1,0:T(8,128)(2,1)S(1)}, bf16[2064,128]{1,0:T(8,128)(2,1)}, u32[]{:S(2)}, u32[]{:S(2)}) collective-permute-start(bf16[2064,128]{1,0:T(8,128)(2,1)S(1)} %get-tuple-element.20.refs_4_), channel_id=1, source_target_pairs={{0,4},{4,8},{8,12},{12,14},{14,10},{10,6},{6,2},{2,0},{1,5},{5,9},... | collective-permute-start | bytes 1585160 | tf_op jit(solution)/shard_map/low_ahead/ppermute | solution.py:285
  6.8 23.8 %collective-permute-start.4 = (bf16[2048,128]{1,0:T(8,128)(2,1)}, bf16[2048,128]{1,0:T(8,128)(2,1)}, u32[]{:S(2)}, u32[]{:S(2)}) collective-permute-start(bf16[2048,128]{1,0:T(8,128)(2,1)} %bitcast.5), channel_id=1, source_target_pairs={{0,4},{4,8},{8,12},{12,14},{14,10},{10,6},{6,2},{2,0},{1,5},{5,9},... | collective-permute-start | bytes 1572872 | tf_op jit(solution)/shard_map/high_ahead/ppermute | solution.py:285
  8.8 21.9 %collective-permute-start.5 = (bf16[2048,128]{1,0:T(8,128)(2,1)}, bf16[2048,128]{1,0:T(8,128)(2,1)}, u32[]{:S(2)}, u32[]{:S(2)}) collective-permute-start(bf16[2048,128]{1,0:T(8,128)(2,1)} %bitcast.6), channel_id=1, source_target_pairs={{4,0},{8,4},{12,8},{14,12},{10,14},{6,10},{2,6},{0,2},{5,1},{9,5},... | collective-permute-start | bytes 1572872 | tf_op jit(solution)/shard_map/low_back/ppermute | solution.py:285
  19.4 29.8 %collective-permute-start.1 = (bf16[2064,128]{1,0:T(8,128)(2,1)}, bf16[2064,128]{1,0:T(8,128)(2,1)S(1)}, u32[]{:S(2)}, u32[]{:S(2)}) collective-permute-start(bf16[2064,128]{1,0:T(8,128)(2,1)} %collective-permute-done.refs_6_), channel_id=1, source_target_pairs={{0,4},{4,8},{8,12},{12,14},{14,10},{10,6},{6,2},{2,0},{1,5},{5,9},... | collective-permute-start | bytes 1585160 | tf_op jit(solution)/shard_map/low_ahead/ppermute | solution.py:285
  19.5 29.7 %collective-permute-start.3 = (bf16[2064,128]{1,0:T(8,128)(2,1)}, bf16[2064,128]{1,0:T(8,128)(2,1)S(1)}, u32[]{:S(2)}, u32[]{:S(2)}) collective-permute-start(bf16[2064,128]{1,0:T(8,128)(2,1)} %collective-permute-done.2.refs_9_), channel_id=1, source_target_pairs={{4,0},{8,4},{12,8},{14,12},{10,14},{6,10},{2,6},{0,2},{5,1},{9,5},... | collective-permute-start | bytes 1585160 | tf_op jit(solution)/shard_map/high_back/ppermute | solution.py:285
  30.6 22.0 %collective-permute-start.10 = (bf16[2048,128]{1,0:T(8,128)(2,1)}, bf16[2048,128]{1,0:T(8,128)(2,1)}, u32[]{:S(2)}, u32[]{:S(2)}) collective-permute-start(bf16[2048,128]{1,0:T(8,128)(2,1)} %collective-permute-done.4.refs_7_), channel_id=1, source_target_pairs={{0,4},{4,8},{8,12},{12,14},{14,10},{10,6},{6,2},{2,0},{1,5},{5,9},... | collective-permute-start | bytes 1572872 | tf_op jit(solution)/shard_map/high_ahead/ppermute | solution.py:285
  30.7 22.3 %collective-permute-start.11 = (bf16[2048,128]{1,0:T(8,128)(2,1)}, bf16[2048,128]{1,0:T(8,128)(2,1)}, u32[]{:S(2)}, u32[]{:S(2)}) collective-permute-start(bf16[2048,128]{1,0:T(8,128)(2,1)} %collective-permute-done.5.refs_8_), channel_id=1, source_target_pairs={{4,0},{8,4},{12,8},{14,12},{10,14},{6,10},{2,6},{0,2},{5,1},{9,5},... | collective-permute-start | bytes 1572872 | tf_op jit(solution)/shard_map/low_back/ppermute | solution.py:285
  34.1 1.2 %collective-permute-start.7 = (s32[64]{0:T(128)S(1)}, s32[64]{0:T(128)S(1)}, u32[]{:S(2)}, u32[]{:S(2)}) collective-permute-start(s32[64]{0:T(128)S(1)} %reshape.9.own_index), channel_id=1, source_target_pairs={{0,1},{1,0},{2,3},{3,2},{4,5},{5,4},{6,7},{7,6},{8,9},{9,8},{10,11... | collective-permute-start | bytes 776 | tf_op jit(solution)/shard_map/ppermute | solution.py:302
  35.3 1.6 %copy-start = (bf16[16,1,4,128,128]{4,3,2,1,0:T(8,128)(2,1)S(1)}, bf16[16,1,4,128,128]{4,3,2,1,0:T(8,128)(2,1)}, u32[]{:S(2)}) copy-start(bf16[16,1,4,128,128]{4,3,2,1,0:T(8,128)(2,1)} %param.7) | copy-start | bytes 6291460
  36.9 5.9 %copy-start.2 = (bf16[2064,128]{1,0:T(8,128)(2,1)S(1)}, bf16[2064,128]{1,0:T(8,128)(2,1)}, u32[]{:S(2)}) copy-start(bf16[2064,128]{1,0:T(8,128)(2,1)} %copy-done.1) | copy-start | bytes 1585156
  36.9 5.9 %copy-start.4 = (bf16[2064,128]{1,0:T(8,128)(2,1)S(1)}, bf16[2064,128]{1,0:T(8,128)(2,1)}, u32[]{:S(2)}) copy-start(bf16[2064,128]{1,0:T(8,128)(2,1)} %copy-done.3) | copy-start | bytes 1585156
  49.2 14.9 %collective-permute-start.8 = (bf16[2064,128]{1,0:T(8,128)(2,1)S(1)}, bf16[2064,128]{1,0:T(8,128)(2,1)S(1)}, u32[]{:S(2)}, u32[]{:S(2)}) collective-permute-start(bf16[2064,128]{1,0:T(8,128)(2,1)S(1)} %collective-permute-done.1.refs_3_), channel_id=1, source_target_pairs={{0,4},{4,8},{8,12},{12,14},{14,10},{10,6},{6,2},{2,0},{1,5},{5,9},... | collective-permute-start | bytes 1585160 | tf_op jit(solution)/shard_map/low_ahead/ppermute | solution.py:285
  49.3 14.9 %collective-permute-start.9 = (bf16[2064,128]{1,0:T(8,128)(2,1)S(1)}, bf16[2064,128]{1,0:T(8,128)(2,1)S(1)}, u32[]{:S(2)}, u32[]{:S(2)}) collective-permute-start(bf16[2064,128]{1,0:T(8,128)(2,1)S(1)} %collective-permute-done.3.refs_6_), channel_id=1, source_target_pairs={{4,0},{8,4},{12,8},{14,12},{10,14},{6,10},{2,6},{0,2},{5,1},{9,5},... | collective-permute-start | bytes 1585160 | tf_op jit(solution)/shard_map/high_back/ppermute | solution.py:285
  52.6 22.7 %collective-permute-start.13 = (bf16[2048,128]{1,0:T(8,128)(2,1)}, bf16[2048,128]{1,0:T(8,128)(2,1)S(1)}, u32[]{:S(2)}, u32[]{:S(2)}) collective-permute-start(bf16[2048,128]{1,0:T(8,128)(2,1)} %collective-permute-done.10.refs_4_), channel_id=1, source_target_pairs={{0,4},{4,8},{8,12},{12,14},{14,10},{10,6},{6,2},{2,0},{1,5},{5,9},... | collective-permute-start | bytes 1572872 | tf_op jit(solution)/shard_map/high_ahead/ppermute | solution.py:285
  53.0 23.9 %collective-permute-start.14 = (bf16[2048,128]{1,0:T(8,128)(2,1)}, bf16[2048,128]{1,0:T(8,128)(2,1)S(1)}, u32[]{:S(2)}, u32[]{:S(2)}) collective-permute-start(bf16[2048,128]{1,0:T(8,128)(2,1)} %collective-permute-done.11.refs_5_), channel_id=1, source_target_pairs={{4,0},{8,4},{12,8},{14,12},{10,14},{6,10},{2,6},{0,2},{5,1},{9,5},... | collective-permute-start | bytes 1572872 | tf_op jit(solution)/shard_map/low_back/ppermute | solution.py:285
  64.3 19.5 %collective-permute-start.12 = (bf16[1552,128]{1,0:T(8,128)(2,1)S(1)}, bf16[1552,128]{1,0:T(8,128)(2,1)S(1)}, u32[]{:S(2)}, u32[]{:S(2)}) collective-permute-start(bf16[1552,128]{1,0:T(8,128)(2,1)S(1)} %slice.67), channel_id=1, source_target_pairs={{0,4},{4,8},{8,12},{12,14},{14,10},{10,6},{6,2},{2,0},{1,5},{5,9},... | collective-permute-start | bytes 1191944 | tf_op jit(solution)/shard_map/far_low_ahead/ppermute | solution.py:285
  66.3 17.5 %collective-permute-start.17 = (bf16[1536,128]{1,0:T(8,128)(2,1)S(1)}, bf16[1536,128]{1,0:T(8,128)(2,1)S(1)}, u32[]{:S(2)}, u32[]{:S(2)}) collective-permute-start(bf16[1536,128]{1,0:T(8,128)(2,1)S(1)} %slice.73), channel_id=1, source_target_pairs={{4,0},{8,4},{12,8},{14,12},{10,14},{6,10},{2,6},{0,2},{5,1},{9,5},... | collective-permute-start | bytes 1179656 | tf_op jit(solution)/shard_map/far_high_back/ppermute | solution.py:285
  66.4 19.8 %collective-permute-start.15 = (bf16[512,128]{1,0:T(8,128)(2,1)S(1)}, bf16[512,128]{1,0:T(8,128)(2,1)S(1)}, u32[]{:S(2)}, u32[]{:S(2)}) collective-permute-start(bf16[512,128]{1,0:T(8,128)(2,1)S(1)} %slice.71), channel_id=1, source_target_pairs={{0,4},{4,8},{8,12},{12,14},{14,10},{10,6},{6,2},{2,0},{1,5},{5,9},... | collective-permute-start | bytes 393224 | tf_op jit(solution)/shard_map/last_low_ahead/ppermute | solution.py:285
  75.3 10.9 %collective-permute-start.16 = (bf16[512,128]{1,0:T(8,128)(2,1)S(1)}, bf16[512,128]{1,0:T(8,128)(2,1)S(1)}, u32[]{:S(2)}, u32[]{:S(2)}) collective-permute-start(bf16[512,128]{1,0:T(8,128)(2,1)S(1)} %slice.72), channel_id=1, source_target_pairs={{4,0},{8,4},{12,8},{14,12},{10,14},{6,10},{2,6},{0,2},{5,1},{9,5},... | collective-permute-start | bytes 393224 | tf_op jit(solution)/shard_map/last_high_back/ppermute | solution.py:285

commit v8 on v6

--- a/solution.py
+++ b/solution.py
@@ -274,6 +274,7 @@
     cut = half * slots * blk
     own_index = a_index[:, 0].T
     low_first, high_first = pack(flat, own_index)
+    low_first, high_first, b_values = lax.optimization_barrier((low_first, high_first, b_values))
     low_second, high_second = flat[:cut], flat[cut:]
 
     def read_note(message):

time: 87.9 us -> 88 us (level)
  transfers between devices with their start and end apart: 18 -> 18, of which waited for: 9 -> 9; matrix products, arithmetic and copies ran while one was open for 6% -> 6% of each run, Pallas kernels for 28% -> 26%
where the time goes in v8:
time: 88 us; the launch traced here: 87.6 us
  waiting for transfers between devices  36.9 us (42%)
  Pallas kernels  25.9 us (29%)
  starting transfers between devices  17.8 us (20%)
  local copies, waits for them, and re-layouts  5.51 us (6%)
  other arithmetic  1.37 us (2%)
    ppermute x16, waiting for transfers between devices, move(): return lax.ppermute(array, 'row', way)  36.5 us
    ppermute x16, starting transfers between devices, move(): return lax.ppermute(array, 'row', way)  17.2 us
    pallas_call x3, Pallas kernels, product(): pl.pallas_call(functools.partial(product_kernel, offsets, sides, starts,...  15.2 us
    pallas_call x1, Pallas kernels, densify(): pl.pallas_call(densify_kernel, out_shape=jax.ShapeDtypeStruct((2 * pieces...  5.9 us
    pallas_call x2, Pallas kernels, finish(): pl.pallas_call(functools.partial(finish_kernel, parts, offset), out_shape...  3.46 us
    slice x1, local copies, waits for them, and re-layouts, body(): low_second, high_second = (flat[:cut], flat[cut:])  2.28 us
  transfers between devices with their start and end apart: 18, of which 9 were waited for; matrix products, arithmetic and copies ran while one was open for 6% of the time, Pallas kernels for 26%

profile of v8, /device:TPU:0, one launch (start us, length us, event | category | flops | bytes accessed | tf_op | source)
XLA Modules:
  0.0 87.6 jit_solution(16101961846805794731)
XLA Ops:
  0.0 1.3 %pack.1 = (bf16[2064,128]{1,0:T(8,128)(2,1)S(1)}, bf16[2064,128]{1,0:T(8,128)(2,1)S(1)}) custom-call(bf16[4096,128]{1,0:T(8,128)(2,1)} %bitcast.16, s32[2,16]{1,0:T(2,128)} %bitcast.14), custom_call_target="tpu_custom_call" | custom-call | tf_op jit(solution)/shard_map/pack/pallas_call | solution.py:247
  1.8 2.6 %collective-permute-start.2 = (bf16[2064,128]{1,0:T(8,128)(2,1)S(1)}, bf16[2064,128]{1,0:T(8,128)(2,1)}, u32[]{:S(2)}, u32[]{:S(2)}) collective-permute-start(bf16[2064,128]{1,0:T(8,128)(2,1)S(1)} %get-tuple-element.21.refs_5_), channel_id=1, source_target_pairs={{4,0},{8,4},{12,8},{14,12},{10,14},{6,10},{2,6},{0,2},{5,1},{9,5},... | collective-permute-start | bytes 1585160 | tf_op jit(solution)/shard_map/high_back/ppermute | solution.py:285
  4.5 2.3 %fusion.1 = (bf16[8,1,2,128,128]{4,3,2,1,0:T(8,128)(2,1)}, bf16[8,1,2,128,128]{4,3,2,1,0:T(8,128)(2,1)}) fusion(bf16[16,1,2,128,128]{4,3,2,1,0:T(8,128)(2,1)} %param.5), kind=kLoop, calls=%fused_computation.9 | loop fusion | bytes 2097152 | tf_op jit(solution)/shard_map/slice | solution.py:278
  6.8 1.9 %collective-permute-start.4 = (bf16[2048,128]{1,0:T(8,128)(2,1)}, bf16[2048,128]{1,0:T(8,128)(2,1)}, u32[]{:S(2)}, u32[]{:S(2)}) collective-permute-start(bf16[2048,128]{1,0:T(8,128)(2,1)} %bitcast.5), channel_id=1, source_target_pairs={{0,4},{4,8},{8,12},{12,14},{14,10},{10,6},{6,2},{2,0},{1,5},{5,9},... | collective-permute-start | bytes 1572872 | tf_op jit(solution)/shard_map/high_ahead/ppermute | solution.py:285
  8.8 10.5 %collective-permute-done.refs_6_ = bf16[2064,128]{1,0:T(8,128)(2,1)} collective-permute-done((bf16[2064,128]{1,0:T(8,128)(2,1)S(1)}, bf16[2064,128]{1,0:T(8,128)(2,1)}, u32[]{:S(2)}, u32[]{:S(2)}) %collective-permute-start) | collective-permute-done | bytes 528416 | tf_op jit(solution)/shard_map/low_ahead/ppermute | solution.py:285
  19.5 1.9 %collective-permute-start.3 = (bf16[2064,128]{1,0:T(8,128)(2,1)}, bf16[2064,128]{1,0:T(8,128)(2,1)S(1)}, u32[]{:S(2)}, u32[]{:S(2)}) collective-permute-start(bf16[2064,128]{1,0:T(8,128)(2,1)} %collective-permute-done.2.refs_9_), channel_id=1, source_target_pairs={{4,0},{8,4},{12,8},{14,12},{10,14},{6,10},{2,6},{0,2},{5,1},{9,5},... | collective-permute-start | bytes 1585160 | tf_op jit(solution)/shard_map/high_back/ppermute | solution.py:285
  22.1 8.5 %collective-permute-done.4.refs_7_ = bf16[2048,128]{1,0:T(8,128)(2,1)} collective-permute-done((bf16[2048,128]{1,0:T(8,128)(2,1)}, bf16[2048,128]{1,0:T(8,128)(2,1)}, u32[]{:S(2)}, u32[]{:S(2)}) %collective-permute-start.4) | collective-permute-done | bytes 524320 | tf_op jit(solution)/shard_map/high_ahead/ppermute | solution.py:285
  30.7 1.9 %collective-permute-start.11 = (bf16[2048,128]{1,0:T(8,128)(2,1)}, bf16[2048,128]{1,0:T(8,128)(2,1)}, u32[]{:S(2)}, u32[]{:S(2)}) collective-permute-start(bf16[2048,128]{1,0:T(8,128)(2,1)} %collective-permute-done.5.refs_8_), channel_id=1, source_target_pairs={{4,0},{8,4},{12,8},{14,12},{10,14},{6,10},{2,6},{0,2},{5,1},{9,5},... | collective-permute-start | bytes 1572872 | tf_op jit(solution)/shard_map/low_back/ppermute | solution.py:285
  33.3 0.8 copy.10
  35.3 1.6 %copy-done = bf16[16,1,4,128,128]{4,3,2,1,0:T(8,128)(2,1)S(1)} copy-done((bf16[16,1,4,128,128]{4,3,2,1,0:T(8,128)(2,1)S(1)}, bf16[16,1,4,128,128]{4,3,2,1,0:T(8,128)(2,1)}, u32[]{:S(2)}) %copy-start) | copy-done | bytes 2097176
  36.9 5.9 %densify.1.refs_10_.refs_11_.refs_12_.refs_7_.refs_8_.right = bf16[8,4,128,1024]{3,2,1,0:T(8,128)(2,1)S(1)} custom-call(s32[1]{0:T(128)} %bitcast.7.col_ref, s32[64]{0:T(128)S(1)} %reshape.9.own_index, s32[64]{0:T(128)S(1)} %collective-permute-done.7.other_index, bf16[16,4,128,128]{3,2,1,0:T(8,128)(2,1)S(1)} %bitcast.13, ...), custom_call_target="tpu_custom_call" | custom-call | tf_op jit(solution)/shard_map/densify/pallas_call | solution.py:44
  42.9 6.3 %product.3.refs_9_ = f32[16,128,1024]{2,1,0:T(8,128)S(1)} custom-call(s32[8]{0:T(128)S(1)} %get-tuple-element.33.refs_0_, s32[2,16]{1,0:T(2,128)S(1)} %bitcast.15, s32[2,16]{1,0:T(2,128)S(1)} %slice_convert_fusion.2.refs_2_, s32[2,16]{1,0:T(2,128)S(1)} %slice_convert_fusion.1.refs_3_, bf16[2064,128]{1,0:T(8,128)(2,1)S(1)} %copy-done.2, ...), custom_call_target="tpu_custom_call" | custom-call | tf_op jit(solution)/shard_map/product/pallas_call | solution.py:148
  49.3 1.9 %collective-permute-start.9 = (bf16[2064,128]{1,0:T(8,128)(2,1)S(1)}, bf16[2064,128]{1,0:T(8,128)(2,1)S(1)}, u32[]{:S(2)}, u32[]{:S(2)}) collective-permute-start(bf16[2064,128]{1,0:T(8,128)(2,1)S(1)} %collective-permute-done.3.refs_6_), channel_id=1, source_target_pairs={{4,0},{8,4},{12,8},{14,12},{10,14},{6,10},{2,6},{0,2},{5,1},{9,5},... | collective-permute-start | bytes 1585160 | tf_op jit(solution)/shard_map/high_back/ppermute | solution.py:285
  51.2 1.3 %collective-permute-done.10.refs_4_ = bf16[2048,128]{1,0:T(8,128)(2,1)} collective-permute-done((bf16[2048,128]{1,0:T(8,128)(2,1)}, bf16[2048,128]{1,0:T(8,128)(2,1)}, u32[]{:S(2)}, u32[]{:S(2)}) %collective-permute-start.10) | collective-permute-done | bytes 524320 | tf_op jit(solution)/shard_map/high_ahead/ppermute | solution.py:285
  53.0 1.6 %collective-permute-start.14 = (bf16[2048,128]{1,0:T(8,128)(2,1)}, bf16[2048,128]{1,0:T(8,128)(2,1)S(1)}, u32[]{:S(2)}, u32[]{:S(2)}) collective-permute-start(bf16[2048,128]{1,0:T(8,128)(2,1)} %collective-permute-done.11.refs_5_), channel_id=1, source_target_pairs={{4,0},{8,4},{12,8},{14,12},{10,14},{6,10},{2,6},{0,2},{5,1},{9,5},... | collective-permute-start | bytes 1572872 | tf_op jit(solution)/shard_map/low_back/ppermute | solution.py:285
  54.6 5.1 %product.4.refs_9_ = f32[16,128,1024]{2,1,0:T(8,128)S(1)} custom-call(s32[8]{0:T(128)S(1)} %get-tuple-element.33.refs_0_, s32[2,16]{1,0:T(2,128)S(1)} %get-tuple-element.36.refs_1_, s32[2,16]{1,0:T(2,128)S(1)} %get-tuple-element.35.refs_2_, bf16[2064,128]{1,0:T(8,128)(2,1)S(1)} %collective-permute-done.1.refs_3_, ...), custom_call_target="tpu_custom_call", output_to_operand_aliasing={{}: (9, {})} | custom-call | tf_op jit(solution)/shard_map/product/pallas_call | solution.py:148
  59.7 4.4 %collective-permute-done.8.refs_3_ = bf16[2064,128]{1,0:T(8,128)(2,1)S(1)} collective-permute-done((bf16[2064,128]{1,0:T(8,128)(2,1)S(1)}, bf16[2064,128]{1,0:T(8,128)(2,1)S(1)}, u32[]{:S(2)}, u32[]{:S(2)}) %collective-permute-start.8) | collective-permute-done | bytes 528416 | tf_op jit(solution)/shard_map/low_ahead/ppermute | solution.py:285
  64.2 2.1 %collective-permute-start.12 = (bf16[1552,128]{1,0:T(8,128)(2,1)S(1)}, bf16[1552,128]{1,0:T(8,128)(2,1)S(1)}, u32[]{:S(2)}, u32[]{:S(2)}) collective-permute-start(bf16[1552,128]{1,0:T(8,128)(2,1)S(1)} %slice.67), channel_id=1, source_target_pairs={{0,4},{4,8},{8,12},{12,14},{14,10},{10,6},{6,2},{2,0},{1,5},{5,9},... | collective-permute-start | bytes 1191944 | tf_op jit(solution)/shard_map/far_low_ahead/ppermute | solution.py:285
  66.4 2.0 %collective-permute-start.16 = (bf16[768,128]{1,0:T(8,128)(2,1)S(1)}, bf16[768,128]{1,0:T(8,128)(2,1)S(1)}, u32[]{:S(2)}, u32[]{:S(2)}) collective-permute-start(bf16[768,128]{1,0:T(8,128)(2,1)S(1)} %slice.72), channel_id=1, source_target_pairs={{4,0},{8,4},{12,8},{14,12},{10,14},{6,10},{2,6},{0,2},{5,1},{9,5},... | collective-permute-start | bytes 589832 | tf_op jit(solution)/shard_map/last_high_back/ppermute | solution.py:285
  68.4 6.9 %collective-permute-done.13.refs_4_ = bf16[2048,128]{1,0:T(8,128)(2,1)S(1)} collective-permute-done((bf16[2048,128]{1,0:T(8,128)(2,1)}, bf16[2048,128]{1,0:T(8,128)(2,1)S(1)}, u32[]{:S(2)}, u32[]{:S(2)}) %collective-permute-start.13) | collective-permute-done | bytes 524320 | tf_op jit(solution)/shard_map/high_ahead/ppermute | solution.py:285
  75.4 3.9 %product.5.total = f32[16,128,1024]{2,1,0:T(8,128)S(1)} custom-call(s32[8]{0:T(128)S(1)} %get-tuple-element.33.refs_0_, s32[2,16]{1,0:T(2,128)S(1)} %slice_convert_fusion.4.refs_1_, s32[2,16]{1,0:T(2,128)S(1)} %slice_convert_fusion.3.refs_2_, bf16[2064,128]{1,0:T(8,128)(2,1)S(1)} %collective-permute-done.8.refs_3_, ...), custom_call_target="tpu_custom_call", output_to_operand_aliasing={{}: (9, {})} | custom-call | tf_op jit(solution)/shard_map/product/pallas_call | solution.py:148
  79.4 4.4 %collective-permute-done.12.refs_0_ = bf16[1552,128]{1,0:T(8,128)(2,1)S(1)} collective-permute-done((bf16[1552,128]{1,0:T(8,128)(2,1)S(1)}, bf16[1552,128]{1,0:T(8,128)(2,1)S(1)}, u32[]{:S(2)}, u32[]{:S(2)}) %collective-permute-start.12) | collective-permute-done | bytes 397344 | tf_op jit(solution)/shard_map/far_low_ahead/ppermute | solution.py:285
  83.8 2.0 %finish.2.refs_2_ = bf16[16,1,8,128,128]{4,3,2,1,0:T(8,128)(2,1)} custom-call(s32[1,8]{1,0:T(1,128)S(1)} %get-tuple-element.34.cycle_ref, s32[2,16]{1,0:T(2,128)S(1)} %slice_convert_fusion.index_ref, bf16[8,4,128,1024]{3,2,1,0:T(8,128)(2,1)S(1)} %densify.1.refs_10_.refs_11_.refs_12_.refs_7_.refs_8_.right, f32[16,128,1024]{2,1,0:T(8,128)S(1)} %product.5.total, ...), custom_call_target="tpu_custom_call" | custom-call | tf_op jit(solution)/shard_map/finish/pallas_call | solution.py:206
  86.1 1.4 %finish.3 = bf16[16,1,8,128,128]{4,3,2,1,0:T(8,128)(2,1)} custom-call(s32[1,8]{1,0:T(1,128)S(1)} %get-tuple-element.34.cycle_ref, s32[2,16]{1,0:T(2,128)S(1)} %slice_convert_fusion.index_ref, bf16[8,4,128,1024]{3,2,1,0:T(8,128)(2,1)S(1)} %densify.1.refs_10_.refs_11_.refs_12_.refs_7_.refs_8_.right, ...), custom_call_target="tpu_custom_call", output_to_operand_aliasing={{}: (6, {})} | custom-call | tf_op jit(solution)/shard_map/finish/pallas_call | solution.py:206
  (45 shorter events, 4.9 us)
Async XLA Ops:
  0.0 42.8 %copy-start.5 = (s32[16,1,2]{0,2,1:T(2,128)S(1)}, s32[16,1,2]{0,2,1:T(2,128)}, u32[]{:S(2)}) copy-start(s32[16,1,2]{0,2,1:T(2,128)} %param.6) | copy-start | bytes 388
  1.3 7.6 %copy-start.1 = (bf16[2064,128]{1,0:T(8,128)(2,1)}, bf16[2064,128]{1,0:T(8,128)(2,1)S(1)}, u32[]{:S(2)}) copy-start(bf16[2064,128]{1,0:T(8,128)(2,1)S(1)} %get-tuple-element.20.refs_4_) | copy-start | bytes 1585156
  1.3 18.2 %copy-start.3 = (bf16[2064,128]{1,0:T(8,128)(2,1)}, bf16[2064,128]{1,0:T(8,128)(2,1)S(1)}, u32[]{:S(2)}) copy-start(bf16[2064,128]{1,0:T(8,128)(2,1)S(1)} %get-tuple-element.21.refs_5_) | copy-start | bytes 1585156
  1.3 32.0 %collective-permute-start.6 = (bf16[16,4,128,128]{3,2,1,0:T(8,128)(2,1)}, bf16[16,4,128,128]{3,2,1,0:T(8,128)(2,1)S(1)}, u32[]{:S(2)}, u32[]{:S(2)}) collective-permute-start(bf16[16,4,128,128]{3,2,1,0:T(8,128)(2,1)} %bitcast.12), channel_id=1, source_target_pairs={{0,1},{1,0},{2,3},{3,2},{4,5},{5,4},{6,7},{7,6},{8,9},{9,8},{10,11... | collective-permute-start | bytes 6291464 | tf_op jit(solution)/shard_map/ppermute | solution.py:300
  1.8 17.7 %collective-permute-start.2 = (bf16[2064,128]{1,0:T(8,128)(2,1)S(1)}, bf16[2064,128]{1,0:T(8,128)(2,1)}, u32[]{:S(2)}, u32[]{:S(2)}) collective-permute-start(bf16[2064,128]{1,0:T(8,128)(2,1)S(1)} %get-tuple-element.21.refs_5_), channel_id=1, source_target_pairs={{4,0},{8,4},{12,8},{14,12},{10,14},{6,10},{2,6},{0,2},{5,1},{9,5},... | collective-permute-start | bytes 1585160 | tf_op jit(solution)/shard_map/high_back/ppermute | solution.py:285
  4.4 15.0 %collective-permute-start = (bf16[2064,128]{1,0:T(8,128)(2,1)S(1)}, bf16[2064,128]{1,0:T(8,128)(2,1)}, u32[]{:S(2)}, u32[]{:S(2)}) collective-permute-start(bf16[2064,128]{1,0:T(8,128)(2,1)S(1)} %get-tuple-element.20.refs_4_), channel_id=1, source_target_pairs={{0,4},{4,8},{8,12},{12,14},{14,10},{10,6},{6,2},{2,0},{1,5},{5,9},... | collective-permute-start | bytes 1585160 | tf_op jit(solution)/shard_map/low_ahead/ppermute | solution.py:285
  6.8 23.8 %collective-permute-start.4 = (bf16[2048,128]{1,0:T(8,128)(2,1)}, bf16[2048,128]{1,0:T(8,128)(2,1)}, u32[]{:S(2)}, u32[]{:S(2)}) collective-permute-start(bf16[2048,128]{1,0:T(8,128)(2,1)} %bitcast.5), channel_id=1, source_target_pairs={{0,4},{4,8},{8,12},{12,14},{14,10},{10,6},{6,2},{2,0},{1,5},{5,9},... | collective-permute-start | bytes 1572872 | tf_op jit(solution)/shard_map/high_ahead/ppermute | solution.py:285
  8.8 21.9 %collective-permute-start.5 = (bf16[2048,128]{1,0:T(8,128)(2,1)}, bf16[2048,128]{1,0:T(8,128)(2,1)}, u32[]{:S(2)}, u32[]{:S(2)}) collective-permute-start(bf16[2048,128]{1,0:T(8,128)(2,1)} %bitcast.6), channel_id=1, source_target_pairs={{4,0},{8,4},{12,8},{14,12},{10,14},{6,10},{2,6},{0,2},{5,1},{9,5},... | collective-permute-start | bytes 1572872 | tf_op jit(solution)/shard_map/low_back/ppermute | solution.py:285
  19.4 29.8 %collective-permute-start.1 = (bf16[2064,128]{1,0:T(8,128)(2,1)}, bf16[2064,128]{1,0:T(8,128)(2,1)S(1)}, u32[]{:S(2)}, u32[]{:S(2)}) collective-permute-start(bf16[2064,128]{1,0:T(8,128)(2,1)} %collective-permute-done.refs_6_), channel_id=1, source_target_pairs={{0,4},{4,8},{8,12},{12,14},{14,10},{10,6},{6,2},{2,0},{1,5},{5,9},... | collective-permute-start | bytes 1585160 | tf_op jit(solution)/shard_map/low_ahead/ppermute | solution.py:285
  19.5 29.7 %collective-permute-start.3 = (bf16[2064,128]{1,0:T(8,128)(2,1)}, bf16[2064,128]{1,0:T(8,128)(2,1)S(1)}, u32[]{:S(2)}, u32[]{:S(2)}) collective-permute-start(bf16[2064,128]{1,0:T(8,128)(2,1)} %collective-permute-done.2.refs_9_), channel_id=1, source_target_pairs={{4,0},{8,4},{12,8},{14,12},{10,14},{6,10},{2,6},{0,2},{5,1},{9,5},... | collective-permute-start | bytes 1585160 | tf_op jit(solution)/shard_map/high_back/ppermute | solution.py:285
  30.6 22.0 %collective-permute-start.10 = (bf16[2048,128]{1,0:T(8,128)(2,1)}, bf16[2048,128]{1,0:T(8,128)(2,1)}, u32[]{:S(2)}, u32[]{:S(2)}) collective-permute-start(bf16[2048,128]{1,0:T(8,128)(2,1)} %collective-permute-done.4.refs_7_), channel_id=1, source_target_pairs={{0,4},{4,8},{8,12},{12,14},{14,10},{10,6},{6,2},{2,0},{1,5},{5,9},... | collective-permute-start | bytes 1572872 | tf_op jit(solution)/shard_map/high_ahead/ppermute | solution.py:285
  30.7 22.3 %collective-permute-start.11 = (bf16[2048,128]{1,0:T(8,128)(2,1)}, bf16[2048,128]{1,0:T(8,128)(2,1)}, u32[]{:S(2)}, u32[]{:S(2)}) collective-permute-start(bf16[2048,128]{1,0:T(8,128)(2,1)} %collective-permute-done.5.refs_8_), channel_id=1, source_target_pairs={{4,0},{8,4},{12,8},{14,12},{10,14},{6,10},{2,6},{0,2},{5,1},{9,5},... | collective-permute-start | bytes 1572872 | tf_op jit(solution)/shard_map/low_back/ppermute | solution.py:285
  34.1 1.2 %collective-permute-start.7 = (s32[64]{0:T(128)S(1)}, s32[64]{0:T(128)S(1)}, u32[]{:S(2)}, u32[]{:S(2)}) collective-permute-start(s32[64]{0:T(128)S(1)} %reshape.9.own_index), channel_id=1, source_target_pairs={{0,1},{1,0},{2,3},{3,2},{4,5},{5,4},{6,7},{7,6},{8,9},{9,8},{10,11... | collective-permute-start | bytes 776 | tf_op jit(solution)/shard_map/ppermute | solution.py:302
  35.3 1.6 %copy-start = (bf16[16,1,4,128,128]{4,3,2,1,0:T(8,128)(2,1)S(1)}, bf16[16,1,4,128,128]{4,3,2,1,0:T(8,128)(2,1)}, u32[]{:S(2)}) copy-start(bf16[16,1,4,128,128]{4,3,2,1,0:T(8,128)(2,1)} %param.7) | copy-start | bytes 6291460
  36.9 5.9 %copy-start.2 = (bf16[2064,128]{1,0:T(8,128)(2,1)S(1)}, bf16[2064,128]{1,0:T(8,128)(2,1)}, u32[]{:S(2)}) copy-start(bf16[2064,128]{1,0:T(8,128)(2,1)} %copy-done.1) | copy-start | bytes 1585156
  36.9 5.9 %copy-start.4 = (bf16[2064,128]{1,0:T(8,128)(2,1)S(1)}, bf16[2064,128]{1,0:T(8,128)(2,1)}, u32[]{:S(2)}) copy-start(bf16[2064,128]{1,0:T(8,128)(2,1)} %copy-done.3) | copy-start | bytes 1585156
  49.2 14.9 %collective-permute-start.8 = (bf16[2064,128]{1,0:T(8,128)(2,1)S(1)}, bf16[2064,128]{1,0:T(8,128)(2,1)S(1)}, u32[]{:S(2)}, u32[]{:S(2)}) collective-permute-start(bf16[2064,128]{1,0:T(8,128)(2,1)S(1)} %collective-permute-done.1.refs_3_), channel_id=1, source_target_pairs={{0,4},{4,8},{8,12},{12,14},{14,10},{10,6},{6,2},{2,0},{1,5},{5,9},... | collective-permute-start | bytes 1585160 | tf_op jit(solution)/shard_map/low_ahead/ppermute | solution.py:285
  49.3 14.9 %collective-permute-start.9 = (bf16[2064,128]{1,0:T(8,128)(2,1)S(1)}, bf16[2064,128]{1,0:T(8,128)(2,1)S(1)}, u32[]{:S(2)}, u32[]{:S(2)}) collective-permute-start(bf16[2064,128]{1,0:T(8,128)(2,1)S(1)} %collective-permute-done.3.refs_6_), channel_id=1, source_target_pairs={{4,0},{8,4},{12,8},{14,12},{10,14},{6,10},{2,6},{0,2},{5,1},{9,5},... | collective-permute-start | bytes 1585160 | tf_op jit(solution)/shard_map/high_back/ppermute | solution.py:285
  52.6 22.7 %collective-permute-start.13 = (bf16[2048,128]{1,0:T(8,128)(2,1)}, bf16[2048,128]{1,0:T(8,128)(2,1)S(1)}, u32[]{:S(2)}, u32[]{:S(2)}) collective-permute-start(bf16[2048,128]{1,0:T(8,128)(2,1)} %collective-permute-done.10.refs_4_), channel_id=1, source_target_pairs={{0,4},{4,8},{8,12},{12,14},{14,10},{10,6},{6,2},{2,0},{1,5},{5,9},... | collective-permute-start | bytes 1572872 | tf_op jit(solution)/shard_map/high_ahead/ppermute | solution.py:285
  53.0 22.5 %collective-permute-start.14 = (bf16[2048,128]{1,0:T(8,128)(2,1)}, bf16[2048,128]{1,0:T(8,128)(2,1)S(1)}, u32[]{:S(2)}, u32[]{:S(2)}) collective-permute-start(bf16[2048,128]{1,0:T(8,128)(2,1)} %collective-permute-done.11.refs_5_), channel_id=1, source_target_pairs={{4,0},{8,4},{12,8},{14,12},{10,14},{6,10},{2,6},{0,2},{5,1},{9,5},... | collective-permute-start | bytes 1572872 | tf_op jit(solution)/shard_map/low_back/ppermute | solution.py:285
  64.2 19.6 %collective-permute-start.12 = (bf16[1552,128]{1,0:T(8,128)(2,1)S(1)}, bf16[1552,128]{1,0:T(8,128)(2,1)S(1)}, u32[]{:S(2)}, u32[]{:S(2)}) collective-permute-start(bf16[1552,128]{1,0:T(8,128)(2,1)S(1)} %slice.67), channel_id=1, source_target_pairs={{0,4},{4,8},{8,12},{12,14},{14,10},{10,6},{6,2},{2,0},{1,5},{5,9},... | collective-permute-start | bytes 1191944 | tf_op jit(solution)/shard_map/far_low_ahead/ppermute | solution.py:285
  66.3 17.5 %collective-permute-start.17 = (bf16[1280,128]{1,0:T(8,128)(2,1)S(1)}, bf16[1280,128]{1,0:T(8,128)(2,1)S(1)}, u32[]{:S(2)}, u32[]{:S(2)}) collective-permute-start(bf16[1280,128]{1,0:T(8,128)(2,1)S(1)} %slice.73), channel_id=1, source_target_pairs={{4,0},{8,4},{12,8},{14,12},{10,14},{6,10},{2,6},{0,2},{5,1},{9,5},... | collective-permute-start | bytes 983048 | tf_op jit(solution)/shard_map/far_high_back/ppermute | solution.py:285
  66.4 19.7 %collective-permute-start.16 = (bf16[768,128]{1,0:T(8,128)(2,1)S(1)}, bf16[768,128]{1,0:T(8,128)(2,1)S(1)}, u32[]{:S(2)}, u32[]{:S(2)}) collective-permute-start(bf16[768,128]{1,0:T(8,128)(2,1)S(1)} %slice.72), channel_id=1, source_target_pairs={{4,0},{8,4},{12,8},{14,12},{10,14},{6,10},{2,6},{0,2},{5,1},{9,5},... | collective-permute-start | bytes 589832 | tf_op jit(solution)/shard_map/last_high_back/ppermute | solution.py:285
  75.3 10.9 %collective-permute-start.15 = (bf16[512,128]{1,0:T(8,128)(2,1)S(1)}, bf16[512,128]{1,0:T(8,128)(2,1)S(1)}, u32[]{:S(2)}, u32[]{:S(2)}) collective-permute-start(bf16[512,128]{1,0:T(8,128)(2,1)S(1)} %slice.71), channel_id=1, source_target_pairs={{0,4},{4,8},{8,12},{12,14},{14,10},{10,6},{6,2},{2,0},{1,5},{5,9},... | collective-permute-start | bytes 393224 | tf_op jit(solution)/shard_map/last_low_ahead/ppermute | solution.py:285

commit v9 on v7

--- a/solution.py
+++ b/solution.py
@@ -187,8 +187,14 @@
             result = (total[row, :, columns] + term).astype(jnp.bfloat16)
             for j in range(2):
                 staged[at, c * 2 + j] = result[:, j * blk : (j + 1) * blk]
-        copies.append(pltpu.make_async_copy(staged.at[at], out_ref.at[row, 0], sems.at[at]))
-        copies[-1].start()
+            if c % 2 == 1:
+                part = pl.ds(c * 2 - 2, 4)
+                copies.append(
+                    pltpu.make_async_copy(
+                        staged.at[at, part], out_ref.at[row, 0, part], sems.at[at, c // 2]
+                    )
+                )
+                copies[-1].start()
     for copy in copies:
         copy.wait()
 
@@ -210,7 +216,7 @@
         out_specs=pl.BlockSpec(memory_space=pl.ANY),
         scratch_shapes=[
             pltpu.VMEM((len(parts), BJ, blk, blk), jnp.bfloat16),
-            pltpu.SemaphoreType.DMA((len(parts),)),
+            pltpu.SemaphoreType.DMA((len(parts), 2)),
         ],
         input_output_aliases=aliases,
         compiler_params=pltpu.CompilerParams(vmem_limit_bytes=VMEM_LIMIT // 2),

time: 87.9 us -> 87.9 us (level)
  no operation moved by 1% of the time
where the time goes in v9:
time: 87.9 us; the launch traced here: 87.5 us
  waiting for transfers between devices  35.4 us (40%)
  Pallas kernels  25.9 us (29%)
  starting transfers between devices  19.1 us (22%)
  local copies, waits for them, and re-layouts  5.51 us (6%)
  other arithmetic  1.37 us (2%)
    ppermute x16, waiting for transfers between devices, move(): return lax.ppermute(array, 'row', way)  35 us
    ppermute x16, starting transfers between devices, move(): return lax.ppermute(array, 'row', way)  18.6 us
    pallas_call x3, Pallas kernels, product(): pl.pallas_call(functools.partial(product_kernel, offsets, sides, starts,...  15.2 us
    pallas_call x1, Pallas kernels, densify(): pl.pallas_call(densify_kernel, out_shape=jax.ShapeDtypeStruct((2 * pieces...  5.9 us
    pallas_call x2, Pallas kernels, finish(): pl.pallas_call(functools.partial(finish_kernel, parts, offset), out_shape...  3.51 us
    slice x1, local copies, waits for them, and re-layouts, body(): low_second, high_second = (flat[:cut], flat[cut:])  2.28 us
  transfers between devices with their start and end apart: 18, of which 9 were waited for; matrix products, arithmetic and copies ran while one was open for 6% of the time, Pallas kernels for 27%

profile of v9, /device:TPU:0, one launch (start us, length us, event | category | flops | bytes accessed | tf_op | source)
XLA Modules:
  0.0 87.5 jit_solution(16780007068328220038)
XLA Ops:
  0.0 1.3 %pack.1 = (bf16[2064,128]{1,0:T(8,128)(2,1)S(1)}, bf16[2064,128]{1,0:T(8,128)(2,1)S(1)}) custom-call(bf16[4096,128]{1,0:T(8,128)(2,1)} %bitcast.16, s32[2,16]{1,0:T(2,128)} %bitcast.14), custom_call_target="tpu_custom_call" | custom-call | tf_op jit(solution)/shard_map/pack/pallas_call | solution.py:253
  1.8 2.6 %collective-permute-start.2 = (bf16[2064,128]{1,0:T(8,128)(2,1)S(1)}, bf16[2064,128]{1,0:T(8,128)(2,1)}, u32[]{:S(2)}, u32[]{:S(2)}) collective-permute-start(bf16[2064,128]{1,0:T(8,128)(2,1)S(1)} %get-tuple-element.21.refs_5_), channel_id=1, source_target_pairs={{4,0},{8,4},{12,8},{14,12},{10,14},{6,10},{2,6},{0,2},{5,1},{9,5},... | collective-permute-start | bytes 1585160 | tf_op jit(solution)/shard_map/high_back/ppermute | solution.py:291
  4.5 2.3 %fusion.1 = (bf16[8,1,2,128,128]{4,3,2,1,0:T(8,128)(2,1)}, bf16[8,1,2,128,128]{4,3,2,1,0:T(8,128)(2,1)}) fusion(bf16[16,1,2,128,128]{4,3,2,1,0:T(8,128)(2,1)} %param.5), kind=kLoop, calls=%fused_computation.9 | loop fusion | bytes 2097152 | tf_op jit(solution)/shard_map/slice | solution.py:284
  6.8 1.9 %collective-permute-start.4 = (bf16[2048,128]{1,0:T(8,128)(2,1)}, bf16[2048,128]{1,0:T(8,128)(2,1)}, u32[]{:S(2)}, u32[]{:S(2)}) collective-permute-start(bf16[2048,128]{1,0:T(8,128)(2,1)} %bitcast.5), channel_id=1, source_target_pairs={{0,4},{4,8},{8,12},{12,14},{14,10},{10,6},{6,2},{2,0},{1,5},{5,9},... | collective-permute-start | bytes 1572872 | tf_op jit(solution)/shard_map/high_ahead/ppermute | solution.py:291
  8.8 10.5 %collective-permute-done.refs_6_ = bf16[2064,128]{1,0:T(8,128)(2,1)} collective-permute-done((bf16[2064,128]{1,0:T(8,128)(2,1)S(1)}, bf16[2064,128]{1,0:T(8,128)(2,1)}, u32[]{:S(2)}, u32[]{:S(2)}) %collective-permute-start) | collective-permute-done | bytes 528416 | tf_op jit(solution)/shard_map/low_ahead/ppermute | solution.py:291
  19.5 1.9 %collective-permute-start.3 = (bf16[2064,128]{1,0:T(8,128)(2,1)}, bf16[2064,128]{1,0:T(8,128)(2,1)S(1)}, u32[]{:S(2)}, u32[]{:S(2)}) collective-permute-start(bf16[2064,128]{1,0:T(8,128)(2,1)} %collective-permute-done.2.refs_9_), channel_id=1, source_target_pairs={{4,0},{8,4},{12,8},{14,12},{10,14},{6,10},{2,6},{0,2},{5,1},{9,5},... | collective-permute-start | bytes 1585160 | tf_op jit(solution)/shard_map/high_back/ppermute | solution.py:291
  22.1 8.5 %collective-permute-done.4.refs_7_ = bf16[2048,128]{1,0:T(8,128)(2,1)} collective-permute-done((bf16[2048,128]{1,0:T(8,128)(2,1)}, bf16[2048,128]{1,0:T(8,128)(2,1)}, u32[]{:S(2)}, u32[]{:S(2)}) %collective-permute-start.4) | collective-permute-done | bytes 524320 | tf_op jit(solution)/shard_map/high_ahead/ppermute | solution.py:291
  30.7 1.9 %collective-permute-start.11 = (bf16[2048,128]{1,0:T(8,128)(2,1)}, bf16[2048,128]{1,0:T(8,128)(2,1)}, u32[]{:S(2)}, u32[]{:S(2)}) collective-permute-start(bf16[2048,128]{1,0:T(8,128)(2,1)} %collective-permute-done.5.refs_8_), channel_id=1, source_target_pairs={{4,0},{8,4},{12,8},{14,12},{10,14},{6,10},{2,6},{0,2},{5,1},{9,5},... | collective-permute-start | bytes 1572872 | tf_op jit(solution)/shard_map/low_back/ppermute | solution.py:291
  35.3 1.6 %copy-done = bf16[16,1,4,128,128]{4,3,2,1,0:T(8,128)(2,1)S(1)} copy-done((bf16[16,1,4,128,128]{4,3,2,1,0:T(8,128)(2,1)S(1)}, bf16[16,1,4,128,128]{4,3,2,1,0:T(8,128)(2,1)}, u32[]{:S(2)}) %copy-start) | copy-done | bytes 2097176
  36.9 5.9 %densify.1.refs_10_.refs_11_.refs_12_.refs_7_.refs_8_.right = bf16[8,4,128,1024]{3,2,1,0:T(8,128)(2,1)S(1)} custom-call(s32[1]{0:T(128)} %bitcast.7.col_ref, s32[64]{0:T(128)S(1)} %reshape.9.own_index, s32[64]{0:T(128)S(1)} %collective-permute-done.7.other_index, bf16[16,4,128,128]{3,2,1,0:T(8,128)(2,1)S(1)} %bitcast.13, ...), custom_call_target="tpu_custom_call" | custom-call | tf_op jit(solution)/shard_map/densify/pallas_call | solution.py:44
  42.9 6.3 %product.3.refs_9_ = f32[16,128,1024]{2,1,0:T(8,128)S(1)} custom-call(s32[8]{0:T(128)S(1)} %get-tuple-element.33.refs_0_, s32[2,16]{1,0:T(2,128)S(1)} %bitcast.15, s32[2,16]{1,0:T(2,128)S(1)} %slice_convert_fusion.2.refs_2_, s32[2,16]{1,0:T(2,128)S(1)} %slice_convert_fusion.1.refs_3_, bf16[2064,128]{1,0:T(8,128)(2,1)S(1)} %copy-done.2, ...), custom_call_target="tpu_custom_call" | custom-call | tf_op jit(solution)/shard_map/product/pallas_call | solution.py:148
  49.3 1.9 %collective-permute-start.9 = (bf16[2064,128]{1,0:T(8,128)(2,1)S(1)}, bf16[2064,128]{1,0:T(8,128)(2,1)S(1)}, u32[]{:S(2)}, u32[]{:S(2)}) collective-permute-start(bf16[2064,128]{1,0:T(8,128)(2,1)S(1)} %collective-permute-done.3.refs_6_), channel_id=1, source_target_pairs={{4,0},{8,4},{12,8},{14,12},{10,14},{6,10},{2,6},{0,2},{5,1},{9,5},... | collective-permute-start | bytes 1585160 | tf_op jit(solution)/shard_map/high_back/ppermute | solution.py:291
  51.2 1.3 %collective-permute-done.10.refs_4_ = bf16[2048,128]{1,0:T(8,128)(2,1)} collective-permute-done((bf16[2048,128]{1,0:T(8,128)(2,1)}, bf16[2048,128]{1,0:T(8,128)(2,1)}, u32[]{:S(2)}, u32[]{:S(2)}) %collective-permute-start.10) | collective-permute-done | bytes 524320 | tf_op jit(solution)/shard_map/high_ahead/ppermute | solution.py:291
  53.0 1.6 %collective-permute-start.14 = (bf16[2048,128]{1,0:T(8,128)(2,1)}, bf16[2048,128]{1,0:T(8,128)(2,1)S(1)}, u32[]{:S(2)}, u32[]{:S(2)}) collective-permute-start(bf16[2048,128]{1,0:T(8,128)(2,1)} %collective-permute-done.11.refs_5_), channel_id=1, source_target_pairs={{4,0},{8,4},{12,8},{14,12},{10,14},{6,10},{2,6},{0,2},{5,1},{9,5},... | collective-permute-start | bytes 1572872 | tf_op jit(solution)/shard_map/low_back/ppermute | solution.py:291
  54.6 5.1 %product.4.refs_9_ = f32[16,128,1024]{2,1,0:T(8,128)S(1)} custom-call(s32[8]{0:T(128)S(1)} %get-tuple-element.33.refs_0_, s32[2,16]{1,0:T(2,128)S(1)} %get-tuple-element.36.refs_1_, s32[2,16]{1,0:T(2,128)S(1)} %get-tuple-element.35.refs_2_, bf16[2064,128]{1,0:T(8,128)(2,1)S(1)} %collective-permute-done.1.refs_3_, ...), custom_call_target="tpu_custom_call", output_to_operand_aliasing={{}: (9, {})} | custom-call | tf_op jit(solution)/shard_map/product/pallas_call | solution.py:148
  59.7 4.4 %collective-permute-done.8.refs_3_ = bf16[2064,128]{1,0:T(8,128)(2,1)S(1)} collective-permute-done((bf16[2064,128]{1,0:T(8,128)(2,1)S(1)}, bf16[2064,128]{1,0:T(8,128)(2,1)S(1)}, u32[]{:S(2)}, u32[]{:S(2)}) %collective-permute-start.8) | collective-permute-done | bytes 528416 | tf_op jit(solution)/shard_map/low_ahead/ppermute | solution.py:291
  64.3 2.1 %collective-permute-start.12 = (bf16[1552,128]{1,0:T(8,128)(2,1)S(1)}, bf16[1552,128]{1,0:T(8,128)(2,1)S(1)}, u32[]{:S(2)}, u32[]{:S(2)}) collective-permute-start(bf16[1552,128]{1,0:T(8,128)(2,1)S(1)} %slice.67), channel_id=1, source_target_pairs={{0,4},{4,8},{8,12},{12,14},{14,10},{10,6},{6,2},{2,0},{1,5},{5,9},... | collective-permute-start | bytes 1191944 | tf_op jit(solution)/shard_map/far_low_ahead/ppermute | solution.py:291
  66.4 2.0 %collective-permute-start.15 = (bf16[512,128]{1,0:T(8,128)(2,1)S(1)}, bf16[512,128]{1,0:T(8,128)(2,1)S(1)}, u32[]{:S(2)}, u32[]{:S(2)}) collective-permute-start(bf16[512,128]{1,0:T(8,128)(2,1)S(1)} %slice.71), channel_id=1, source_target_pairs={{0,4},{4,8},{8,12},{12,14},{14,10},{10,6},{6,2},{2,0},{1,5},{5,9},... | collective-permute-start | bytes 393224 | tf_op jit(solution)/shard_map/last_low_ahead/ppermute | solution.py:291
  68.4 6.9 %collective-permute-done.13.refs_4_ = bf16[2048,128]{1,0:T(8,128)(2,1)S(1)} collective-permute-done((bf16[2048,128]{1,0:T(8,128)(2,1)}, bf16[2048,128]{1,0:T(8,128)(2,1)S(1)}, u32[]{:S(2)}, u32[]{:S(2)}) %collective-permute-start.13) | collective-permute-done | bytes 524320 | tf_op jit(solution)/shard_map/high_ahead/ppermute | solution.py:291
  75.3 1.6 %collective-permute-start.16 = (bf16[512,128]{1,0:T(8,128)(2,1)S(1)}, bf16[512,128]{1,0:T(8,128)(2,1)S(1)}, u32[]{:S(2)}, u32[]{:S(2)}) collective-permute-start(bf16[512,128]{1,0:T(8,128)(2,1)S(1)} %slice.72), channel_id=1, source_target_pairs={{4,0},{8,4},{12,8},{14,12},{10,14},{6,10},{2,6},{0,2},{5,1},{9,5},... | collective-permute-start | bytes 393224 | tf_op jit(solution)/shard_map/last_high_back/ppermute | solution.py:291
  76.9 3.9 %product.5.total = f32[16,128,1024]{2,1,0:T(8,128)S(1)} custom-call(s32[8]{0:T(128)S(1)} %get-tuple-element.33.refs_0_, s32[2,16]{1,0:T(2,128)S(1)} %slice_convert_fusion.4.refs_1_, s32[2,16]{1,0:T(2,128)S(1)} %slice_convert_fusion.3.refs_2_, bf16[2064,128]{1,0:T(8,128)(2,1)S(1)} %collective-permute-done.8.refs_3_, ...), custom_call_target="tpu_custom_call", output_to_operand_aliasing={{}: (9, {})} | custom-call | tf_op jit(solution)/shard_map/product/pallas_call | solution.py:148
  80.8 3.0 %collective-permute-done.12.refs_0_ = bf16[1552,128]{1,0:T(8,128)(2,1)S(1)} collective-permute-done((bf16[1552,128]{1,0:T(8,128)(2,1)S(1)}, bf16[1552,128]{1,0:T(8,128)(2,1)S(1)}, u32[]{:S(2)}, u32[]{:S(2)}) %collective-permute-start.12) | collective-permute-done | bytes 397344 | tf_op jit(solution)/shard_map/far_low_ahead/ppermute | solution.py:291
  83.8 2.2 %finish.2.refs_2_ = bf16[16,1,8,128,128]{4,3,2,1,0:T(8,128)(2,1)} custom-call(s32[1,8]{1,0:T(1,128)S(1)} %get-tuple-element.34.cycle_ref, s32[2,16]{1,0:T(2,128)S(1)} %slice_convert_fusion.index_ref, bf16[8,4,128,1024]{3,2,1,0:T(8,128)(2,1)S(1)} %densify.1.refs_10_.refs_11_.refs_12_.refs_7_.refs_8_.right, f32[16,128,1024]{2,1,0:T(8,128)S(1)} %product.5.total, ...), custom_call_target="tpu_custom_call" | custom-call | tf_op jit(solution)/shard_map/finish/pallas_call | solution.py:212
  86.1 1.3 %finish.3 = bf16[16,1,8,128,128]{4,3,2,1,0:T(8,128)(2,1)} custom-call(s32[1,8]{1,0:T(1,128)S(1)} %get-tuple-element.34.cycle_ref, s32[2,16]{1,0:T(2,128)S(1)} %slice_convert_fusion.index_ref, bf16[8,4,128,1024]{3,2,1,0:T(8,128)(2,1)S(1)} %densify.1.refs_10_.refs_11_.refs_12_.refs_7_.refs_8_.right, ...), custom_call_target="tpu_custom_call", output_to_operand_aliasing={{}: (6, {})} | custom-call | tf_op jit(solution)/shard_map/finish/pallas_call | solution.py:212
  (45 shorter events, 5.3 us)
Async XLA Ops:
  0.0 42.8 %copy-start.5 = (s32[16,1,2]{0,2,1:T(2,128)S(1)}, s32[16,1,2]{0,2,1:T(2,128)}, u32[]{:S(2)}) copy-start(s32[16,1,2]{0,2,1:T(2,128)} %param.6) | copy-start | bytes 388
  1.3 7.6 %copy-start.1 = (bf16[2064,128]{1,0:T(8,128)(2,1)}, bf16[2064,128]{1,0:T(8,128)(2,1)S(1)}, u32[]{:S(2)}) copy-start(bf16[2064,128]{1,0:T(8,128)(2,1)S(1)} %get-tuple-element.20.refs_4_) | copy-start | bytes 1585156
  1.3 18.2 %copy-start.3 = (bf16[2064,128]{1,0:T(8,128)(2,1)}, bf16[2064,128]{1,0:T(8,128)(2,1)S(1)}, u32[]{:S(2)}) copy-start(bf16[2064,128]{1,0:T(8,128)(2,1)S(1)} %get-tuple-element.21.refs_5_) | copy-start | bytes 1585156
  1.3 32.0 %collective-permute-start.6 = (bf16[16,4,128,128]{3,2,1,0:T(8,128)(2,1)}, bf16[16,4,128,128]{3,2,1,0:T(8,128)(2,1)S(1)}, u32[]{:S(2)}, u32[]{:S(2)}) collective-permute-start(bf16[16,4,128,128]{3,2,1,0:T(8,128)(2,1)} %bitcast.12), channel_id=1, source_target_pairs={{0,1},{1,0},{2,3},{3,2},{4,5},{5,4},{6,7},{7,6},{8,9},{9,8},{10,11... | collective-permute-start | bytes 6291464 | tf_op jit(solution)/shard_map/ppermute | solution.py:306
  1.8 17.7 %collective-permute-start.2 = (bf16[2064,128]{1,0:T(8,128)(2,1)S(1)}, bf16[2064,128]{1,0:T(8,128)(2,1)}, u32[]{:S(2)}, u32[]{:S(2)}) collective-permute-start(bf16[2064,128]{1,0:T(8,128)(2,1)S(1)} %get-tuple-element.21.refs_5_), channel_id=1, source_target_pairs={{4,0},{8,4},{12,8},{14,12},{10,14},{6,10},{2,6},{0,2},{5,1},{9,5},... | collective-permute-start | bytes 1585160 | tf_op jit(solution)/shard_map/high_back/ppermute | solution.py:291
  4.4 15.0 %collective-permute-start = (bf16[2064,128]{1,0:T(8,128)(2,1)S(1)}, bf16[2064,128]{1,0:T(8,128)(2,1)}, u32[]{:S(2)}, u32[]{:S(2)}) collective-permute-start(bf16[2064,128]{1,0:T(8,128)(2,1)S(1)} %get-tuple-element.20.refs_4_), channel_id=1, source_target_pairs={{0,4},{4,8},{8,12},{12,14},{14,10},{10,6},{6,2},{2,0},{1,5},{5,9},... | collective-permute-start | bytes 1585160 | tf_op jit(solution)/shard_map/low_ahead/ppermute | solution.py:291
  6.8 23.8 %collective-permute-start.4 = (bf16[2048,128]{1,0:T(8,128)(2,1)}, bf16[2048,128]{1,0:T(8,128)(2,1)}, u32[]{:S(2)}, u32[]{:S(2)}) collective-permute-start(bf16[2048,128]{1,0:T(8,128)(2,1)} %bitcast.5), channel_id=1, source_target_pairs={{0,4},{4,8},{8,12},{12,14},{14,10},{10,6},{6,2},{2,0},{1,5},{5,9},... | collective-permute-start | bytes 1572872 | tf_op jit(solution)/shard_map/high_ahead/ppermute | solution.py:291
  8.8 21.9 %collective-permute-start.5 = (bf16[2048,128]{1,0:T(8,128)(2,1)}, bf16[2048,128]{1,0:T(8,128)(2,1)}, u32[]{:S(2)}, u32[]{:S(2)}) collective-permute-start(bf16[2048,128]{1,0:T(8,128)(2,1)} %bitcast.6), channel_id=1, source_target_pairs={{4,0},{8,4},{12,8},{14,12},{10,14},{6,10},{2,6},{0,2},{5,1},{9,5},... | collective-permute-start | bytes 1572872 | tf_op jit(solution)/shard_map/low_back/ppermute | solution.py:291
  19.4 29.8 %collective-permute-start.1 = (bf16[2064,128]{1,0:T(8,128)(2,1)}, bf16[2064,128]{1,0:T(8,128)(2,1)S(1)}, u32[]{:S(2)}, u32[]{:S(2)}) collective-permute-start(bf16[2064,128]{1,0:T(8,128)(2,1)} %collective-permute-done.refs_6_), channel_id=1, source_target_pairs={{0,4},{4,8},{8,12},{12,14},{14,10},{10,6},{6,2},{2,0},{1,5},{5,9},... | collective-permute-start | bytes 1585160 | tf_op jit(solution)/shard_map/low_ahead/ppermute | solution.py:291
  19.5 29.7 %collective-permute-start.3 = (bf16[2064,128]{1,0:T(8,128)(2,1)}, bf16[2064,128]{1,0:T(8,128)(2,1)S(1)}, u32[]{:S(2)}, u32[]{:S(2)}) collective-permute-start(bf16[2064,128]{1,0:T(8,128)(2,1)} %collective-permute-done.2.refs_9_), channel_id=1, source_target_pairs={{4,0},{8,4},{12,8},{14,12},{10,14},{6,10},{2,6},{0,2},{5,1},{9,5},... | collective-permute-start | bytes 1585160 | tf_op jit(solution)/shard_map/high_back/ppermute | solution.py:291
  30.6 22.0 %collective-permute-start.10 = (bf16[2048,128]{1,0:T(8,128)(2,1)}, bf16[2048,128]{1,0:T(8,128)(2,1)}, u32[]{:S(2)}, u32[]{:S(2)}) collective-permute-start(bf16[2048,128]{1,0:T(8,128)(2,1)} %collective-permute-done.4.refs_7_), channel_id=1, source_target_pairs={{0,4},{4,8},{8,12},{12,14},{14,10},{10,6},{6,2},{2,0},{1,5},{5,9},... | collective-permute-start | bytes 1572872 | tf_op jit(solution)/shard_map/high_ahead/ppermute | solution.py:291
  30.7 22.3 %collective-permute-start.11 = (bf16[2048,128]{1,0:T(8,128)(2,1)}, bf16[2048,128]{1,0:T(8,128)(2,1)}, u32[]{:S(2)}, u32[]{:S(2)}) collective-permute-start(bf16[2048,128]{1,0:T(8,128)(2,1)} %collective-permute-done.5.refs_8_), channel_id=1, source_target_pairs={{4,0},{8,4},{12,8},{14,12},{10,14},{6,10},{2,6},{0,2},{5,1},{9,5},... | collective-permute-start | bytes 1572872 | tf_op jit(solution)/shard_map/low_back/ppermute | solution.py:291
  34.1 1.2 %collective-permute-start.7 = (s32[64]{0:T(128)S(1)}, s32[64]{0:T(128)S(1)}, u32[]{:S(2)}, u32[]{:S(2)}) collective-permute-start(s32[64]{0:T(128)S(1)} %reshape.9.own_index), channel_id=1, source_target_pairs={{0,1},{1,0},{2,3},{3,2},{4,5},{5,4},{6,7},{7,6},{8,9},{9,8},{10,11... | collective-permute-start | bytes 776 | tf_op jit(solution)/shard_map/ppermute | solution.py:308
  35.3 1.6 %copy-start = (bf16[16,1,4,128,128]{4,3,2,1,0:T(8,128)(2,1)S(1)}, bf16[16,1,4,128,128]{4,3,2,1,0:T(8,128)(2,1)}, u32[]{:S(2)}) copy-start(bf16[16,1,4,128,128]{4,3,2,1,0:T(8,128)(2,1)} %param.7) | copy-start | bytes 6291460
  36.9 5.9 %copy-start.2 = (bf16[2064,128]{1,0:T(8,128)(2,1)S(1)}, bf16[2064,128]{1,0:T(8,128)(2,1)}, u32[]{:S(2)}) copy-start(bf16[2064,128]{1,0:T(8,128)(2,1)} %copy-done.1) | copy-start | bytes 1585156
  36.9 5.9 %copy-start.4 = (bf16[2064,128]{1,0:T(8,128)(2,1)S(1)}, bf16[2064,128]{1,0:T(8,128)(2,1)}, u32[]{:S(2)}) copy-start(bf16[2064,128]{1,0:T(8,128)(2,1)} %copy-done.3) | copy-start | bytes 1585156
  49.2 14.9 %collective-permute-start.8 = (bf16[2064,128]{1,0:T(8,128)(2,1)S(1)}, bf16[2064,128]{1,0:T(8,128)(2,1)S(1)}, u32[]{:S(2)}, u32[]{:S(2)}) collective-permute-start(bf16[2064,128]{1,0:T(8,128)(2,1)S(1)} %collective-permute-done.1.refs_3_), channel_id=1, source_target_pairs={{0,4},{4,8},{8,12},{12,14},{14,10},{10,6},{6,2},{2,0},{1,5},{5,9},... | collective-permute-start | bytes 1585160 | tf_op jit(solution)/shard_map/low_ahead/ppermute | solution.py:291
  49.3 14.9 %collective-permute-start.9 = (bf16[2064,128]{1,0:T(8,128)(2,1)S(1)}, bf16[2064,128]{1,0:T(8,128)(2,1)S(1)}, u32[]{:S(2)}, u32[]{:S(2)}) collective-permute-start(bf16[2064,128]{1,0:T(8,128)(2,1)S(1)} %collective-permute-done.3.refs_6_), channel_id=1, source_target_pairs={{4,0},{8,4},{12,8},{14,12},{10,14},{6,10},{2,6},{0,2},{5,1},{9,5},... | collective-permute-start | bytes 1585160 | tf_op jit(solution)/shard_map/high_back/ppermute | solution.py:291
  52.6 22.7 %collective-permute-start.13 = (bf16[2048,128]{1,0:T(8,128)(2,1)}, bf16[2048,128]{1,0:T(8,128)(2,1)S(1)}, u32[]{:S(2)}, u32[]{:S(2)}) collective-permute-start(bf16[2048,128]{1,0:T(8,128)(2,1)} %collective-permute-done.10.refs_4_), channel_id=1, source_target_pairs={{0,4},{4,8},{8,12},{12,14},{14,10},{10,6},{6,2},{2,0},{1,5},{5,9},... | collective-permute-start | bytes 1572872 | tf_op jit(solution)/shard_map/high_ahead/ppermute | solution.py:291
  53.0 23.9 %collective-permute-start.14 = (bf16[2048,128]{1,0:T(8,128)(2,1)}, bf16[2048,128]{1,0:T(8,128)(2,1)S(1)}, u32[]{:S(2)}, u32[]{:S(2)}) collective-permute-start(bf16[2048,128]{1,0:T(8,128)(2,1)} %collective-permute-done.11.refs_5_), channel_id=1, source_target_pairs={{4,0},{8,4},{12,8},{14,12},{10,14},{6,10},{2,6},{0,2},{5,1},{9,5},... | collective-permute-start | bytes 1572872 | tf_op jit(solution)/shard_map/low_back/ppermute | solution.py:291
  64.3 19.5 %collective-permute-start.12 = (bf16[1552,128]{1,0:T(8,128)(2,1)S(1)}, bf16[1552,128]{1,0:T(8,128)(2,1)S(1)}, u32[]{:S(2)}, u32[]{:S(2)}) collective-permute-start(bf16[1552,128]{1,0:T(8,128)(2,1)S(1)} %slice.67), channel_id=1, source_target_pairs={{0,4},{4,8},{8,12},{12,14},{14,10},{10,6},{6,2},{2,0},{1,5},{5,9},... | collective-permute-start | bytes 1191944 | tf_op jit(solution)/shard_map/far_low_ahead/ppermute | solution.py:291
  66.3 17.5 %collective-permute-start.17 = (bf16[1536,128]{1,0:T(8,128)(2,1)S(1)}, bf16[1536,128]{1,0:T(8,128)(2,1)S(1)}, u32[]{:S(2)}, u32[]{:S(2)}) collective-permute-start(bf16[1536,128]{1,0:T(8,128)(2,1)S(1)} %slice.73), channel_id=1, source_target_pairs={{4,0},{8,4},{12,8},{14,12},{10,14},{6,10},{2,6},{0,2},{5,1},{9,5},... | collective-permute-start | bytes 1179656 | tf_op jit(solution)/shard_map/far_high_back/ppermute | solution.py:291
  66.4 19.8 %collective-permute-start.15 = (bf16[512,128]{1,0:T(8,128)(2,1)S(1)}, bf16[512,128]{1,0:T(8,128)(2,1)S(1)}, u32[]{:S(2)}, u32[]{:S(2)}) collective-permute-start(bf16[512,128]{1,0:T(8,128)(2,1)S(1)} %slice.71), channel_id=1, source_target_pairs={{0,4},{4,8},{8,12},{12,14},{14,10},{10,6},{6,2},{2,0},{1,5},{5,9},... | collective-permute-start | bytes 393224 | tf_op jit(solution)/shard_map/last_low_ahead/ppermute | solution.py:291
  75.3 10.9 %collective-permute-start.16 = (bf16[512,128]{1,0:T(8,128)(2,1)S(1)}, bf16[512,128]{1,0:T(8,128)(2,1)S(1)}, u32[]{:S(2)}, u32[]{:S(2)}) collective-permute-start(bf16[512,128]{1,0:T(8,128)(2,1)S(1)} %slice.72), channel_id=1, source_target_pairs={{4,0},{8,4},{12,8},{14,12},{10,14},{6,10},{2,6},{0,2},{5,1},{9,5},... | collective-permute-start | bytes 393224 | tf_op jit(solution)/shard_map/last_high_back/ppermute | solution.py:291
